TPU v7x, 1024 devices: a whole 4x8x16 slice. The times are simulated.
1024 devices in a mesh: rep: 64 (over z_hi, y, core), blk: 4 (over x), tp: 4 (over z_lo).
Axes of the slice: x: 4, y: 8, z: 16 (z_hi: 4, z_lo: 4; z = z_hi * 4 + z_lo), core: 2. Of those that a mesh axis runs over, the one named last changes fastest.
Arguments:
- hidden: bfloat16 [8192, 12288], P(('rep', 'blk', 'tp')), may hold values from -700 to 700
- projection_weight: bfloat16 [12288, 2048], P(('blk', 'tp')), may hold values from -1 to 1
- norm_gain: float32 [2048], replicated, may hold values from 0.5 to 1.5
- upstream: bfloat16 [8192, 2048], P('rep'), may hold values from -700 to 700
- loss_mask: int32 [8192], P('rep'), may hold values 0 or 1
Outputs:
- weight_grad: float32 [16, 768, 2048], P(('blk', 'tp'), 'rep')
- grad_norm: float32 [], replicated
All inputs are finite; a program needn't handle non-finite values. No bound on the sum of `loss_mask` on one device may be relied on, other than what follows from the above.
Results may differ from a plain program's by a relative error of at most 0.0085.
Values may be sent and summed in bfloat16 or wider, within the bound.
No kernel may reach another device: no remote copies, remote signals or barrier semaphores. Data moves between devices by JAX's collectives and lax.ppermute only.
A program may use at most 64 MiB of HBM per device.

v0:
```python
import jax
import jax.numpy as jnp
from jax import lax
from jax.sharding import PartitionSpec as P


def norm_backward(projected, norm_gain, cotangent, token_mask):
    inverse_rms = lax.rsqrt(jnp.mean(projected * projected, axis=1, keepdims=True) + 1e-06)
    normed = projected * inverse_rms
    scaled = norm_gain * (cotangent.astype(jnp.float32) * token_mask.astype(jnp.float32)[:, None])
    along = jnp.mean(scaled * normed, axis=1, keepdims=True)
    return (inverse_rms * (scaled - normed * along)).astype(jnp.bfloat16)


def rounded_term(row_block, projection_weight):
    partial_value = jnp.dot(
        row_block, projection_weight, preferred_element_type=jnp.float32
    ).astype(jnp.bfloat16)
    partial_value = lax.optimization_barrier(partial_value)
    return partial_value.astype(jnp.float32)


def body(hidden, projection_weight, norm_gain, upstream, loss_mask):
    tok_rows = hidden.shape[0]
    joined = hidden.shape[1]
    groups = lax.axis_size(("blk", "tp"))
    shard_rows = joined // groups
    arrived = lax.all_to_all(
        hidden.reshape(1, tok_rows, joined), ("blk", "tp"), split_axis=2, concat_axis=0, tiled=True
    )
    columns = arrived.reshape(groups * tok_rows, shard_rows)
    projected = lax.psum_scatter(
        rounded_term(columns, projection_weight).astype(jnp.bfloat16),
        ("blk", "tp"),
        scatter_dimension=0,
        tiled=True,
    ).astype(jnp.float32)
    offset = lax.axis_index(("blk", "tp")) * tok_rows
    own_cotangent = lax.dynamic_slice_in_dim(upstream, offset, tok_rows, 0)
    own_mask = lax.dynamic_slice_in_dim(loss_mask, offset, tok_rows, 0)
    own_grad = norm_backward(projected, norm_gain, own_cotangent, own_mask)
    token_grad = lax.all_gather(own_grad, ("blk", "tp"), axis=0, tiled=True)
    contract = (((0,), (0,)), ((), ()))
    block_grad = lax.dot_general(columns, token_grad, contract, preferred_element_type=jnp.float32)
    own_rows = lax.psum_scatter(block_grad, "rep", scatter_dimension=0, tiled=True)
    squares_sum = lax.psum(jnp.sum(own_rows * own_rows), ("rep", "blk", "tp"))
    grad_norm = jnp.sqrt(squares_sum)
    limit = jnp.sqrt(jnp.float32(joined * projection_weight.shape[1]))
    factor = jnp.minimum(1.0, limit / (grad_norm + 1e-06))
    weight_grad = (own_rows * factor).reshape(1, own_rows.shape[0], own_rows.shape[1])
    return (weight_grad, grad_norm)


def solution(mesh):
    return jax.shard_map(
        body,
        mesh=mesh,
        in_specs=(
            P(("rep", "blk", "tp"), None),
            P(("blk", "tp"), None),
            P(),
            P("rep", None),
            P("rep"),
        ),
        out_specs=(P(("blk", "tp"), "rep", None), P()),
        check_vma=False,
    )
```

profile of v0, /device:TPU:1, one launch (start us, length us, event | category | flops | bytes accessed | tf_op | source)
XLA Modules:
  0.0 1131.7 jit_solution(15355553756378630455)
XLA Ops:
  7.2 0.0 copy-start
  7.2 0.0 reduce-scatter.3.cloned.1.call-start
  7.2 12.0 %copy.10 = bf16[1,8,12288]{1,0,2:T(2,128)(2,1)} copy(bf16[1,8,12288]{2,1,0:T(8,128)(2,1)} %bitcast.31) | data formatting | bytes 393216 | tf_op jit(solution)/shard_map/reshape | solution.py:29
  19.2 0.5 broadcast.30
  19.8 68.7 %reduce = bf16[12288,8]{1,0:T(8,128)(2,1)} reduce(bf16[12288,1,8]{2,1,0:T(2,128)(2,1)} %bitcast.26, bf16[]{:T(256)} %broadcast.30), dimensions={1}, to_apply=%bitcast.20.reduce_sub_computation | reduce | bytes 393218
  88.4 5.0 reshape.34
  93.4 17.7 %all_to_all.15 = bf16[16,2,3072]{2,1,0:T(2,128)(2,1)S(1)} all-to-all(bf16[16,2,3072]{2,1,0:T(2,128)(2,1)S(1)} %reshape.34), channel_id=1, replica_groups=mesh['rep'=64,'blk'=4,'tp'=4] {'blk','tp'}, dimensions={0} | all-to-all | bytes 393216 | tf_op jit(solution)/shard_map/all_to_all | solution.py:28
  111.1 10.4 reshape.35
  121.5 0.0 copy-start.2
  121.5 0.0 copy-start.1
  121.5 11.3 %copy.11 = bf16[1,8,12288]{2,1,0:T(8,128)(2,1)S(1)} copy(bf16[1,8,12288]{1,0,2:T(2,128)(2,1)} %bitcast.27) | data formatting | bytes 393216 | tf_op jit(solution)/shard_map/all_to_all | solution.py:28
  132.9 0.0 copy-done
  133.0 1.4 convolution_convert_fusion
  134.3 0.0 reduce-scatter.3.cloned.1.call-update
  134.4 0.0 all-reduce.3.cloned.1.call-start
  134.4 0.0 copy-done.2
  134.4 0.1 dynamic-slice_convert_fusion
  134.5 86.8 %reduce-scatter.3.cloned.1.call-done = bf16[8,2048]{1,0:T(8,128)(2,1)} async-done(((bf16[128,2048]{1,0:T(8,128)(2,1)}), bf16[8,2048]{1,0:T(8,128)(2,1)}) %reduce-scatter.3.cloned.1.call-update) | async-done | bytes 32784 | tf_op jit(solution)/shard_map/reduce_scatter | solution.py:32
  221.4 0.9 fusion.10
  222.2 0.0 copy-done.1
  222.3 1.0 fusion.6
  223.2 0.9 fusion.9
  224.1 35.1 %all_gather.3 = bf16[128,2048]{1,0:T(8,128)(2,1)S(1)} all-gather(bf16[8,2048]{1,0:T(8,128)(2,1)S(1)} %fusion.9), channel_id=1, replica_groups=mesh['rep'=64,'blk'=4,'tp'=4] {'blk','tp'}, dimensions={0}, use_global_device_ids=true | all-gather | bytes 557056 | tf_op jit(solution)/shard_map/all_gather | solution.py:42
  259.2 3.7 convolution_bitcast_fusion
  262.9 0.0 all-reduce.3.cloned.1.call-update
  262.9 1.3 dynamic-slice
  264.9 726.8 %all-reduce.3.cloned.1.call-done = f32[768,2048]{0,1:T(8,128)} async-done(((f32[768,2048]{0,1:T(8,128)}), f32[768,2048]{0,1:T(8,128)}) %all-reduce.3.cloned.1.call-update) | async-done | bytes 6291472
  991.7 2.5 multiply_reduce_fusion
  994.2 123.6 %psum.7 = f32[]{:T(128)} all-reduce(f32[]{:T(128)} %multiply_reduce_fusion), channel_id=1, replica_groups=mesh['rep'=64,'blk'=4,'tp'=4] {'rep','blk','tp'}, use_global_device_ids=true, to_apply=%region_5.0 | all-reduce | flops 1 | bytes 8 | tf_op jit(solution)/shard_map/psum | solution.py:46
  1118.6 2.9 multiply_bitcast_fusion
  1121.5 2.2 copy.13
  (3 shorter events, 0.1 us)
Async XLA Ops:
  7.2 125.8 %copy-start = (bf16[768,2048]{1,0:T(8,128)(2,1)S(1)}, bf16[768,2048]{1,0:T(8,128)(2,1)}, u32[]{:S(2)}) copy-start(bf16[768,2048]{1,0:T(8,128)(2,1)} %param.6) | copy-start | bytes 9437188
  7.2 214.2 %reduce-scatter.3.cloned.1.call-start = ((), (), s32[]{:S(2)}) async-start(), calls=%async_computation.2 | async-start | bytes 557056 | tf_op jit(solution)/shard_map/reduce_scatter | solution.py:32
  121.5 12.9 %copy-start.2 = (s32[128]{0:T(128)S(1)}, s32[128]{0:T(128)}, u32[]{:S(2)}) copy-start(s32[128]{0:T(128)} %param.9) | copy-start | bytes 1540
  121.5 100.7 %copy-start.1 = (f32[2048]{0:T(1024)S(1)}, f32[2048]{0:T(1024)}, u32[]{:S(2)}) copy-start(f32[2048]{0:T(1024)} %param.7) | copy-start | bytes 24580
  134.4 857.3 %all-reduce.3.cloned.1.call-start = ((), (), s32[]{:S(2)}) async-start(), calls=%async_computation.3 | async-start | bytes 12582912
Sparse Core Ops, SparseCore 0:
  134.5 86.8 reduce-scatter.2
  263.0 728.6 all-reduce.2
where the time goes:
time: 1130 us
  waiting for transfers between devices  814 us (72%)
  blocking collectives  176 us (16%)
  other arithmetic  77 us (7%)
  local copies, waits for them, and re-layouts  42.8 us (4%)
  between operations  16.6 us (1%)
    unnamed x3, waiting for transfers between devices  727 us
    psum x1, blocking collectives, body(): squares_sum = lax.psum(jnp.sum(own_rows * own_rows), ('rep', 'blk', 'tp'))  124 us
    reduce_scatter x1, waiting for transfers between devices, body(): lax.psum_scatter(rounded_term(columns, projection_weight).astype(jnp.bflo...  86.8 us
    unnamed x1, other arithmetic  68.7 us
    all_gather x1, blocking collectives, body(): token_grad = lax.all_gather(own_grad, ('blk', 'tp'), axis=0, tiled=True)  35.1 us
  transfers between devices with their start and end apart: 2, of which 2 were waited for; matrix products, arithmetic and copies ran while one was open for 0% of the time, Pallas kernels for 0%

commit v1 on v0

v1 whole, which is shorter than its diff:
```python
import jax
import jax.numpy as jnp
import numpy as np
from jax import lax
from jax.sharding import Mesh, PartitionSpec as P

ZHI, YS, CORES = 4, 8, 2
REP = ("zh", "y", "core")
GROUP = ("blk", "tp")
BF16, F32 = jnp.bfloat16, jnp.float32


def norm_backward(projected, norm_gain, cotangent, token_mask):
    inverse_rms = lax.rsqrt(jnp.mean(projected * projected, axis=1, keepdims=True) + 1e-06)
    normed = projected * inverse_rms
    scaled = norm_gain * (cotangent.astype(F32) * token_mask.astype(F32)[:, None])
    along = jnp.mean(scaled * normed, axis=1, keepdims=True)
    return (inverse_rms * (scaled - normed * along)).astype(BF16)


def exchange(blocks, axes):
    return lax.all_to_all(blocks, axes, split_axis=0, concat_axis=0, tiled=True)


def total_over(value, axes, size):
    arrived = exchange(lax.optimization_barrier(jnp.full((size, 1, 128), value, F32)), axes)
    return jnp.sum(arrived[:, 0, 0])


def body(hidden, projection_weight, norm_gain, upstream, loss_mask):
    tok, joined = hidden.shape
    groups = lax.axis_size(GROUP)
    shard, width = projection_weight.shape
    own_rows = shard // (ZHI * YS * CORES)
    core = lax.axis_index("core")
    zh = lax.axis_index("zh")
    swap = [(0, 1), (1, 0)]

    sent = lax.optimization_barrier(hidden.reshape(tok, groups, shard).transpose(1, 0, 2))
    columns = exchange(sent, GROUP).reshape(groups * tok, shard)

    order = np.arange(shard).reshape(ZHI, YS, CORES, own_rows).transpose(2, 1, 0, 3).reshape(CORES, -1)
    kept = shard // CORES
    mine = jnp.asarray(order.astype(np.int32))
    feature = lax.broadcasted_iota(jnp.int32, (shard, kept), 0)
    pick_own = (feature == lax.dynamic_index_in_dim(mine, core, 0)).astype(BF16)
    pick_other = (feature == lax.dynamic_index_in_dim(mine, 1 - core, 0)).astype(BF16)
    own_cols = jnp.dot(columns, pick_own, preferred_element_type=F32).astype(BF16)
    give_cols = jnp.dot(columns, pick_other, preferred_element_type=F32).astype(BF16)
    got_cols = lax.ppermute(give_cols, "core", swap)

    partial_value = jnp.dot(columns, projection_weight, preferred_element_type=F32).astype(BF16)
    parts = exchange(lax.optimization_barrier(partial_value.reshape(groups, tok, width)), GROUP)
    projected = jnp.sum(parts.astype(F32), axis=0)
    offset = lax.axis_index(GROUP) * tok
    own_cotangent = lax.dynamic_slice_in_dim(upstream, offset, tok, 0)
    own_mask = lax.dynamic_slice_in_dim(loss_mask, offset, tok, 0)
    own_grad = norm_backward(projected, norm_gain, own_cotangent, own_mask)
    spread = lax.optimization_barrier(jnp.broadcast_to(own_grad[None], (groups, tok, width)))
    token_grad = exchange(spread, GROUP).reshape(groups * tok, width)
    other_grad = lax.ppermute(token_grad, "core", swap)

    contract = (((0,), (0,)), ((), ()))
    block = lax.dot_general(
        jnp.concatenate([own_cols, got_cols], 0),
        jnp.concatenate([token_grad, other_grad], 0),
        contract,
        preferred_element_type=F32,
    ).astype(BF16)
    by_y = exchange(lax.optimization_barrier(block.reshape(YS, ZHI * own_rows, width)), "y")
    over_y = jnp.sum(by_y.astype(F32), axis=0).reshape(ZHI, own_rows, width)

    total = lax.dynamic_index_in_dim(over_y, zh, 0, keepdims=False)
    for step in (2, 1, 3):
        piece = lax.dynamic_index_in_dim(over_y, (zh + step) % ZHI, 0, keepdims=False).astype(BF16)
        total = total + lax.ppermute(
            piece, "zh", [(i, (i + step) % ZHI) for i in range(ZHI)]
        ).astype(F32)

    squares = total_over(jnp.sum(total * total), ("core", "blk", "tp"), CORES * groups)
    squares = total_over(squares, ("zh", "y"), ZHI * YS)
    grad_norm = jnp.sqrt(squares)
    limit = jnp.sqrt(jnp.float32(joined * width))
    factor = jnp.minimum(1.0, limit / (grad_norm + 1e-06))
    return ((total * factor)[None], grad_norm)


def solution(mesh):
    sizes = (ZHI, YS, CORES, mesh.shape["blk"], mesh.shape["tp"])
    fine = Mesh(mesh.devices.reshape(sizes), REP + GROUP)
    return jax.shard_map(
        body,
        mesh=fine,
        in_specs=(
            P(REP + GROUP, None),
            P(GROUP, None),
            P(),
            P(REP, None),
            P(REP),
        ),
        out_specs=(P(GROUP, REP, None), P()),
        check_vma=False,
    )
```

time: 1130 us -> 198 us (0.18)
  waiting for transfers between devices: 814 us -> 56.5 us
  blocking collectives: 176 us -> 68.6 us
  other arithmetic: 77 us -> 8.59 us
  starting transfers between devices: 0.08 us -> 51.8 us
  local copies, waits for them, and re-layouts: 42.8 us -> 4.02 us
  between operations: 16.6 us -> 2.66 us
    unnamed x3 -> x0, waiting for transfers between devices: 727 us -> none
    psum x1 -> x0, blocking collectives: 124 us -> none  [body(): squares_sum = lax.psum(jnp.sum(own_rows * own_rows), ('rep', 'blk', 'tp'))]
    reduce_scatter x1 -> x0, waiting for transfers between devices: 86.8 us -> none  [body(): lax.psum_scatter(rounded_term(columns, projection_weight).astype(jnp.bflo...]
    unnamed x1 -> x0, other arithmetic: 68.7 us -> none
    all_to_all x1 -> x4, blocking collectives: 17.7 us -> 68.6 us  [exchange(): return lax.all_to_all(blocks, axes, split_axis=0, concat_axis=0, tiled=True)]
    all_to_all x0 -> x2, waiting for transfers between devices: none -> 49.4 us  [exchange(): return lax.all_to_all(blocks, axes, split_axis=0, concat_axis=0, tiled=True)]
    ppermute x0 -> x5, starting transfers between devices: none -> 40.1 us  [the longest x3 25.6 us: body(): lax.ppermute(piece, 'zh', [(i, (i + step) % ZHI) for i in range(ZHI)])]
    all_gather x1 -> x0, blocking collectives: 35.1 us -> none  [body(): token_grad = lax.all_gather(own_grad, ('blk', 'tp'), axis=0, tiled=True)]
  transfers between devices with their start and end apart: 2 -> 7, of which waited for: 2 -> 5; matrix products, arithmetic and copies ran while one was open for 0% -> 0% of each run, Pallas kernels for 0% -> 0%
where the time goes in v1:
time: 198 us; the launch traced here: 197 us
  blocking collectives  68.6 us (35%)
  waiting for transfers between devices  56.5 us (29%)
  starting transfers between devices  51.8 us (26%)
  other arithmetic  8.59 us (4%)
  matrix products  5.05 us (3%)
  local copies, waits for them, and re-layouts  4.02 us (2%)
  between operations  2.66 us (1%)
    all_to_all x4, blocking collectives, exchange(): return lax.all_to_all(blocks, axes, split_axis=0, concat_axis=0, tiled=True)  68.6 us
    all_to_all x2, waiting for transfers between devices, exchange(): return lax.all_to_all(blocks, axes, split_axis=0, concat_axis=0, tiled=True)  49.4 us
    ppermute x3, starting transfers between devices, body(): lax.ppermute(piece, 'zh', [(i, (i + step) % ZHI) for i in range(ZHI)])  25.6 us
    ppermute x1, starting transfers between devices, body(): other_grad = lax.ppermute(token_grad, 'core', swap)  12.6 us
    all_to_all x2, starting transfers between devices, exchange(): return lax.all_to_all(blocks, axes, split_axis=0, concat_axis=0, tiled=True)  11.7 us
    ppermute x3, waiting for transfers between devices, body(): lax.ppermute(piece, 'zh', [(i, (i + step) % ZHI) for i in range(ZHI)])  6.15 us
  transfers between devices with their start and end apart: 7, of which 5 were waited for; matrix products, arithmetic and copies ran while one was open for 0% of the time, Pallas kernels for 0%

profile of v1, /device:TPU:1, one launch (start us, length us, event | category | flops | bytes accessed | tf_op | source)
XLA Modules:
  0.0 197.2 jit_solution(12977610743268354530)
XLA Ops:
  0.6 0.0 copy-start
  0.6 18.2 %all_to_all.30 = bf16[16,8,768]{2,1,0:T(8,128)(2,1)S(1)} all-to-all(bf16[16,8,768]{2,1,0:T(8,128)(2,1)} %bitcast.38), channel_id=1, replica_groups=mesh['zh'=4,'y'=8,'core'=2,'blk'=4,'tp'=4] {'blk','tp'}, dimensions={0} | all-to-all | bytes 393216 | tf_op jit(solution)/shard_map/all_to_all | solution.py:22
  18.8 0.0 copy-done
  18.8 0.0 copy-start.3
  18.8 0.0 copy-start.1
  18.8 1.4 fusion
  20.2 0.0 copy-start.2
  20.2 4.4 %all-to-all-start.1 = ((bf16[16,8,2048]{2,1,0:T(8,128)(2,1)}), bf16[16,8,2048]{2,1,0:T(8,128)(2,1)}, u32[]{:S(2)}, u32[]{:S(2)}) async-start(bf16[16,8,2048]{2,1,0:T(8,128)(2,1)} %fusion), calls=%async_computation.1 | async-start | bytes 1048576 | tf_op jit(solution)/shard_map/all_to_all | solution.py:22
  24.6 0.0 copy-done.3
  24.6 0.1 dynamic-slice_convert_fusion.3
  24.7 11.1 %all-to-all-done.1 = bf16[16,8,2048]{2,1,0:T(8,128)(2,1)} async-done(((bf16[16,8,2048]{2,1,0:T(8,128)(2,1)}), bf16[16,8,2048]{2,1,0:T(8,128)(2,1)}, u32[]{:S(2)}, u32[]{:S(2)}) %all-to-all-start.1) | async-done | bytes 524320 | tf_op jit(solution)/shard_map/all_to_all | solution.py:22
  35.7 1.1 convert_reduce_fusion.1
  36.9 0.1 multiply_reduce_fusion.2
  37.0 0.0 copy-done.1
  37.0 1.0 multiply_reduce_fusion.1
  38.0 0.8 multiply_convert_fusion
  38.9 14.4 %all_to_all.31 = bf16[16,8,2048]{2,1,0:T(8,128)(2,1)} all-to-all(bf16[16,8,2048]{2,1,0:T(8,128)(2,1)S(1)} %broadcast_in_dim.8), channel_id=1, replica_groups=mesh['zh'=4,'y'=8,'core'=2,'blk'=4,'tp'=4] {'blk','tp'}, dimensions={0} | all-to-all | bytes 1048576 | tf_op jit(solution)/shard_map/all_to_all | solution.py:22
  53.3 12.6 %collective-permute-start.1 = (bf16[128,2048]{1,0:T(8,128)(2,1)}, bf16[128,2048]{1,0:T(8,128)(2,1)}, u32[]{:S(2)}, u32[]{:S(2)}) collective-permute-start(bf16[128,2048]{1,0:T(8,128)(2,1)} %bitcast.6), channel_id=1, source_target_pairs={{0,16},{16,0},{1,17},{17,1},{2,18},{18,2},{3,19},{19,3},{4,20},{20... | collective-permute-start | bytes 1572872 | tf_op jit(solution)/shard_map/ppermute | solution.py:61
  65.9 0.0 copy-done.2
  65.9 0.3 fusion.6
  66.3 1.9 collective-permute-start
  68.2 0.3 fusion.5
  68.6 0.9 collective-permute-done
  69.5 0.0 collective-permute-done.1
  69.5 3.0 %convolution_convert_fusion = bf16[384,2048]{1,0:T(8,128)(2,1)} fusion(bf16[128,2048]{1,0:T(8,128)(2,1)} %collective-permute-done.1, bf16[128,2048]{1,0:T(8,128)(2,1)} %bitcast.6, bf16[128,384]{1,0:T(8,128)(2,1)S(1)} %collective-permute-done, bf16[128,384]{1,0:T(8,128)(2,1)S(1)} %fusion.5), kind=kOutput, calls=%fused_computation.1 | convolution fusion | flops 405929984 | bytes 2818048 | tf_op jit(solution)/shard_map/dot_general | solution.py:64
  72.5 7.4 %all-to-all-start.3 = ((bf16[8,48,2048]{2,1,0:T(8,128)(2,1)}), bf16[8,48,2048]{2,1,0:T(8,128)(2,1)}, u32[]{:S(2)}, u32[]{:S(2)}) async-start(bf16[8,48,2048]{2,1,0:T(8,128)(2,1)} %bitcast.37), calls=%async_computation.3 | async-start | bytes 3145728 | tf_op jit(solution)/shard_map/all_to_all | solution.py:22
  79.8 38.4 %all-to-all-done.3 = bf16[8,48,2048]{2,1,0:T(8,128)(2,1)} async-done(((bf16[8,48,2048]{2,1,0:T(8,128)(2,1)}), bf16[8,48,2048]{2,1,0:T(8,128)(2,1)}, u32[]{:S(2)}, u32[]{:S(2)}) %all-to-all-start.3) | async-done | bytes 1572896 | tf_op jit(solution)/shard_map/all_to_all | solution.py:22
  118.2 1.7 convert_reduce_fusion
  119.9 0.8 reshape.45
  120.7 1.1 fusion.20
  121.8 16.4 %collective-permute-start.2 = (bf16[12,2048]{1,0:T(8,128)(2,1)S(1)}, bf16[12,2048]{1,0:T(8,128)(2,1)S(1)}, u32[]{:S(2)}, u32[]{:S(2)}) collective-permute-start(bf16[12,2048]{1,0:T(8,128)(2,1)S(1)} %get-tuple-element.10), channel_id=1, source_target_pairs={{0,512},{256,768},{512,0},{768,256},{1,513},{257,769},{513,1},{769... | collective-permute-start | bytes 147464 | tf_op jit(solution)/shard_map/ppermute | solution.py:76
  138.2 5.8 %collective-permute-start.3 = (bf16[12,2048]{1,0:T(8,128)(2,1)S(1)}, bf16[12,2048]{1,0:T(8,128)(2,1)S(1)}, u32[]{:S(2)}, u32[]{:S(2)}) collective-permute-start(bf16[12,2048]{1,0:T(8,128)(2,1)S(1)} %get-tuple-element.12), channel_id=1, source_target_pairs={{0,256},{256,512},{512,768},{768,0},{1,257},{257,513},{513,769},{7... | collective-permute-start | bytes 147464 | tf_op jit(solution)/shard_map/ppermute | solution.py:76
  144.0 3.4 %collective-permute-start.4 = (bf16[12,2048]{1,0:T(8,128)(2,1)S(1)}, bf16[12,2048]{1,0:T(8,128)(2,1)S(1)}, u32[]{:S(2)}, u32[]{:S(2)}) collective-permute-start(bf16[12,2048]{1,0:T(8,128)(2,1)S(1)} %get-tuple-element.11), channel_id=1, source_target_pairs={{0,768},{256,0},{512,256},{768,512},{1,769},{257,1},{513,257},{769... | collective-permute-start | bytes 147464 | tf_op jit(solution)/shard_map/ppermute | solution.py:76
  147.4 0.0 collective-permute-done.2
  147.4 0.6 collective-permute-done.3
  148.0 5.6 %collective-permute-done.4 = bf16[12,2048]{1,0:T(8,128)(2,1)S(1)} collective-permute-done((bf16[12,2048]{1,0:T(8,128)(2,1)S(1)}, bf16[12,2048]{1,0:T(8,128)(2,1)S(1)}, u32[]{:S(2)}, u32[]{:S(2)}) %collective-permute-start.4) | collective-permute-done | bytes 49184 | tf_op jit(solution)/shard_map/ppermute | solution.py:76
  153.5 1.5 multiply_reduce_fusion
  155.1 0.7 broadcast_in_dim.9
  155.7 15.1 %all_to_all.32 = f32[32,1,128]{2,1,0:T(1,128)S(1)} all-to-all(f32[32,1,128]{2,1,0:T(1,128)S(1)} %broadcast_in_dim.9), channel_id=1, replica_groups=mesh['zh'=4,'y'=8,'core'=2,'blk'=4,'tp'=4] {'core','blk','tp'}, dimensions={0} | all-to-all | bytes 32768 | tf_op jit(solution)/shard_map/all_to_all | solution.py:22
  170.8 0.6 slice_reduce_fusion.1
  171.5 0.7 broadcast_in_dim.10
  172.1 20.9 %all_to_all.33 = f32[32,1,128]{2,1,0:T(1,128)S(1)} all-to-all(f32[32,1,128]{2,1,0:T(1,128)S(1)} %broadcast_in_dim.10), channel_id=1, replica_groups=mesh['zh'=4,'y'=8,'core'=2,'blk'=4,'tp'=4] {'zh','y'}, dimensions={0} | all-to-all | bytes 32768 | tf_op jit(solution)/shard_map/all_to_all | solution.py:22
  193.0 0.6 slice_reduce_fusion
  194.4 0.9 multiply_bitcast_fusion
  195.3 0.7 copy.14
  (4 shorter events, 0.1 us)
Async XLA Ops:
  0.6 18.2 %copy-start = (bf16[768,2048]{1,0:T(8,128)(2,1)S(1)}, bf16[768,2048]{1,0:T(8,128)(2,1)}, u32[]{:S(2)}) copy-start(bf16[768,2048]{1,0:T(8,128)(2,1)} %param.7) | copy-start | bytes 9437188
  18.8 5.8 %copy-start.3 = (s32[128]{0:T(128)S(1)}, s32[128]{0:T(128)}, u32[]{:S(2)}) copy-start(s32[128]{0:T(128)} %param.10) | copy-start | bytes 1540
  18.8 18.2 %copy-start.1 = (f32[2048]{0:T(1024)S(1)}, f32[2048]{0:T(1024)}, u32[]{:S(2)}) copy-start(f32[2048]{0:T(1024)} %param.8) | copy-start | bytes 24580
  20.2 45.7 %copy-start.2 = (s32[2,384]{1,0:T(2,128)S(1)}, s32[2,384]{1,0:T(2,128)}, u32[]{:S(2)}) copy-start(s32[2,384]{1,0:T(2,128)} %constant.80.clone) | copy-start | bytes 9220
  20.2 15.5 %all-to-all-start.1 = ((bf16[16,8,2048]{2,1,0:T(8,128)(2,1)}), bf16[16,8,2048]{2,1,0:T(8,128)(2,1)}, u32[]{:S(2)}, u32[]{:S(2)}) async-start(bf16[16,8,2048]{2,1,0:T(8,128)(2,1)} %fusion), calls=%async_computation.1 | async-start | bytes 1048576 | tf_op jit(solution)/shard_map/all_to_all | solution.py:22
  53.3 16.2 %collective-permute-start.1 = (bf16[128,2048]{1,0:T(8,128)(2,1)}, bf16[128,2048]{1,0:T(8,128)(2,1)}, u32[]{:S(2)}, u32[]{:S(2)}) collective-permute-start(bf16[128,2048]{1,0:T(8,128)(2,1)} %bitcast.6), channel_id=1, source_target_pairs={{0,16},{16,0},{1,17},{17,1},{2,18},{18,2},{3,19},{19,3},{4,20},{20... | collective-permute-start | bytes 1572872 | tf_op jit(solution)/shard_map/ppermute | solution.py:61
  66.3 3.2 %collective-permute-start = (bf16[128,384]{1,0:T(8,128)(2,1)S(1)}, bf16[128,384]{1,0:T(8,128)(2,1)S(1)}, u32[]{:S(2)}, u32[]{:S(2)}) collective-permute-start(bf16[128,384]{1,0:T(8,128)(2,1)S(1)} %fusion.6), channel_id=1, source_target_pairs={{0,16},{16,0},{1,17},{17,1},{2,18},{18,2},{3,19},{19,3},{4,20},{20... | collective-permute-start | bytes 294920 | tf_op jit(solution)/shard_map/ppermute | solution.py:50
  72.5 45.7 %all-to-all-start.3 = ((bf16[8,48,2048]{2,1,0:T(8,128)(2,1)}), bf16[8,48,2048]{2,1,0:T(8,128)(2,1)}, u32[]{:S(2)}, u32[]{:S(2)}) async-start(bf16[8,48,2048]{2,1,0:T(8,128)(2,1)} %bitcast.37), calls=%async_computation.3 | async-start | bytes 3145728 | tf_op jit(solution)/shard_map/all_to_all | solution.py:22
  121.8 25.6 %collective-permute-start.2 = (bf16[12,2048]{1,0:T(8,128)(2,1)S(1)}, bf16[12,2048]{1,0:T(8,128)(2,1)S(1)}, u32[]{:S(2)}, u32[]{:S(2)}) collective-permute-start(bf16[12,2048]{1,0:T(8,128)(2,1)S(1)} %get-tuple-element.10), channel_id=1, source_target_pairs={{0,512},{256,768},{512,0},{768,256},{1,513},{257,769},{513,1},{769... | collective-permute-start | bytes 147464 | tf_op jit(solution)/shard_map/ppermute | solution.py:76
  138.2 9.8 %collective-permute-start.3 = (bf16[12,2048]{1,0:T(8,128)(2,1)S(1)}, bf16[12,2048]{1,0:T(8,128)(2,1)S(1)}, u32[]{:S(2)}, u32[]{:S(2)}) collective-permute-start(bf16[12,2048]{1,0:T(8,128)(2,1)S(1)} %get-tuple-element.12), channel_id=1, source_target_pairs={{0,256},{256,512},{512,768},{768,0},{1,257},{257,513},{513,769},{7... | collective-permute-start | bytes 147464 | tf_op jit(solution)/shard_map/ppermute | solution.py:76
  144.0 9.5 %collective-permute-start.4 = (bf16[12,2048]{1,0:T(8,128)(2,1)S(1)}, bf16[12,2048]{1,0:T(8,128)(2,1)S(1)}, u32[]{:S(2)}, u32[]{:S(2)}) collective-permute-start(bf16[12,2048]{1,0:T(8,128)(2,1)S(1)} %get-tuple-element.11), channel_id=1, source_target_pairs={{0,768},{256,0},{512,256},{768,512},{1,769},{257,1},{513,257},{769... | collective-permute-start | bytes 147464 | tf_op jit(solution)/shard_map/ppermute | solution.py:76

commit v2 on v1

v2 whole, which is shorter than its diff:
```python
import jax
import jax.numpy as jnp
from jax import lax
from jax.sharding import Mesh, PartitionSpec as P

ZHI, YS, CORES = 4, 8, 2
REP = ("zh", "y", "core")
GROUP = ("blk", "tp")
BF16, F32 = jnp.bfloat16, jnp.float32


def norm_backward(projected, norm_gain, cotangent, token_mask):
    inverse_rms = lax.rsqrt(jnp.mean(projected * projected, axis=1, keepdims=True) + 1e-06)
    normed = projected * inverse_rms
    scaled = norm_gain * (cotangent.astype(F32) * token_mask.astype(F32)[:, None])
    along = jnp.mean(scaled * normed, axis=1, keepdims=True)
    return (inverse_rms * (scaled - normed * along)).astype(BF16)


def exchange(blocks, axes):
    return lax.all_to_all(blocks, axes, split_axis=0, concat_axis=0, tiled=True)


def total_over(value, axes, size):
    arrived = exchange(lax.optimization_barrier(jnp.full((size, 1, 128), value, F32)), axes)
    return jnp.sum(arrived[:, 0, 0])


def body(hidden, projection_weight, norm_gain, upstream, loss_mask):
    tok, joined = hidden.shape
    groups = lax.axis_size(GROUP)
    shard, width = projection_weight.shape
    slices = YS * CORES
    part = width // slices

    sent = lax.optimization_barrier(hidden.reshape(tok, groups, shard).transpose(1, 0, 2))
    columns = exchange(sent, GROUP).reshape(groups * tok, shard)
    all_columns = lax.all_gather(columns, ("y", "core"), axis=0, tiled=True)

    partial_value = jnp.dot(columns, projection_weight, preferred_element_type=F32).astype(BF16)
    parts = exchange(lax.optimization_barrier(partial_value.reshape(groups, tok, width)), GROUP)
    projected = jnp.sum(parts.astype(F32), axis=0)
    offset = lax.axis_index(GROUP) * tok
    own_cotangent = lax.dynamic_slice_in_dim(upstream, offset, tok, 0)
    own_mask = lax.dynamic_slice_in_dim(loss_mask, offset, tok, 0)
    own_grad = norm_backward(projected, norm_gain, own_cotangent, own_mask)

    cut = lax.optimization_barrier(own_grad.reshape(tok, slices, part).transpose(1, 0, 2))
    cut = exchange(cut, ("y", "core"))
    spread = lax.optimization_barrier(jnp.broadcast_to(cut[None], (groups, slices, tok, part)))
    arrived = exchange(spread, GROUP)
    token_grad = arrived.transpose(1, 0, 2, 3).reshape(slices * groups * tok, part)

    contract = (((0,), (0,)), ((), ()))
    block = lax.dot_general(all_columns, token_grad, contract, preferred_element_type=F32).astype(BF16)
    by_zh = exchange(lax.optimization_barrier(block.reshape(ZHI, shard // ZHI, part)), "zh")
    over_zh = jnp.sum(by_zh.astype(F32), axis=0)

    own_rows = shard // (ZHI * slices)
    squares = jnp.full((slices, 1, part), jnp.sum(over_zh * over_zh), F32)
    spare = jnp.zeros((slices, 16 - own_rows - 1, part), F32)
    rows = jnp.concatenate([over_zh.reshape(slices, own_rows, part), squares, spare], axis=1)
    back = exchange(lax.optimization_barrier(rows), ("y", "core"))
    total = back[:, :own_rows].transpose(1, 0, 2).reshape(own_rows, width)
    squares = jnp.sum(back[:, own_rows, 0])
    squares = total_over(squares, ("zh", "blk", "tp"), ZHI * groups)
    grad_norm = jnp.sqrt(squares)
    limit = jnp.sqrt(jnp.float32(joined * width))
    factor = jnp.minimum(1.0, limit / (grad_norm + 1e-06))
    return ((total * factor)[None], grad_norm)


def solution(mesh):
    sizes = (ZHI, YS, CORES, mesh.shape["blk"], mesh.shape["tp"])
    fine = Mesh(mesh.devices.reshape(sizes), REP + GROUP)
    return jax.shard_map(
        body,
        mesh=fine,
        in_specs=(
            P(REP + GROUP, None),
            P(GROUP, None),
            P(),
            P(REP, None),
            P(REP),
        ),
        out_specs=(P(GROUP, REP, None), P()),
        check_vma=False,
    )
```

time: 198 us -> 168 us (0.85)
  waiting for transfers between devices: 56.5 us -> 23.8 us
  starting transfers between devices: 51.8 us -> 20.1 us
  blocking collectives: 68.6 us -> 93.1 us
  between operations: 2.66 us -> 16 us
  other arithmetic: 8.59 us -> 5.19 us
    ppermute x5 -> x0, starting transfers between devices: 40.1 us -> none  [the longest x3 25.6 us: body(): lax.ppermute(piece, 'zh', [(i, (i + step) % ZHI) for i in range(ZHI)])]
    all_to_all x2, waiting for transfers between devices: 49.4 us -> 23.8 us  [exchange(): return lax.all_to_all(blocks, axes, split_axis=0, concat_axis=0, tiled=True)]
    all_to_all x4 -> x5, blocking collectives: 68.6 us -> 93.1 us  [exchange(): return lax.all_to_all(blocks, axes, split_axis=0, concat_axis=0, tiled=True)]
    all_to_all x2, starting transfers between devices: 11.7 us -> 20 us  [exchange(): return lax.all_to_all(blocks, axes, split_axis=0, concat_axis=0, tiled=True)]
    ppermute x5 -> x0, waiting for transfers between devices: 7.07 us -> none  [the longest x3 6.15 us: body(): lax.ppermute(piece, 'zh', [(i, (i + step) % ZHI) for i in range(ZHI)])]
  transfers between devices with their start and end apart: 7 -> 3, of which waited for: 5 -> 2; matrix products, arithmetic and copies ran while one was open for 0% -> 4% of each run, Pallas kernels for 0% -> 0%
where the time goes in v2:
time: 168 us; the launch traced here: 167 us
  blocking collectives  93.1 us (55%)
  waiting for transfers between devices  23.8 us (14%)
  starting transfers between devices  20.1 us (12%)
  between operations  16 us (10%)
  other arithmetic  5.19 us (3%)
  matrix products  5 us (3%)
  local copies, waits for them, and re-layouts  3.99 us (2%)
    all_to_all x5, blocking collectives, exchange(): return lax.all_to_all(blocks, axes, split_axis=0, concat_axis=0, tiled=True)  93.1 us
    all_to_all x2, waiting for transfers between devices, exchange(): return lax.all_to_all(blocks, axes, split_axis=0, concat_axis=0, tiled=True)  23.8 us
    all_to_all x2, starting transfers between devices, exchange(): return lax.all_to_all(blocks, axes, split_axis=0, concat_axis=0, tiled=True)  20 us
  transfers between devices with their start and end apart: 3, of which 2 were waited for; matrix products, arithmetic and copies ran while one was open for 4% of the time, Pallas kernels for 0%

profile of v2, /device:TPU:1, one launch (start us, length us, event | category | flops | bytes accessed | tf_op | source)
XLA Modules:
  0.0 167.1 jit_solution(9547628432597958706)
XLA Ops:
  7.2 0.0 copy-start
  7.2 0.0 copy-start.2
  7.2 0.0 copy-start.1
  7.2 0.0 all-gather.2.cloned.1.call-start
  7.2 18.3 %all_to_all.35 = bf16[16,8,768]{2,1,0:T(8,128)(2,1)} all-to-all(bf16[16,8,768]{2,1,0:T(8,128)(2,1)} %bitcast.27), channel_id=1, replica_groups=mesh['zh'=4,'y'=8,'core'=2,'blk'=4,'tp'=4] {'blk','tp'}, dimensions={0} | all-to-all | bytes 393216 | tf_op jit(solution)/shard_map/all_to_all | solution.py:21
  25.5 0.0 all-gather.2.cloned.1.call-update
  25.5 0.0 copy-done
  25.6 2.3 %fusion = bf16[16,8,2048]{2,1,0:T(8,128)(2,1)} fusion(bf16[768,2048]{1,0:T(8,128)(2,1)S(1)} %copy-done, bf16[16,8,768]{2,1,0:T(8,128)(2,1)} %all_to_all.35), kind=kOutput, calls=%fused_computation.1 | convolution fusion | flops 402915328 | bytes 3866624 | tf_op jit(solution)/shard_map/dot_general | solution.py:40
  27.9 4.2 %all-to-all-start.1 = ((bf16[16,8,2048]{2,1,0:T(8,128)(2,1)}), bf16[16,8,2048]{2,1,0:T(8,128)(2,1)}, u32[]{:S(2)}, u32[]{:S(2)}) async-start(bf16[16,8,2048]{2,1,0:T(8,128)(2,1)} %fusion), calls=%async_computation.1 | async-start | bytes 1048576 | tf_op jit(solution)/shard_map/all_to_all | solution.py:21
  32.1 0.0 copy-done.2
  32.1 0.1 dynamic-slice_convert_fusion
  32.2 11.1 %all-to-all-done.1 = bf16[16,8,2048]{2,1,0:T(8,128)(2,1)} async-done(((bf16[16,8,2048]{2,1,0:T(8,128)(2,1)}), bf16[16,8,2048]{2,1,0:T(8,128)(2,1)}, u32[]{:S(2)}, u32[]{:S(2)}) %all-to-all-start.1) | async-done | bytes 524320 | tf_op jit(solution)/shard_map/all_to_all | solution.py:21
  43.3 1.1 convert_reduce_fusion
  44.4 0.1 multiply_reduce_fusion.2
  44.5 0.0 copy-done.1
  44.5 1.0 multiply_reduce_fusion.1
  45.5 0.8 fusion.3
  46.4 21.4 %all_to_all.36 = bf16[16,8,128]{2,1,0:T(8,128)(2,1)S(1)} all-to-all(bf16[16,8,128]{2,1,0:T(8,128)(2,1)S(1)} %fusion.3), channel_id=1, replica_groups=mesh['zh'=4,'y'=8,'core'=2,'blk'=4,'tp'=4] {'y','core'}, dimensions={0} | all-to-all | bytes 65536 | tf_op jit(solution)/shard_map/all_to_all | solution.py:21
  67.7 0.1 broadcast_in_dim.8
  67.8 18.4 %all_to_all.37 = bf16[16,16,8,128]{3,2,1,0:T(8,128)(2,1)S(1)} all-to-all(bf16[16,16,8,128]{3,2,1,0:T(8,128)(2,1)S(1)} %broadcast_in_dim.8), channel_id=1, replica_groups=mesh['zh'=4,'y'=8,'core'=2,'blk'=4,'tp'=4] {'blk','tp'}, dimensions={0} | all-to-all | bytes 1048576 | tf_op jit(solution)/shard_map/all_to_all | solution.py:21
  86.2 0.9 copy.19
  87.1 0.0 all-gather.2.cloned.1.call-done
  87.1 2.7 %fusion.1 = bf16[768,128]{0,1:T(8,128)(2,1)S(1)} fusion(bf16[2048,128]{1,0:T(8,128)(2,1)} %bitcast.25, bf16[2048,768]{1,0:T(8,128)(2,1)} %all-gather.2.cloned.1.call-done), kind=kOutput, calls=%fused_computation.3 | convolution fusion | flops 402751488 | bytes 3866624 | tf_op jit(solution)/shard_map/dot_general | solution.py:55
  89.8 0.8 copy.20
  90.6 15.8 %all-to-all-start.4 = ((bf16[4,192,128]{2,1,0:T(8,128)(2,1)}), bf16[4,192,128]{2,1,0:T(8,128)(2,1)S(1)}, u32[]{:S(2)}, u32[]{:S(2)}) async-start(bf16[4,192,128]{2,1,0:T(8,128)(2,1)} %bitcast.9), calls=%async_computation.4 | async-start | bytes 393216 | tf_op jit(solution)/shard_map/all_to_all | solution.py:21
  106.4 0.1 pad.2.clone
  106.5 12.7 %all-to-all-done.4 = bf16[4,192,128]{2,1,0:T(8,128)(2,1)S(1)} async-done(((bf16[4,192,128]{2,1,0:T(8,128)(2,1)}), bf16[4,192,128]{2,1,0:T(8,128)(2,1)S(1)}, u32[]{:S(2)}, u32[]{:S(2)}) %all-to-all-start.4) | async-done | bytes 196640 | tf_op jit(solution)/shard_map/all_to_all | solution.py:21
  119.3 0.6 multiply_reduce_fusion
  119.9 0.7 pad.1.clone
  120.6 0.1 maximum_maximum_fusion
  120.7 16.6 %all_to_all.38 = f32[16,16,128]{2,1,0:T(8,128)S(1)} all-to-all(f32[16,16,128]{2,1,0:T(8,128)S(1)} %maximum_maximum_fusion), channel_id=1, replica_groups=mesh['zh'=4,'y'=8,'core'=2,'blk'=4,'tp'=4] {'y','core'}, dimensions={0} | all-to-all | bytes 262144 | tf_op jit(solution)/shard_map/all_to_all | solution.py:21
  137.3 0.6 slice_reduce_fusion.1
  137.9 0.7 broadcast_in_dim.11
  138.6 18.5 %all_to_all.39 = f32[64,1,128]{2,1,0:T(1,128)S(1)} all-to-all(f32[64,1,128]{2,1,0:T(1,128)S(1)} %broadcast_in_dim.11), channel_id=1, replica_groups=mesh['zh'=4,'y'=8,'core'=2,'blk'=4,'tp'=4] {'zh','blk','tp'}, dimensions={0} | all-to-all | bytes 65536 | tf_op jit(solution)/shard_map/all_to_all | solution.py:21
  157.0 0.7 slice_reduce_fusion
  158.4 0.7 copy.22
  (6 shorter events, 0.1 us)
Async XLA Ops:
  7.2 18.4 %copy-start = (bf16[768,2048]{1,0:T(8,128)(2,1)S(1)}, bf16[768,2048]{1,0:T(8,128)(2,1)}, u32[]{:S(2)}) copy-start(bf16[768,2048]{1,0:T(8,128)(2,1)} %param.6) | copy-start | bytes 9437188
  7.2 24.9 %copy-start.2 = (s32[128]{0:T(128)S(1)}, s32[128]{0:T(128)}, u32[]{:S(2)}) copy-start(s32[128]{0:T(128)} %param.9) | copy-start | bytes 1540
  7.2 37.4 %copy-start.1 = (f32[2048]{0:T(1024)S(1)}, f32[2048]{0:T(1024)}, u32[]{:S(2)}) copy-start(f32[2048]{0:T(1024)} %param.7) | copy-start | bytes 24580
  7.2 79.9 %all-gather.2.cloned.1.call-start = ((), (), s32[]{:S(2)}) async-start(), calls=%async_computation.7 | async-start | bytes 3342336 | tf_op jit(solution)/shard_map/all_gather | solution.py:38
  27.9 15.4 %all-to-all-start.1 = ((bf16[16,8,2048]{2,1,0:T(8,128)(2,1)}), bf16[16,8,2048]{2,1,0:T(8,128)(2,1)}, u32[]{:S(2)}, u32[]{:S(2)}) async-start(bf16[16,8,2048]{2,1,0:T(8,128)(2,1)} %fusion), calls=%async_computation.1 | async-start | bytes 1048576 | tf_op jit(solution)/shard_map/all_to_all | solution.py:21
  90.6 28.6 %all-to-all-start.4 = ((bf16[4,192,128]{2,1,0:T(8,128)(2,1)}), bf16[4,192,128]{2,1,0:T(8,128)(2,1)S(1)}, u32[]{:S(2)}, u32[]{:S(2)}) async-start(bf16[4,192,128]{2,1,0:T(8,128)(2,1)} %bitcast.9), calls=%async_computation.4 | async-start | bytes 393216 | tf_op jit(solution)/shard_map/all_to_all | solution.py:21
Sparse Core Ops, SparseCore 0:
  25.7 54.4 all-gather.1

commit v3 on v2

v3 whole, which is shorter than its diff:
```python
import functools

import jax
import jax.numpy as jnp
from jax import lax
from jax.experimental import pallas as pl
from jax.experimental.pallas import tpu as pltpu
from jax.sharding import Mesh, PartitionSpec as P

ZHI, YS, CORES = 4, 8, 2
REP = ("zh", "y", "core")
ALONG = ("y", "core")
GROUP = ("blk", "tp")
LANES = 128
BF16, F32 = jnp.bfloat16, jnp.float32


def exchange(blocks, axes):
    return lax.all_to_all(blocks, axes, split_axis=0, concat_axis=0, tiled=True)


def norm_backward_kernel(parts_ref, scaled_ref, out_ref):
    groups = parts_ref.shape[0]
    projected = parts_ref[0].astype(F32)
    for g in range(1, groups):
        projected += parts_ref[g].astype(F32)
    scaled = scaled_ref[...]
    inverse_rms = lax.rsqrt(jnp.mean(projected * projected, axis=1, keepdims=True) + 1e-06)
    normed = projected * inverse_rms
    along = jnp.mean(scaled * normed, axis=1, keepdims=True)
    token_grad = (inverse_rms * (scaled - normed * along)).astype(BF16)
    for j in range(out_ref.shape[0]):
        out_ref[j] = token_grad[:, j * LANES : (j + 1) * LANES]


def norm_backward(parts, scaled, slices):
    _, tok, width = parts.shape
    return pl.pallas_call(
        norm_backward_kernel,
        out_shape=jax.ShapeDtypeStruct((slices, tok, width // slices), BF16),
        name="norm_backward",
    )(parts, scaled)


def product_kernel(columns_ref, grads_ref, out_ref, total_ref):
    step = pl.program_id(0)

    @pl.when(step == 0)
    def _():
        total_ref[...] = jnp.zeros_like(total_ref)

    groups, chunk, tok, part = grads_ref.shape
    grads = grads_ref[...].astype(F32).transpose(1, 0, 2, 3).reshape(chunk * groups * tok, part)
    total_ref[...] += jnp.dot(grads.T.astype(BF16), columns_ref[...], preferred_element_type=F32)

    @pl.when(step == pl.num_programs(0) - 1)
    def _():
        out_ref[...] = total_ref[...].T.astype(BF16)


def product(all_columns, arrived, steps):
    groups, slices, tok, part = arrived.shape
    tokens, shard = all_columns.shape
    return pl.pallas_call(
        product_kernel,
        grid=(steps,),
        in_specs=[
            pl.BlockSpec((tokens // steps, shard), lambda i: (i, 0)),
            pl.BlockSpec((groups, slices // steps, tok, part), lambda i: (0, i, 0, 0)),
        ],
        out_specs=pl.BlockSpec((shard, part), lambda i: (0, 0)),
        out_shape=jax.ShapeDtypeStruct((shard, part), BF16),
        scratch_shapes=[pltpu.VMEM((part, shard), F32)],
        name="product",
    )(all_columns, arrived)


def gather_rows_kernel(own_rows, pieces_ref, out_ref):
    total = pieces_ref[0].astype(F32)
    for k in range(1, pieces_ref.shape[0]):
        total += pieces_ref[k].astype(F32)
    slices, padded, part = out_ref.shape
    squares = jnp.full((padded - own_rows, part), jnp.sum(total * total), F32)
    for j in range(slices):
        out_ref[j, :own_rows] = total[j * own_rows : (j + 1) * own_rows]
        out_ref[j, own_rows:] = squares


def gather_rows(pieces, own_rows, slices, padded):
    return pl.pallas_call(
        functools.partial(gather_rows_kernel, own_rows),
        out_shape=jax.ShapeDtypeStruct((slices, padded, pieces.shape[2]), F32),
        name="gather_rows",
    )(pieces)


def squares_kernel(own_rows, back_ref, out_ref):
    total = jnp.sum(back_ref[:, own_rows : own_rows + 1, :], axis=0)
    out_ref[...] = jnp.broadcast_to(total[None], out_ref.shape)


def spread_squares(back, own_rows, size):
    return pl.pallas_call(
        functools.partial(squares_kernel, own_rows),
        out_shape=jax.ShapeDtypeStruct((size, 1, back.shape[2]), F32),
        name="spread_squares",
    )(back)


def clip_kernel(limit_square, back_ref, squares_ref, out_ref, norm_ref):
    squares = jnp.sum(squares_ref[...], axis=0)
    norm = jnp.sqrt(squares)
    factor = jnp.minimum(1.0, jnp.sqrt(jnp.full_like(norm, limit_square)) / (norm + 1e-06))
    norm_ref[0, 0] = jnp.max(norm)
    slices, _, part = back_ref.shape
    for j in range(slices):
        for r in range(out_ref.shape[0]):
            out_ref[r, :, j * part : (j + 1) * part] = back_ref[j, r : r + 1, :] * factor


def clip(back, squares, own_rows, width, limit_square):
    return pl.pallas_call(
        functools.partial(clip_kernel, limit_square),
        out_shape=(
            jax.ShapeDtypeStruct((own_rows, 1, width), F32),
            jax.ShapeDtypeStruct((1, 1), F32),
        ),
        out_specs=(
            pl.BlockSpec(memory_space=pltpu.VMEM),
            pl.BlockSpec(memory_space=pltpu.SMEM),
        ),
        name="clip",
    )(back, squares)


def body(hidden, projection_weight, norm_gain, upstream, loss_mask):
    tok, joined = hidden.shape
    groups = lax.axis_size(GROUP)
    shard, width = projection_weight.shape
    slices = YS * CORES
    part = width // slices
    own_rows = shard // (ZHI * slices)

    sent = lax.optimization_barrier(hidden.reshape(tok, groups, shard).transpose(1, 0, 2))
    columns = exchange(sent, GROUP).reshape(groups * tok, shard)
    all_columns = lax.all_gather(columns, ALONG, axis=0, tiled=True)

    partial_value = jnp.dot(columns, projection_weight, preferred_element_type=F32).astype(BF16)
    parts = exchange(lax.optimization_barrier(partial_value.reshape(groups, tok, width)), GROUP)
    offset = lax.axis_index(GROUP) * tok
    own_cotangent = lax.dynamic_slice_in_dim(upstream, offset, tok, 0)
    own_mask = lax.dynamic_slice_in_dim(loss_mask, offset, tok, 0)
    scaled = norm_gain * (own_cotangent.astype(F32) * own_mask.astype(F32)[:, None])

    cut = exchange(norm_backward(parts, scaled, slices), ALONG)
    spread = lax.optimization_barrier(jnp.broadcast_to(cut[None], (groups, slices, tok, part)))
    arrived = exchange(spread, GROUP)
    block = product(all_columns, arrived, 4)
    by_zh = exchange(block.reshape(ZHI, shard // ZHI, part), "zh")

    back = exchange(gather_rows(by_zh, own_rows, slices, 16), ALONG)
    squares = exchange(spread_squares(back, own_rows, ZHI * groups), ("zh",) + GROUP)
    rows, grad_norm = clip(back, squares, own_rows, width, float(joined * width))
    return (rows.transpose(1, 0, 2), grad_norm.reshape(()))


def solution(mesh):
    sizes = (ZHI, YS, CORES, mesh.shape["blk"], mesh.shape["tp"])
    fine = Mesh(mesh.devices.reshape(sizes), REP + GROUP)
    return jax.shard_map(
        body,
        mesh=fine,
        in_specs=(
            P(REP + GROUP, None),
            P(GROUP, None),
            P(),
            P(REP, None),
            P(REP),
        ),
        out_specs=(P(GROUP, REP, None), P()),
        check_vma=False,
    )
```

time: 168 us -> 169 us (level)
  blocking collectives: 93.1 us -> 125 us
  starting transfers between devices: 20.1 us -> 4.29 us
  waiting for transfers between devices: 23.8 us -> 9.61 us
  Pallas kernels: 0 us -> 11.1 us
  local copies, waits for them, and re-layouts: 3.99 us -> 0.11 us
  other arithmetic: 5.19 us -> 1.54 us
  matrix products: 5 us -> 2.3 us
  between operations: 16 us -> 14.1 us
    all_to_all x5 -> x6, blocking collectives: 93.1 us -> 125 us  [exchange(): return lax.all_to_all(blocks, axes, split_axis=0, concat_axis=0, tiled=True)]
    all_to_all x2 -> x1, starting transfers between devices: 20 us -> 4.25 us  [exchange(): return lax.all_to_all(blocks, axes, split_axis=0, concat_axis=0, tiled=True)]
    all_to_all x2 -> x1, waiting for transfers between devices: 23.8 us -> 9.59 us  [exchange(): return lax.all_to_all(blocks, axes, split_axis=0, concat_axis=0, tiled=True)]
    pallas_call x0 -> x5, Pallas kernels: none -> 11.1 us  [the longest x1 4.16 us: product(): pl.pallas_call(product_kernel, grid=(steps,), in_specs=[pl.BlockSpec((tok...]
    reduce_sum x7 -> x0, other arithmetic: 4.15 us -> none  [the longest x1 1.12 us: body(): projected = jnp.sum(parts.astype(F32), axis=0)]
    dot_general x1 -> x0, matrix products: 2.68 us -> none  [body(): lax.dot_general(all_columns, token_grad, contract, preferred_element_type...]
  transfers between devices with their start and end apart: 3 -> 2, of which waited for: 2 -> 1; matrix products, arithmetic and copies ran while one was open for 4% -> 2% of each run, Pallas kernels for 0% -> 1%
where the time goes in v3:
time: 169 us; the launch traced here: 168 us
  blocking collectives  125 us (74%)
  between operations  14.1 us (8%)
  Pallas kernels  11.1 us (7%)
  waiting for transfers between devices  9.61 us (6%)
  starting transfers between devices  4.29 us (3%)
  matrix products  2.3 us (1%)
    all_to_all x6, blocking collectives, exchange(): return lax.all_to_all(blocks, axes, split_axis=0, concat_axis=0, tiled=True)  125 us
    all_to_all x1, waiting for transfers between devices, exchange(): return lax.all_to_all(blocks, axes, split_axis=0, concat_axis=0, tiled=True)  9.59 us
    all_to_all x1, starting transfers between devices, exchange(): return lax.all_to_all(blocks, axes, split_axis=0, concat_axis=0, tiled=True)  4.25 us
    pallas_call x1, Pallas kernels, product(): pl.pallas_call(product_kernel, grid=(steps,), in_specs=[pl.BlockSpec((tok...  4.16 us
  transfers between devices with their start and end apart: 2, of which 1 were waited for; matrix products, arithmetic and copies ran while one was open for 2% of the time, Pallas kernels for 1%

profile of v3, /device:TPU:1, one launch (start us, length us, event | category | flops | bytes accessed | tf_op | source)
XLA Modules:
  0.0 167.8 jit_solution(12335476772119912408)
XLA Ops:
  7.2 0.0 copy-start
  7.2 0.0 copy-start.2
  7.2 0.0 copy-start.1
  7.2 0.0 all-gather.2.cloned.1.call-start
  7.2 18.3 %all_to_all.35 = bf16[16,8,768]{2,1,0:T(8,128)(2,1)} all-to-all(bf16[16,8,768]{2,1,0:T(8,128)(2,1)} %bitcast.14), channel_id=1, replica_groups=mesh['zh'=4,'y'=8,'core'=2,'blk'=4,'tp'=4] {'blk','tp'}, dimensions={0} | all-to-all | bytes 393216 | tf_op jit(solution)/shard_map/all_to_all | solution.py:19
  25.5 0.0 all-gather.2.cloned.1.call-update
  25.5 0.0 copy-done
  25.6 2.3 %fusion = bf16[16,8,2048]{2,1,0:T(8,128)(2,1)} fusion(bf16[768,2048]{1,0:T(8,128)(2,1)S(1)} %copy-done, bf16[16,8,768]{2,1,0:T(8,128)(2,1)} %all_to_all.35), kind=kOutput, calls=%fused_computation.1 | convolution fusion | flops 402915328 | bytes 3866624 | tf_op jit(solution)/shard_map/dot_general | solution.py:148
  27.9 4.3 %all-to-all-start.1 = ((bf16[16,8,2048]{2,1,0:T(8,128)(2,1)}), bf16[16,8,2048]{2,1,0:T(8,128)(2,1)}, u32[]{:S(2)}, u32[]{:S(2)}) async-start(bf16[16,8,2048]{2,1,0:T(8,128)(2,1)} %fusion), calls=%async_computation.1 | async-start | bytes 1048576 | tf_op jit(solution)/shard_map/all_to_all | solution.py:19
  32.1 0.0 copy-done.2
  32.1 0.1 dynamic-slice_convert_fusion
  32.2 0.0 copy-done.1
  32.2 1.5 multiply_multiply_fusion.scaled_ref
  33.7 9.6 %all-to-all-done.1.parts_ref = bf16[16,8,2048]{2,1,0:T(8,128)(2,1)} async-done(((bf16[16,8,2048]{2,1,0:T(8,128)(2,1)}), bf16[16,8,2048]{2,1,0:T(8,128)(2,1)}, u32[]{:S(2)}, u32[]{:S(2)}) %all-to-all-start.1) | async-done | bytes 524320 | tf_op jit(solution)/shard_map/all_to_all | solution.py:19
  43.3 1.9 %norm_backward.1 = bf16[16,8,128]{2,1,0:T(8,128)(2,1)} custom-call(bf16[16,8,2048]{2,1,0:T(8,128)(2,1)} %all-to-all-done.1.parts_ref, f32[8,2048]{1,0:T(8,128)} %multiply_multiply_fusion.scaled_ref), custom_call_target="tpu_custom_call" | custom-call | tf_op jit(solution)/shard_map/norm_backward/pallas_call | solution.py:38
  45.2 21.6 %all_to_all.36 = bf16[16,8,128]{2,1,0:T(8,128)(2,1)S(1)} all-to-all(bf16[16,8,128]{2,1,0:T(8,128)(2,1)} %norm_backward.1), channel_id=1, replica_groups=mesh['zh'=4,'y'=8,'core'=2,'blk'=4,'tp'=4] {'y','core'}, dimensions={0} | all-to-all | bytes 65536 | tf_op jit(solution)/shard_map/all_to_all | solution.py:19
  66.8 0.1 broadcast_in_dim.2
  66.9 19.3 %all_to_all.37.grads_ref = bf16[16,16,8,128]{3,2,1,0:T(8,128)(2,1)} all-to-all(bf16[16,16,8,128]{3,2,1,0:T(8,128)(2,1)S(1)} %broadcast_in_dim.2), channel_id=1, replica_groups=mesh['zh'=4,'y'=8,'core'=2,'blk'=4,'tp'=4] {'blk','tp'}, dimensions={0} | all-to-all | bytes 1048576 | tf_op jit(solution)/shard_map/all_to_all | solution.py:19
  86.2 0.0 all-gather.2.cloned.1.call-done.columns_ref
  86.2 4.2 %product.1 = bf16[768,128]{1,0:T(8,128)(2,1)} custom-call(bf16[2048,768]{1,0:T(8,128)(2,1)} %all-gather.2.cloned.1.call-done.columns_ref, bf16[16,16,8,128]{3,2,1,0:T(8,128)(2,1)} %all_to_all.37.grads_ref), custom_call_target="tpu_custom_call" | custom-call | tf_op jit(solution)/shard_map/product/pallas_call | solution.py:64
  90.3 29.7 %all_to_all.38.pieces_ref = bf16[4,192,128]{2,1,0:T(8,128)(2,1)} all-to-all(bf16[4,192,128]{2,1,0:T(8,128)(2,1)} %bitcast.13), channel_id=1, replica_groups=mesh['zh'=4,'y'=8,'core'=2,'blk'=4,'tp'=4] {'zh'}, dimensions={0} | all-to-all | bytes 393216 | tf_op jit(solution)/shard_map/all_to_all | solution.py:19
  120.0 1.7 %gather_rows.1 = f32[16,16,128]{2,1,0:T(8,128)} custom-call(bf16[4,192,128]{2,1,0:T(8,128)(2,1)} %all_to_all.38.pieces_ref), custom_call_target="tpu_custom_call" | custom-call | tf_op jit(solution)/shard_map/gather_rows/pallas_call | solution.py:90
  121.7 16.9 %all_to_all.39.back_ref = f32[16,16,128]{2,1,0:T(8,128)} all-to-all(f32[16,16,128]{2,1,0:T(8,128)} %gather_rows.1), channel_id=1, replica_groups=mesh['zh'=4,'y'=8,'core'=2,'blk'=4,'tp'=4] {'y','core'}, dimensions={0} | all-to-all | bytes 262144 | tf_op jit(solution)/shard_map/all_to_all | solution.py:19
  138.6 1.6 spread_squares.1
  140.2 19.0 %all_to_all.40.squares_ref = f32[64,1,128]{2,1,0:T(1,128)} all-to-all(f32[64,1,128]{2,1,0:T(1,128)} %spread_squares.1), channel_id=1, replica_groups=mesh['zh'=4,'y'=8,'core'=2,'blk'=4,'tp'=4] {'zh','blk','tp'}, dimensions={0} | all-to-all | bytes 65536 | tf_op jit(solution)/shard_map/all_to_all | solution.py:19
  159.2 1.7 %clip.1 = (f32[12,1,2048]{2,1,0:T(1,128)}, f32[1,1]{1,0:T(1,128)}) custom-call(f32[16,16,128]{2,1,0:T(8,128)} %all_to_all.39.back_ref, f32[64,1,128]{2,1,0:T(1,128)} %all_to_all.40.squares_ref), custom_call_target="tpu_custom_call" | custom-call | tf_op jit(solution)/shard_map/clip/pallas_call | solution.py:122
Async XLA Ops:
  7.2 18.4 %copy-start = (bf16[768,2048]{1,0:T(8,128)(2,1)S(1)}, bf16[768,2048]{1,0:T(8,128)(2,1)}, u32[]{:S(2)}) copy-start(bf16[768,2048]{1,0:T(8,128)(2,1)} %param.6) | copy-start | bytes 9437188
  7.2 24.9 %copy-start.2 = (s32[128]{0:T(128)S(1)}, s32[128]{0:T(128)}, u32[]{:S(2)}) copy-start(s32[128]{0:T(128)} %param.9) | copy-start | bytes 1540
  7.2 25.0 %copy-start.1 = (f32[2048]{0:T(1024)S(1)}, f32[2048]{0:T(1024)}, u32[]{:S(2)}) copy-start(f32[2048]{0:T(1024)} %param.7) | copy-start | bytes 24580
  7.2 79.0 %all-gather.2.cloned.1.call-start = ((), (), s32[]{:S(2)}) async-start(), calls=%async_computation.7 | async-start | bytes 3342336 | tf_op jit(solution)/shard_map/all_gather | solution.py:146
  27.9 15.4 %all-to-all-start.1 = ((bf16[16,8,2048]{2,1,0:T(8,128)(2,1)}), bf16[16,8,2048]{2,1,0:T(8,128)(2,1)}, u32[]{:S(2)}, u32[]{:S(2)}) async-start(bf16[16,8,2048]{2,1,0:T(8,128)(2,1)} %fusion), calls=%async_computation.1 | async-start | bytes 1048576 | tf_op jit(solution)/shard_map/all_to_all | solution.py:19
Sparse Core Ops, SparseCore 0:
  25.7 54.3 all-gather.1

commit v4 on v3

--- a/solution.py
+++ b/solution.py
@@ -11,7 +11,7 @@
 REP = ("zh", "y", "core")
 ALONG = ("y", "core")
 GROUP = ("blk", "tp")
-LANES = 128
+EARLY = (3, 5, 2, 6)
 BF16, F32 = jnp.bfloat16, jnp.float32
 
 
@@ -29,8 +29,9 @@
     normed = projected * inverse_rms
     along = jnp.mean(scaled * normed, axis=1, keepdims=True)
     token_grad = (inverse_rms * (scaled - normed * along)).astype(BF16)
+    part = out_ref.shape[2]
     for j in range(out_ref.shape[0]):
-        out_ref[j] = token_grad[:, j * LANES : (j + 1) * LANES]
+        out_ref[j] = token_grad[:, j * part : (j + 1) * part]
 
 
 def norm_backward(parts, scaled, slices):
@@ -42,37 +43,35 @@
     )(parts, scaled)
 
 
-def product_kernel(columns_ref, grads_ref, out_ref, total_ref):
-    step = pl.program_id(0)
-
-    @pl.when(step == 0)
-    def _():
-        total_ref[...] = jnp.zeros_like(total_ref)
-
-    groups, chunk, tok, part = grads_ref.shape
-    grads = grads_ref[...].astype(F32).transpose(1, 0, 2, 3).reshape(chunk * groups * tok, part)
-    total_ref[...] += jnp.dot(grads.T.astype(BF16), columns_ref[...], preferred_element_type=F32)
-
-    @pl.when(step == pl.num_programs(0) - 1)
-    def _():
-        out_ref[...] = total_ref[...].T.astype(BF16)
+def product_kernel(place_ref, *refs):
+    column_refs, (grads_ref, keep_ref, give_ref, total_ref) = refs[:YS], refs[YS:]
+    y, core = place_ref[0], place_ref[1]
+    groups, _, tok, cols = grads_ref.shape
+    part = keep_ref.shape[1]
+    for step in range(YS):
+        source = lax.rem(y + (YS - step), YS)
+        grads = grads_ref[:, source].astype(F32).reshape(groups * tok, cols)
+        term = jnp.dot(grads.T.astype(BF16), column_refs[step][...], preferred_element_type=F32)
+        if step == 0:
+            total_ref[...] = term
+        else:
+            total_ref[...] += term
+    keep_ref[...] = total_ref[pl.ds(pl.multiple_of(core * part, part), part)].T
+    give_ref[...] = total_ref[pl.ds(pl.multiple_of((1 - core) * part, part), part)].T.astype(BF16)
 
 
-def product(all_columns, arrived, steps):
-    groups, slices, tok, part = arrived.shape
-    tokens, shard = all_columns.shape
+def product(chunks, arrived, place):
+    groups, _, tok, cols = arrived.shape
+    shard = chunks[0].shape[1]
+    half = (shard, cols // CORES)
     return pl.pallas_call(
         product_kernel,
-        grid=(steps,),
-        in_specs=[
-            pl.BlockSpec((tokens // steps, shard), lambda i: (i, 0)),
-            pl.BlockSpec((groups, slices // steps, tok, part), lambda i: (0, i, 0, 0)),
-        ],
-        out_specs=pl.BlockSpec((shard, part), lambda i: (0, 0)),
-        out_shape=jax.ShapeDtypeStruct((shard, part), BF16),
-        scratch_shapes=[pltpu.VMEM((part, shard), F32)],
+        in_specs=[pl.BlockSpec(memory_space=pltpu.SMEM)]
+        + [pl.BlockSpec(memory_space=pltpu.VMEM)] * (YS + 1),
+        out_shape=(jax.ShapeDtypeStruct(half, F32), jax.ShapeDtypeStruct(half, BF16)),
+        scratch_shapes=[pltpu.VMEM((cols, shard), F32)],
         name="product",
-    )(all_columns, arrived)
+    )(place, *chunks, arrived)
 
 
 def gather_rows_kernel(own_rows, pieces_ref, out_ref):
@@ -143,7 +142,9 @@
 
     sent = lax.optimization_barrier(hidden.reshape(tok, groups, shard).transpose(1, 0, 2))
     columns = exchange(sent, GROUP).reshape(groups * tok, shard)
-    all_columns = lax.all_gather(columns, ALONG, axis=0, tiled=True)
+    chunks = {0: columns}
+    for step in EARLY + (4, 1, 7):
+        chunks[step] = lax.ppermute(columns, "y", [(i, (i + step) % YS) for i in range(YS)])
 
     partial_value = jnp.dot(columns, projection_weight, preferred_element_type=F32).astype(BF16)
     parts = exchange(lax.optimization_barrier(partial_value.reshape(groups, tok, width)), GROUP)
@@ -152,10 +153,15 @@
     own_mask = lax.dynamic_slice_in_dim(loss_mask, offset, tok, 0)
     scaled = norm_gain * (own_cotangent.astype(F32) * own_mask.astype(F32)[:, None])
 
-    cut = exchange(norm_backward(parts, scaled, slices), ALONG)
-    spread = lax.optimization_barrier(jnp.broadcast_to(cut[None], (groups, slices, tok, part)))
+    cut = exchange(norm_backward(parts, scaled, YS), "y")
+    cut, *early = lax.optimization_barrier((cut, *(chunks[step] for step in EARLY)))
+    for step, chunk in zip(EARLY, early):
+        chunks[step] = chunk
+    spread = lax.optimization_barrier(jnp.broadcast_to(cut[None], (groups, YS, tok, CORES * part)))
     arrived = exchange(spread, GROUP)
-    block = product(all_columns, arrived, 4)
+    place = jnp.stack([lax.axis_index("y"), lax.axis_index("core")]).astype(jnp.int32)
+    keep, give = product([chunks[step] for step in range(YS)], arrived, place)
+    block = (keep + lax.ppermute(give, "core", [(0, 1), (1, 0)]).astype(F32)).astype(BF16)
     by_zh = exchange(block.reshape(ZHI, shard // ZHI, part), "zh")
 
     back = exchange(gather_rows(by_zh, own_rows, slices, 16), ALONG)

time: 169 us -> 175 us (1.036)
  starting transfers between devices: 4.29 us -> 52.7 us
  blocking collectives: 125 us -> 88.5 us
  between operations: 14.1 us -> 0.82 us
  waiting for transfers between devices: 9.61 us -> 14.9 us
    all_to_all x6 -> x4, blocking collectives: 125 us -> 88.5 us  [exchange(): return lax.all_to_all(blocks, axes, split_axis=0, concat_axis=0, tiled=True)]
    ppermute x0 -> x8, starting transfers between devices: none -> 35.1 us  [the longest x7 28.2 us: body(): lax.ppermute(columns, 'y', [(i, (i + step) % YS) for i in range(YS)])]
    ppermute x0 -> x8, waiting for transfers between devices: none -> 14 us  [the longest x7 12.8 us: body(): lax.ppermute(columns, 'y', [(i, (i + step) % YS) for i in range(YS)])]
    all_to_all x1 -> x3, starting transfers between devices: 4.25 us -> 17.6 us  [exchange(): return lax.all_to_all(blocks, axes, split_axis=0, concat_axis=0, tiled=True)]
    all_to_all x1 -> x3, waiting for transfers between devices: 9.59 us -> 0.85 us  [exchange(): return lax.all_to_all(blocks, axes, split_axis=0, concat_axis=0, tiled=True)]
  transfers between devices with their start and end apart: 2 -> 11, of which waited for: 1 -> 4; matrix products, arithmetic and copies ran while one was open for 2% -> 1% of each run, Pallas kernels for 1% -> 1%
where the time goes in v4:
time: 175 us; the launch traced here: 174 us
  blocking collectives  88.5 us (51%)
  starting transfers between devices  52.7 us (30%)
  waiting for transfers between devices  14.9 us (9%)
  Pallas kernels  10.6 us (6%)
  other arithmetic  3.17 us (2%)
    all_to_all x4, blocking collectives, exchange(): return lax.all_to_all(blocks, axes, split_axis=0, concat_axis=0, tiled=True)  88.5 us
    ppermute x7, starting transfers between devices, body(): lax.ppermute(columns, 'y', [(i, (i + step) % YS) for i in range(YS)])  28.2 us
    all_to_all x3, starting transfers between devices, exchange(): return lax.all_to_all(blocks, axes, split_axis=0, concat_axis=0, tiled=True)  17.6 us
    ppermute x7, waiting for transfers between devices, body(): lax.ppermute(columns, 'y', [(i, (i + step) % YS) for i in range(YS)])  12.8 us
    ppermute x1, starting transfers between devices, body(): lax.ppermute(give, 'core', [(0, 1), (1, 0)]).astype(F32)  6.93 us
    pallas_call x1, Pallas kernels, product(): pl.pallas_call(product_kernel, in_specs=[pl.BlockSpec(memory_space=pltpu....  3.67 us
  transfers between devices with their start and end apart: 11, of which 4 were waited for; matrix products, arithmetic and copies ran while one was open for 1% of the time, Pallas kernels for 1%

profile of v4, /device:TPU:1, one launch (start us, length us, event | category | flops | bytes accessed | tf_op | source)
XLA Modules:
  0.0 173.7 jit_solution(4869666327980945423)
XLA Ops:
  0.6 0.0 copy-start
  0.6 0.0 copy-start.4
  0.7 0.0 copy-start.3
  0.7 18.2 %all_to_all.35 = bf16[16,8,768]{2,1,0:T(8,128)(2,1)S(1)} all-to-all(bf16[16,8,768]{2,1,0:T(8,128)(2,1)} %bitcast.23), channel_id=1, replica_groups=mesh['zh'=4,'y'=8,'core'=2,'blk'=4,'tp'=4] {'blk','tp'}, dimensions={0} | all-to-all | bytes 393216 | tf_op jit(solution)/shard_map/all_to_all | solution.py:19
  18.8 0.0 copy-done
  18.8 0.0 copy-start.1
  18.8 1.4 fusion
  20.2 4.2 %all-to-all-start.1 = ((bf16[16,8,2048]{2,1,0:T(8,128)(2,1)}), bf16[16,8,2048]{2,1,0:T(8,128)(2,1)}, u32[]{:S(2)}, u32[]{:S(2)}) async-start(bf16[16,8,2048]{2,1,0:T(8,128)(2,1)} %fusion), calls=%async_computation.1 | async-start | bytes 1048576 | tf_op jit(solution)/shard_map/all_to_all | solution.py:19
  24.5 0.0 copy-done.4
  24.5 0.1 dynamic-slice_convert_fusion
  24.6 5.8 %collective-permute-start.1 = (bf16[128,768]{1,0:T(8,128)(2,1)S(1)}, bf16[128,768]{1,0:T(8,128)(2,1)S(1)}, u32[]{:S(2)}, u32[]{:S(2)}) collective-permute-start(bf16[128,768]{1,0:T(8,128)(2,1)S(1)} %bitcast.14), channel_id=1, source_target_pairs={{0,96},{32,128},{64,160},{96,192},{128,224},{160,0},{192,32},{224,... | collective-permute-start | bytes 589832 | tf_op jit(solution)/shard_map/ppermute | solution.py:147
  30.4 3.4 %collective-permute-start.2 = (bf16[128,768]{1,0:T(8,128)(2,1)S(1)}, bf16[128,768]{1,0:T(8,128)(2,1)}, u32[]{:S(2)}, u32[]{:S(2)}) collective-permute-start(bf16[128,768]{1,0:T(8,128)(2,1)S(1)} %bitcast.15), channel_id=1, source_target_pairs={{0,160},{32,192},{64,224},{96,0},{128,32},{160,64},{192,96},{224,1... | collective-permute-start | bytes 589832 | tf_op jit(solution)/shard_map/ppermute | solution.py:147
  33.8 3.9 %collective-permute-start.3 = (bf16[128,768]{1,0:T(8,128)(2,1)S(1)}, bf16[128,768]{1,0:T(8,128)(2,1)}, u32[]{:S(2)}, u32[]{:S(2)}) collective-permute-start(bf16[128,768]{1,0:T(8,128)(2,1)S(1)} %bitcast.16), channel_id=1, source_target_pairs={{0,64},{32,96},{64,128},{96,160},{128,192},{160,224},{192,0},{224,... | collective-permute-start | bytes 589832 | tf_op jit(solution)/shard_map/ppermute | solution.py:147
  37.7 3.6 %collective-permute-start.4 = (bf16[128,768]{1,0:T(8,128)(2,1)S(1)}, bf16[128,768]{1,0:T(8,128)(2,1)}, u32[]{:S(2)}, u32[]{:S(2)}) collective-permute-start(bf16[128,768]{1,0:T(8,128)(2,1)S(1)} %bitcast.17), channel_id=1, source_target_pairs={{0,192},{32,224},{64,0},{96,32},{128,64},{160,96},{192,128},{224,1... | collective-permute-start | bytes 589832 | tf_op jit(solution)/shard_map/ppermute | solution.py:147
  41.3 0.0 copy-done.3
  41.3 1.5 multiply_multiply_fusion.scaled_ref
  42.8 0.0 all-to-all-done.1.parts_ref
  42.8 1.9 %norm_backward.1 = bf16[8,8,256]{2,1,0:T(8,128)(2,1)} custom-call(bf16[16,8,2048]{2,1,0:T(8,128)(2,1)} %all-to-all-done.1.parts_ref, f32[8,2048]{1,0:T(8,128)} %multiply_multiply_fusion.scaled_ref), custom_call_target="tpu_custom_call" | custom-call | tf_op jit(solution)/shard_map/norm_backward/pallas_call | solution.py:39
  44.7 6.4 %all-to-all-start.2 = ((bf16[8,8,256]{2,1,0:T(8,128)(2,1)}), bf16[8,8,256]{2,1,0:T(8,128)(2,1)}, u32[]{:S(2)}, u32[]{:S(2)}) async-start(bf16[8,8,256]{2,1,0:T(8,128)(2,1)} %norm_backward.1), calls=%async_computation.2 | async-start | bytes 65536 | tf_op jit(solution)/shard_map/all_to_all | solution.py:19
  51.1 0.0 collective-permute-done.1.refs_3_
  51.1 0.0 copy-start.2
  51.1 0.0 collective-permute-done.2.refs_5_
  51.1 0.0 collective-permute-done.3.refs_2_
  51.1 6.1 %collective-permute-done.4.refs_6_ = bf16[128,768]{1,0:T(8,128)(2,1)} collective-permute-done((bf16[128,768]{1,0:T(8,128)(2,1)S(1)}, bf16[128,768]{1,0:T(8,128)(2,1)}, u32[]{:S(2)}, u32[]{:S(2)}) %collective-permute-start.4) | collective-permute-done | bytes 196640 | tf_op jit(solution)/shard_map/ppermute | solution.py:147
  57.2 0.8 all-to-all-done.2
  58.0 1.6 broadcast_in_dim.2
  59.6 6.9 %all-to-all-start.3 = ((bf16[16,8,8,256]{3,2,1,0:T(8,128)(2,1)}), bf16[16,8,8,256]{3,2,1,0:T(8,128)(2,1)}, u32[]{:S(2)}, u32[]{:S(2)}) async-start(bf16[16,8,8,256]{3,2,1,0:T(8,128)(2,1)} %broadcast_in_dim.2), calls=%async_computation.3 | async-start | bytes 1048576 | tf_op jit(solution)/shard_map/all_to_all | solution.py:19
  66.6 5.4 %collective-permute-start = (bf16[128,768]{1,0:T(8,128)(2,1)S(1)}, bf16[128,768]{1,0:T(8,128)(2,1)}, u32[]{:S(2)}, u32[]{:S(2)}) collective-permute-start(bf16[128,768]{1,0:T(8,128)(2,1)S(1)} %bitcast.18), channel_id=1, source_target_pairs={{0,32},{32,64},{64,96},{96,128},{128,160},{160,192},{192,224},{224... | collective-permute-start | bytes 589832 | tf_op jit(solution)/shard_map/ppermute | solution.py:147
  72.0 1.9 %collective-permute-start.5 = (bf16[128,768]{1,0:T(8,128)(2,1)S(1)}, bf16[128,768]{1,0:T(8,128)(2,1)}, u32[]{:S(2)}, u32[]{:S(2)}) collective-permute-start(bf16[128,768]{1,0:T(8,128)(2,1)S(1)} %bitcast.19), channel_id=1, source_target_pairs={{0,128},{32,160},{64,192},{96,224},{128,0},{160,32},{192,64},{224,... | collective-permute-start | bytes 589832 | tf_op jit(solution)/shard_map/ppermute | solution.py:147
  73.9 0.0 copy-done.1
  73.9 4.1 %collective-permute-start.6 = (bf16[128,768]{1,0:T(8,128)(2,1)S(1)}, bf16[128,768]{1,0:T(8,128)(2,1)}, u32[]{:S(2)}, u32[]{:S(2)}) collective-permute-start(bf16[128,768]{1,0:T(8,128)(2,1)S(1)} %bitcast.20), channel_id=1, source_target_pairs={{0,224},{32,0},{64,32},{96,64},{128,96},{160,128},{192,160},{224,1... | collective-permute-start | bytes 589832 | tf_op jit(solution)/shard_map/ppermute | solution.py:147
  78.1 0.6 pad_add_fusion.place_ref
  78.7 0.0 collective-permute-done.refs_1_
  78.7 6.7 %collective-permute-done.5.refs_4_ = bf16[128,768]{1,0:T(8,128)(2,1)} collective-permute-done((bf16[128,768]{1,0:T(8,128)(2,1)S(1)}, bf16[128,768]{1,0:T(8,128)(2,1)}, u32[]{:S(2)}, u32[]{:S(2)}) %collective-permute-start.5) | collective-permute-done | bytes 196640 | tf_op jit(solution)/shard_map/ppermute | solution.py:147
  85.4 0.0 collective-permute-done.6.refs_7_
  85.4 0.0 all-to-all-done.3.refs_8_
  85.4 0.0 copy-done.2
  85.4 3.7 %product.1 = (f32[768,128]{1,0:T(8,128)}, bf16[768,128]{1,0:T(8,128)(2,1)}) custom-call(s32[2]{0:T(128)} %pad_add_fusion.place_ref, bf16[128,768]{1,0:T(8,128)(2,1)} %bitcast.21, bf16[128,768]{1,0:T(8,128)(2,1)} %collective-permute-done.refs_1_, bf16[128,768]{1,0:T(8,128)(2,1)} %collective-permute-done.3.refs_2_, bf16[128,768]{1,0:T(8,128)(2,1)} %copy-done.2, ...), custom_call_target="tpu_custom_call" | custom-call | tf_op jit(solution)/shard_map/product/pallas_call | solution.py:67
  89.1 6.9 %collective-permute-start.7 = (bf16[768,128]{1,0:T(8,128)(2,1)}, bf16[768,128]{1,0:T(8,128)(2,1)S(1)}, u32[]{:S(2)}, u32[]{:S(2)}) collective-permute-start(bf16[768,128]{1,0:T(8,128)(2,1)} %get-tuple-element.17), channel_id=1, source_target_pairs={{0,16},{16,0},{1,17},{17,1},{2,18},{18,2},{3,19},{19,3},{4,20},{20... | collective-permute-start | bytes 589832 | tf_op jit(solution)/shard_map/ppermute | solution.py:164
  96.0 1.3 collective-permute-done.7
  97.3 1.0 add_convert_fusion
  98.3 27.6 %all_to_all.36.pieces_ref = bf16[4,192,128]{2,1,0:T(8,128)(2,1)} all-to-all(bf16[4,192,128]{2,1,0:T(8,128)(2,1)S(1)} %bitcast.22), channel_id=1, replica_groups=mesh['zh'=4,'y'=8,'core'=2,'blk'=4,'tp'=4] {'zh'}, dimensions={0} | all-to-all | bytes 393216 | tf_op jit(solution)/shard_map/all_to_all | solution.py:19
  125.9 1.7 %gather_rows.1 = f32[16,16,128]{2,1,0:T(8,128)} custom-call(bf16[4,192,128]{2,1,0:T(8,128)(2,1)} %all_to_all.36.pieces_ref), custom_call_target="tpu_custom_call" | custom-call | tf_op jit(solution)/shard_map/gather_rows/pallas_call | solution.py:89
  127.7 21.5 %all_to_all.37.back_ref = f32[16,16,128]{2,1,0:T(8,128)} all-to-all(f32[16,16,128]{2,1,0:T(8,128)} %gather_rows.1), channel_id=1, replica_groups=mesh['zh'=4,'y'=8,'core'=2,'blk'=4,'tp'=4] {'y','core'}, dimensions={0} | all-to-all | bytes 262144 | tf_op jit(solution)/shard_map/all_to_all | solution.py:19
  149.2 1.6 spread_squares.1
  150.8 21.2 %all_to_all.38.squares_ref = f32[64,1,128]{2,1,0:T(1,128)} all-to-all(f32[64,1,128]{2,1,0:T(1,128)} %spread_squares.1), channel_id=1, replica_groups=mesh['zh'=4,'y'=8,'core'=2,'blk'=4,'tp'=4] {'zh','blk','tp'}, dimensions={0} | all-to-all | bytes 65536 | tf_op jit(solution)/shard_map/all_to_all | solution.py:19
  172.0 1.7 clip.1
Async XLA Ops:
  0.6 18.2 %copy-start = (bf16[768,2048]{1,0:T(8,128)(2,1)S(1)}, bf16[768,2048]{1,0:T(8,128)(2,1)}, u32[]{:S(2)}) copy-start(bf16[768,2048]{1,0:T(8,128)(2,1)} %param.6) | copy-start | bytes 9437188
  0.6 23.8 %copy-start.4 = (s32[128]{0:T(128)S(1)}, s32[128]{0:T(128)}, u32[]{:S(2)}) copy-start(s32[128]{0:T(128)} %param.9) | copy-start | bytes 1540
  0.7 40.6 %copy-start.3 = (f32[2048]{0:T(1024)S(1)}, f32[2048]{0:T(1024)}, u32[]{:S(2)}) copy-start(f32[2048]{0:T(1024)} %param.7) | copy-start | bytes 24580
  18.8 55.1 %copy-start.1 = (bf16[16,8,768]{2,1,0:T(8,128)(2,1)}, bf16[16,8,768]{2,1,0:T(8,128)(2,1)S(1)}, u32[]{:S(2)}) copy-start(bf16[16,8,768]{2,1,0:T(8,128)(2,1)S(1)} %all_to_all.35) | copy-start | bytes 589828
  20.2 22.6 %all-to-all-start.1 = ((bf16[16,8,2048]{2,1,0:T(8,128)(2,1)}), bf16[16,8,2048]{2,1,0:T(8,128)(2,1)}, u32[]{:S(2)}, u32[]{:S(2)}) async-start(bf16[16,8,2048]{2,1,0:T(8,128)(2,1)} %fusion), calls=%async_computation.1 | async-start | bytes 1048576 | tf_op jit(solution)/shard_map/all_to_all | solution.py:19
  24.6 26.5 %collective-permute-start.1 = (bf16[128,768]{1,0:T(8,128)(2,1)S(1)}, bf16[128,768]{1,0:T(8,128)(2,1)S(1)}, u32[]{:S(2)}, u32[]{:S(2)}) collective-permute-start(bf16[128,768]{1,0:T(8,128)(2,1)S(1)} %bitcast.14), channel_id=1, source_target_pairs={{0,96},{32,128},{64,160},{96,192},{128,224},{160,0},{192,32},{224,... | collective-permute-start | bytes 589832 | tf_op jit(solution)/shard_map/ppermute | solution.py:147
  30.4 20.7 %collective-permute-start.2 = (bf16[128,768]{1,0:T(8,128)(2,1)S(1)}, bf16[128,768]{1,0:T(8,128)(2,1)}, u32[]{:S(2)}, u32[]{:S(2)}) collective-permute-start(bf16[128,768]{1,0:T(8,128)(2,1)S(1)} %bitcast.15), channel_id=1, source_target_pairs={{0,160},{32,192},{64,224},{96,0},{128,32},{160,64},{192,96},{224,1... | collective-permute-start | bytes 589832 | tf_op jit(solution)/shard_map/ppermute | solution.py:147
  33.8 17.4 %collective-permute-start.3 = (bf16[128,768]{1,0:T(8,128)(2,1)S(1)}, bf16[128,768]{1,0:T(8,128)(2,1)}, u32[]{:S(2)}, u32[]{:S(2)}) collective-permute-start(bf16[128,768]{1,0:T(8,128)(2,1)S(1)} %bitcast.16), channel_id=1, source_target_pairs={{0,64},{32,96},{64,128},{96,160},{128,192},{160,224},{192,0},{224,... | collective-permute-start | bytes 589832 | tf_op jit(solution)/shard_map/ppermute | solution.py:147
  37.7 19.5 %collective-permute-start.4 = (bf16[128,768]{1,0:T(8,128)(2,1)S(1)}, bf16[128,768]{1,0:T(8,128)(2,1)}, u32[]{:S(2)}, u32[]{:S(2)}) collective-permute-start(bf16[128,768]{1,0:T(8,128)(2,1)S(1)} %bitcast.17), channel_id=1, source_target_pairs={{0,192},{32,224},{64,0},{96,32},{128,64},{160,96},{192,128},{224,1... | collective-permute-start | bytes 589832 | tf_op jit(solution)/shard_map/ppermute | solution.py:147
  44.7 13.3 %all-to-all-start.2 = ((bf16[8,8,256]{2,1,0:T(8,128)(2,1)}), bf16[8,8,256]{2,1,0:T(8,128)(2,1)}, u32[]{:S(2)}, u32[]{:S(2)}) async-start(bf16[8,8,256]{2,1,0:T(8,128)(2,1)} %norm_backward.1), calls=%async_computation.2 | async-start | bytes 65536 | tf_op jit(solution)/shard_map/all_to_all | solution.py:19
  51.1 34.3 %copy-start.2 = (bf16[128,768]{1,0:T(8,128)(2,1)}, bf16[128,768]{1,0:T(8,128)(2,1)S(1)}, u32[]{:S(2)}) copy-start(bf16[128,768]{1,0:T(8,128)(2,1)S(1)} %collective-permute-done.1.refs_3_) | copy-start | bytes 589828
  59.6 25.8 %all-to-all-start.3 = ((bf16[16,8,8,256]{3,2,1,0:T(8,128)(2,1)}), bf16[16,8,8,256]{3,2,1,0:T(8,128)(2,1)}, u32[]{:S(2)}, u32[]{:S(2)}) async-start(bf16[16,8,8,256]{3,2,1,0:T(8,128)(2,1)} %broadcast_in_dim.2), calls=%async_computation.3 | async-start | bytes 1048576 | tf_op jit(solution)/shard_map/all_to_all | solution.py:19
  66.6 12.1 %collective-permute-start = (bf16[128,768]{1,0:T(8,128)(2,1)S(1)}, bf16[128,768]{1,0:T(8,128)(2,1)}, u32[]{:S(2)}, u32[]{:S(2)}) collective-permute-start(bf16[128,768]{1,0:T(8,128)(2,1)S(1)} %bitcast.18), channel_id=1, source_target_pairs={{0,32},{32,64},{64,96},{96,128},{128,160},{160,192},{192,224},{224... | collective-permute-start | bytes 589832 | tf_op jit(solution)/shard_map/ppermute | solution.py:147
  72.0 13.4 %collective-permute-start.5 = (bf16[128,768]{1,0:T(8,128)(2,1)S(1)}, bf16[128,768]{1,0:T(8,128)(2,1)}, u32[]{:S(2)}, u32[]{:S(2)}) collective-permute-start(bf16[128,768]{1,0:T(8,128)(2,1)S(1)} %bitcast.19), channel_id=1, source_target_pairs={{0,128},{32,160},{64,192},{96,224},{128,0},{160,32},{192,64},{224,... | collective-permute-start | bytes 589832 | tf_op jit(solution)/shard_map/ppermute | solution.py:147
  73.9 11.5 %collective-permute-start.6 = (bf16[128,768]{1,0:T(8,128)(2,1)S(1)}, bf16[128,768]{1,0:T(8,128)(2,1)}, u32[]{:S(2)}, u32[]{:S(2)}) collective-permute-start(bf16[128,768]{1,0:T(8,128)(2,1)S(1)} %bitcast.20), channel_id=1, source_target_pairs={{0,224},{32,0},{64,32},{96,64},{128,96},{160,128},{192,160},{224,1... | collective-permute-start | bytes 589832 | tf_op jit(solution)/shard_map/ppermute | solution.py:147
  89.1 8.2 %collective-permute-start.7 = (bf16[768,128]{1,0:T(8,128)(2,1)}, bf16[768,128]{1,0:T(8,128)(2,1)S(1)}, u32[]{:S(2)}, u32[]{:S(2)}) collective-permute-start(bf16[768,128]{1,0:T(8,128)(2,1)} %get-tuple-element.17), channel_id=1, source_target_pairs={{0,16},{16,0},{1,17},{17,1},{2,18},{18,2},{3,19},{19,3},{4,20},{20... | collective-permute-start | bytes 589832 | tf_op jit(solution)/shard_map/ppermute | solution.py:164

commit v5 on v3

v5 whole, which is shorter than its diff:
```python
import functools

import jax
import jax.numpy as jnp
from jax import lax
from jax.experimental import pallas as pl
from jax.experimental.pallas import tpu as pltpu
from jax.sharding import Mesh, PartitionSpec as P

ZHI, QS, PS, CORES = 4, 4, 2, 2
REP = ("zh", "q", "p", "core")
NEAR = ("q", "core")
ALONG = ("q", "p", "core")
GROUP = ("blk", "tp")
PAIR = [(0, 1), (1, 0)]
BF16, F32 = jnp.bfloat16, jnp.float32


def exchange(blocks, axes):
    return lax.all_to_all(blocks, axes, split_axis=0, concat_axis=0, tiled=True)


def norm_backward_kernel(parts_ref, scaled_ref, out_ref):
    groups = parts_ref.shape[0]
    projected = parts_ref[0].astype(F32)
    for g in range(1, groups):
        projected += parts_ref[g].astype(F32)
    scaled = scaled_ref[...]
    inverse_rms = lax.rsqrt(jnp.mean(projected * projected, axis=1, keepdims=True) + 1e-06)
    normed = projected * inverse_rms
    along = jnp.mean(scaled * normed, axis=1, keepdims=True)
    token_grad = (inverse_rms * (scaled - normed * along)).astype(BF16)
    part = out_ref.shape[2]
    for j in range(out_ref.shape[0]):
        out_ref[j] = token_grad[:, j * part : (j + 1) * part]


def norm_backward(parts, scaled, slices):
    _, tok, width = parts.shape
    return pl.pallas_call(
        norm_backward_kernel,
        out_shape=jax.ShapeDtypeStruct((slices, tok, width // slices), BF16),
        name="norm_backward",
    )(parts, scaled)


def product_kernel(place_ref, own_ref, other_ref, grads_ref, keep_ref, give_ref, rows_ref, total_ref):
    q, p, core = place_ref[0], place_ref[1], place_ref[2]
    groups, _, _, tok, part = grads_ref.shape
    for step in range(QS):
        source = lax.rem(q + (QS - step), QS)
        for place, columns_ref in ((core, own_ref), (1 - core, other_ref)):
            grads = grads_ref[:, source, place].astype(F32).reshape(groups * tok, part)
            term = jnp.dot(grads.T.astype(BF16), columns_ref[step], preferred_element_type=F32)
            if step == 0 and columns_ref is own_ref:
                total_ref[...] = term
            else:
                total_ref[...] += term
    rows_ref[...] = total_ref[...].T.reshape(rows_ref.shape)
    keep_ref[...] = rows_ref[:, p].reshape(keep_ref.shape)
    give_ref[...] = rows_ref[:, 1 - p].reshape(give_ref.shape).astype(BF16)


def product(own, other, arrived, place, own_rows):
    part = arrived.shape[-1]
    shard = own.shape[2]
    half = (shard // PS, part)
    return pl.pallas_call(
        product_kernel,
        in_specs=[pl.BlockSpec(memory_space=pltpu.SMEM)]
        + [pl.BlockSpec(memory_space=pltpu.VMEM)] * 3,
        out_shape=(jax.ShapeDtypeStruct(half, F32), jax.ShapeDtypeStruct(half, BF16)),
        scratch_shapes=[
            pltpu.VMEM((ZHI * QS, PS, CORES * own_rows, part), F32),
            pltpu.VMEM((part, shard), F32),
        ],
        name="product",
    )(place, own, other, arrived)


def gather_rows_kernel(own_rows, pieces_ref, out_ref):
    total = pieces_ref[0].astype(F32)
    for k in range(1, pieces_ref.shape[0]):
        total += pieces_ref[k].astype(F32)
    slices, padded, part = out_ref.shape
    squares = jnp.full((padded - own_rows, part), jnp.sum(total * total), F32)
    for j in range(slices):
        k = (j // (PS * CORES)) * CORES + j % CORES
        out_ref[j, :own_rows] = total[k * own_rows : (k + 1) * own_rows]
        out_ref[j, own_rows:] = squares


def gather_rows(pieces, own_rows, slices, padded):
    return pl.pallas_call(
        functools.partial(gather_rows_kernel, own_rows),
        out_shape=jax.ShapeDtypeStruct((slices, padded, pieces.shape[2]), F32),
        name="gather_rows",
    )(pieces)


def squares_kernel(own_rows, back_ref, out_ref):
    total = jnp.sum(back_ref[:, own_rows : own_rows + 1, :], axis=0)
    out_ref[...] = jnp.broadcast_to(total[None, :, : out_ref.shape[2]], out_ref.shape)


def spread_squares(back, own_rows, size):
    return pl.pallas_call(
        functools.partial(squares_kernel, own_rows),
        out_shape=jax.ShapeDtypeStruct((size, 1, 128), F32),
        name="spread_squares",
    )(back)


def clip_kernel(limit_square, place_ref, back_ref, squares_ref, out_ref, norm_ref):
    squares = jnp.sum(squares_ref[...], axis=0)
    norm = jnp.sqrt(squares)
    factor = jnp.minimum(1.0, jnp.sqrt(jnp.full_like(norm, limit_square)) / (norm + 1e-06))
    norm_ref[0, 0] = jnp.max(norm)
    factor = jnp.concatenate([factor] * (back_ref.shape[2] // factor.shape[1]), axis=1)
    part = back_ref.shape[2]
    p = place_ref[1]
    for k in range(QS * CORES):
        rows = back_ref[(k // CORES) * (PS * CORES) + p * CORES + k % CORES]
        for r in range(out_ref.shape[0]):
            out_ref[r, :, k * part : (k + 1) * part] = rows[r : r + 1, :] * factor


def clip(place, back, squares, own_rows, width, limit_square):
    return pl.pallas_call(
        functools.partial(clip_kernel, limit_square),
        out_shape=(
            jax.ShapeDtypeStruct((own_rows, 1, width), F32),
            jax.ShapeDtypeStruct((1, 1), F32),
        ),
        in_specs=[
            pl.BlockSpec(memory_space=pltpu.SMEM),
            pl.BlockSpec(memory_space=pltpu.VMEM),
            pl.BlockSpec(memory_space=pltpu.VMEM),
        ],
        out_specs=(
            pl.BlockSpec(memory_space=pltpu.VMEM),
            pl.BlockSpec(memory_space=pltpu.SMEM),
        ),
        name="clip",
    )(place, back, squares)


def body(hidden, projection_weight, norm_gain, upstream, loss_mask):
    tok, joined = hidden.shape
    groups = lax.axis_size(GROUP)
    shard, width = projection_weight.shape
    slices = QS * CORES
    part = width // slices
    own_rows = shard // (ZHI * slices * PS)
    place = jnp.stack([lax.axis_index(axis) for axis in ALONG]).astype(jnp.int32)

    sent = lax.optimization_barrier(hidden.reshape(tok, groups, shard).transpose(1, 0, 2))
    columns = exchange(sent, GROUP).reshape(groups * tok, shard)
    chunks = {0: columns}
    for step in (2, 1, 3):
        chunks[step] = lax.ppermute(columns, "q", [(i, (i + step) % QS) for i in range(QS)])

    partial_value = jnp.dot(columns, projection_weight, preferred_element_type=F32).astype(BF16)
    parts = exchange(lax.optimization_barrier(partial_value.reshape(groups, tok, width)), GROUP)
    offset = lax.axis_index(GROUP) * tok
    own_cotangent = lax.dynamic_slice_in_dim(upstream, offset, tok, 0)
    own_mask = lax.dynamic_slice_in_dim(loss_mask, offset, tok, 0)
    scaled = norm_gain * (own_cotangent.astype(F32) * own_mask.astype(F32)[:, None])

    cut = exchange(norm_backward(parts, scaled, slices), NEAR)
    cut, *own_columns = lax.optimization_barrier((cut, *(chunks[step] for step in range(QS))))
    own_columns = jnp.stack(own_columns)
    other_columns = lax.ppermute(own_columns, "core", PAIR)
    spread = lax.optimization_barrier(jnp.broadcast_to(cut[None], (groups, slices, tok, part)))
    arrived = exchange(spread, GROUP).reshape(groups, QS, CORES, tok, part)
    keep, give = product(own_columns, other_columns, arrived, place, own_rows)
    block = (keep + lax.ppermute(give, "p", PAIR).astype(F32)).astype(BF16)
    by_zh = exchange(block.reshape(ZHI, slices * own_rows, part), "zh")

    back = exchange(gather_rows(by_zh, own_rows, slices * PS, 16), ALONG)
    squares = exchange(spread_squares(back, own_rows, ZHI * groups), ("zh",) + GROUP)
    rows, grad_norm = clip(place, back, squares, own_rows, width, float(joined * width))
    return (rows.transpose(1, 0, 2), grad_norm.reshape(()))


def solution(mesh):
    sizes = (ZHI, QS, PS, CORES, mesh.shape["blk"], mesh.shape["tp"])
    fine = Mesh(mesh.devices.reshape(sizes), REP + GROUP)
    return jax.shard_map(
        body,
        mesh=fine,
        in_specs=(
            P(REP + GROUP, None),
            P(GROUP, None),
            P(),
            P(REP, None),
            P(REP),
        ),
        out_specs=(P(GROUP, REP, None), P()),
        check_vma=False,
    )
```

time: 169 us -> 169 us (level)
  blocking collectives: 125 us -> 85.5 us
  starting transfers between devices: 4.29 us -> 40.4 us
  between operations: 14.1 us -> 0.76 us
  waiting for transfers between devices: 9.61 us -> 22.1 us
  other arithmetic: 1.54 us -> 5.2 us
    all_to_all x6 -> x4, blocking collectives: 125 us -> 85.5 us  [exchange(): return lax.all_to_all(blocks, axes, split_axis=0, concat_axis=0, tiled=True)]
    ppermute x0 -> x5, starting transfers between devices: none -> 19.1 us  [the longest x3 14.2 us: body(): lax.ppermute(columns, 'q', [(i, (i + step) % QS) for i in range(QS)])]
    all_to_all x1 -> x3, starting transfers between devices: 4.25 us -> 21.4 us  [exchange(): return lax.all_to_all(blocks, axes, split_axis=0, concat_axis=0, tiled=True)]
    ppermute x0 -> x5, waiting for transfers between devices: none -> 6.35 us  [the longest x1 4.7 us: body(): block = (keep + lax.ppermute(give, 'p', PAIR).astype(F32)).astype(BF16)]
    all_to_all x1 -> x3, waiting for transfers between devices: 9.59 us -> 15.8 us  [exchange(): return lax.all_to_all(blocks, axes, split_axis=0, concat_axis=0, tiled=True)]
    another operation x0 -> x2, other arithmetic: none -> 2.61 us  [the longest x1 2.03 us: body(): own_columns = jnp.stack(own_columns)]
  transfers between devices with their start and end apart: 2 -> 8, of which waited for: 1 -> 4; matrix products, arithmetic and copies ran while one was open for 2% -> 2% of each run, Pallas kernels for 1% -> 1%
where the time goes in v5:
time: 169 us; the launch traced here: 168 us
  blocking collectives  85.5 us (51%)
  starting transfers between devices  40.4 us (24%)
  waiting for transfers between devices  22.1 us (13%)
  Pallas kernels  10.7 us (6%)
  other arithmetic  5.2 us (3%)
    all_to_all x4, blocking collectives, exchange(): return lax.all_to_all(blocks, axes, split_axis=0, concat_axis=0, tiled=True)  85.5 us
    all_to_all x3, starting transfers between devices, exchange(): return lax.all_to_all(blocks, axes, split_axis=0, concat_axis=0, tiled=True)  21.4 us
    all_to_all x3, waiting for transfers between devices, exchange(): return lax.all_to_all(blocks, axes, split_axis=0, concat_axis=0, tiled=True)  15.8 us
    ppermute x3, starting transfers between devices, body(): lax.ppermute(columns, 'q', [(i, (i + step) % QS) for i in range(QS)])  14.2 us
    ppermute x1, waiting for transfers between devices, body(): block = (keep + lax.ppermute(give, 'p', PAIR).astype(F32)).astype(BF16)  4.7 us
    pallas_call x1, Pallas kernels, product(): pl.pallas_call(product_kernel, in_specs=[pl.BlockSpec(memory_space=pltpu....  3.56 us
  transfers between devices with their start and end apart: 8, of which 4 were waited for; matrix products, arithmetic and copies ran while one was open for 2% of the time, Pallas kernels for 1%

profile of v5, /device:TPU:1, one launch (start us, length us, event | category | flops | bytes accessed | tf_op | source)
XLA Modules:
  0.0 167.7 jit_solution(13679485494442800552)
XLA Ops:
  0.6 0.0 copy-start
  0.6 0.0 copy-start.2
  0.7 0.0 copy-start.1
  0.7 18.2 %all_to_all.35 = bf16[16,8,768]{2,1,0:T(8,128)(2,1)S(1)} all-to-all(bf16[16,8,768]{2,1,0:T(8,128)(2,1)} %bitcast.26), channel_id=1, replica_groups=mesh['zh'=4,'q'=4,'p'=2,'core'=2,'blk'=4,'tp'=4] {'blk','tp'}, dimensions={0} | all-to-all | bytes 393216 | tf_op jit(solution)/shard_map/all_to_all | solution.py:20
  18.8 0.0 copy-done
  18.8 1.4 fusion
  20.2 4.2 %all-to-all-start.1 = ((bf16[16,8,2048]{2,1,0:T(8,128)(2,1)}), bf16[16,8,2048]{2,1,0:T(8,128)(2,1)}, u32[]{:S(2)}, u32[]{:S(2)}) async-start(bf16[16,8,2048]{2,1,0:T(8,128)(2,1)} %fusion), calls=%async_computation.1 | async-start | bytes 1048576 | tf_op jit(solution)/shard_map/all_to_all | solution.py:20
  24.5 0.0 copy-done.2
  24.5 0.1 dynamic-slice_convert_fusion
  24.6 6.5 %collective-permute-start.2 = (bf16[128,768]{1,0:T(8,128)(2,1)S(1)}, bf16[128,768]{1,0:T(8,128)(2,1)S(1)}, u32[]{:S(2)}, u32[]{:S(2)}) collective-permute-start(bf16[128,768]{1,0:T(8,128)(2,1)S(1)} %bitcast.20), channel_id=1, source_target_pairs={{0,192},{64,0},{128,64},{192,128},{1,193},{65,1},{129,65},{193,129... | collective-permute-start | bytes 589832 | tf_op jit(solution)/shard_map/ppermute | solution.py:161
  31.1 3.5 %collective-permute-start.1 = (bf16[128,768]{1,0:T(8,128)(2,1)S(1)}, bf16[128,768]{1,0:T(8,128)(2,1)}, u32[]{:S(2)}, u32[]{:S(2)}) collective-permute-start(bf16[128,768]{1,0:T(8,128)(2,1)S(1)} %bitcast.21), channel_id=1, source_target_pairs={{0,128},{64,192},{128,0},{192,64},{1,129},{65,193},{129,1},{193,65... | collective-permute-start | bytes 589832 | tf_op jit(solution)/shard_map/ppermute | solution.py:161
  34.6 4.2 %collective-permute-start = (bf16[128,768]{1,0:T(8,128)(2,1)S(1)}, bf16[128,768]{1,0:T(8,128)(2,1)}, u32[]{:S(2)}, u32[]{:S(2)}) collective-permute-start(bf16[128,768]{1,0:T(8,128)(2,1)S(1)} %bitcast.22), channel_id=1, source_target_pairs={{0,64},{64,128},{128,192},{192,0},{1,65},{65,129},{129,193},{193,1... | collective-permute-start | bytes 589832 | tf_op jit(solution)/shard_map/ppermute | solution.py:161
  38.8 0.0 copy-done.1
  38.8 1.5 multiply_multiply_fusion.scaled_ref
  40.3 0.0 all-to-all-done.1.parts_ref
  40.3 1.9 %norm_backward.1 = bf16[8,8,256]{2,1,0:T(8,128)(2,1)} custom-call(bf16[16,8,2048]{2,1,0:T(8,128)(2,1)} %all-to-all-done.1.parts_ref, f32[8,2048]{1,0:T(8,128)} %multiply_multiply_fusion.scaled_ref), custom_call_target="tpu_custom_call" | custom-call | tf_op jit(solution)/shard_map/norm_backward/pallas_call | solution.py:40
  42.2 10.0 %all-to-all-start.2 = ((bf16[8,8,256]{2,1,0:T(8,128)(2,1)}), bf16[8,8,256]{2,1,0:T(8,128)(2,1)}, u32[]{:S(2)}, u32[]{:S(2)}) async-start(bf16[8,8,256]{2,1,0:T(8,128)(2,1)} %norm_backward.1), calls=%async_computation.2 | async-start | bytes 65536 | tf_op jit(solution)/shard_map/all_to_all | solution.py:20
  52.2 0.0 collective-permute-done.2
  52.2 0.0 collective-permute-done.1
  52.2 0.0 collective-permute-done
  52.2 7.2 %all-to-all-done.2 = bf16[8,8,256]{2,1,0:T(8,128)(2,1)} async-done(((bf16[8,8,256]{2,1,0:T(8,128)(2,1)}), bf16[8,8,256]{2,1,0:T(8,128)(2,1)}, u32[]{:S(2)}, u32[]{:S(2)}) %all-to-all-start.2) | async-done | bytes 32800 | tf_op jit(solution)/shard_map/all_to_all | solution.py:20
  59.4 1.6 broadcast_in_dim.2
  61.0 7.2 %all-to-all-start.3 = ((bf16[16,8,8,256]{3,2,1,0:T(8,128)(2,1)}), bf16[16,8,8,256]{3,2,1,0:T(8,128)(2,1)}, u32[]{:S(2)}, u32[]{:S(2)}) async-start(bf16[16,8,8,256]{3,2,1,0:T(8,128)(2,1)} %broadcast_in_dim.2), calls=%async_computation.3 | async-start | bytes 1048576 | tf_op jit(solution)/shard_map/all_to_all | solution.py:20
  68.2 2.0 %pad_maximum_fusion.own_ref = bf16[4,128,768]{2,1,0:T(8,128)(2,1)} fusion(bf16[1,128,768]{2,1,0:T(8,128)(2,1)S(1)} %bitcast.25, bf16[1,128,768]{2,1,0:T(8,128)(2,1)} %bitcast.9, bf16[1,128,768]{2,1,0:T(8,128)(2,1)} %bitcast.8, bf16[1,128,768]{2,1,0:T(8,128)(2,1)S(1)} %bitcast.23), kind=kLoop, calls=%fused_computation.2 | loop fusion | flops 1179648 | bytes 1572864 | tf_op jit(solution)/shard_map/stack | solution.py:172
  70.2 2.9 %collective-permute-start.3 = (bf16[4,128,768]{2,1,0:T(8,128)(2,1)}, bf16[4,128,768]{2,1,0:T(8,128)(2,1)}, u32[]{:S(2)}, u32[]{:S(2)}) collective-permute-start(bf16[4,128,768]{2,1,0:T(8,128)(2,1)} %pad_maximum_fusion.own_ref), channel_id=1, source_target_pairs={{0,16},{16,0},{1,17},{17,1},{2,18},{18,2},{3,19},{19,3},{4,20},{20... | collective-permute-start | bytes 2359304 | tf_op jit(solution)/shard_map/ppermute | solution.py:173
  73.2 0.6 pad_add_fusion.place_ref
  73.7 1.6 collective-permute-done.3.other_ref
  75.4 8.6 %all-to-all-done.3 = bf16[16,8,8,256]{3,2,1,0:T(8,128)(2,1)} async-done(((bf16[16,8,8,256]{3,2,1,0:T(8,128)(2,1)}), bf16[16,8,8,256]{3,2,1,0:T(8,128)(2,1)}, u32[]{:S(2)}, u32[]{:S(2)}) %all-to-all-start.3) | async-done | bytes 524320 | tf_op jit(solution)/shard_map/all_to_all | solution.py:20
  84.0 3.6 %product.1 = (f32[384,256]{1,0:T(8,128)}, bf16[384,256]{1,0:T(8,128)(2,1)}) custom-call(s32[3]{0:T(128)} %pad_add_fusion.place_ref, bf16[4,128,768]{2,1,0:T(8,128)(2,1)} %pad_maximum_fusion.own_ref, bf16[4,128,768]{2,1,0:T(8,128)(2,1)} %collective-permute-done.3.other_ref, bf16[16,4,2,8,256]{4,3,2,1,0:T(8,128)(2,1)} %bitcast.11.grads_ref), custom_call_target="tpu_custom_call" | custom-call | tf_op jit(solution)/shard_map/product/pallas_call | solution.py:68
  87.5 1.9 %collective-permute-start.4 = (bf16[384,256]{1,0:T(8,128)(2,1)}, bf16[384,256]{1,0:T(8,128)(2,1)S(1)}, u32[]{:S(2)}, u32[]{:S(2)}) collective-permute-start(bf16[384,256]{1,0:T(8,128)(2,1)} %get-tuple-element.17), channel_id=1, source_target_pairs={{0,32},{32,0},{1,33},{33,1},{2,34},{34,2},{3,35},{35,3},{4,36},{36... | collective-permute-start | bytes 589832 | tf_op jit(solution)/shard_map/ppermute | solution.py:177
  89.4 4.7 %collective-permute-done.4 = bf16[384,256]{1,0:T(8,128)(2,1)S(1)} collective-permute-done((bf16[384,256]{1,0:T(8,128)(2,1)}, bf16[384,256]{1,0:T(8,128)(2,1)S(1)}, u32[]{:S(2)}, u32[]{:S(2)}) %collective-permute-start.4) | collective-permute-done | bytes 196640 | tf_op jit(solution)/shard_map/ppermute | solution.py:177
  94.1 1.0 add_convert_fusion
  95.2 28.8 %all_to_all.36.pieces_ref = bf16[4,96,256]{2,1,0:T(8,128)(2,1)} all-to-all(bf16[4,96,256]{2,1,0:T(8,128)(2,1)S(1)} %bitcast.24), channel_id=1, replica_groups=mesh['zh'=4,'q'=4,'p'=2,'core'=2,'blk'=4,'tp'=4] {'zh'}, dimensions={0} | all-to-all | bytes 393216 | tf_op jit(solution)/shard_map/all_to_all | solution.py:20
  124.0 1.8 %gather_rows.1 = f32[16,16,256]{2,1,0:T(8,128)} custom-call(bf16[4,96,256]{2,1,0:T(8,128)(2,1)} %all_to_all.36.pieces_ref), custom_call_target="tpu_custom_call" | custom-call | tf_op jit(solution)/shard_map/gather_rows/pallas_call | solution.py:94
  125.8 18.6 %all_to_all.37.back_ref = f32[16,16,256]{2,1,0:T(8,128)} all-to-all(f32[16,16,256]{2,1,0:T(8,128)} %gather_rows.1), channel_id=1, replica_groups=mesh['zh'=4,'q'=4,'p'=2,'core'=2,'blk'=4,'tp'=4] {'q','p','core'}, dimensions={0} | all-to-all | bytes 524288 | tf_op jit(solution)/shard_map/all_to_all | solution.py:20
  144.4 1.6 spread_squares.1
  146.0 19.9 %all_to_all.38.squares_ref = f32[64,1,128]{2,1,0:T(1,128)} all-to-all(f32[64,1,128]{2,1,0:T(1,128)} %spread_squares.1), channel_id=1, replica_groups=mesh['zh'=4,'q'=4,'p'=2,'core'=2,'blk'=4,'tp'=4] {'zh','blk','tp'}, dimensions={0} | all-to-all | bytes 65536 | tf_op jit(solution)/shard_map/all_to_all | solution.py:20
  165.9 1.8 %clip.1 = (f32[12,1,2048]{2,1,0:T(1,128)}, f32[1,1]{1,0:T(1,128)}) custom-call(s32[3]{0:T(128)} %pad_add_fusion.place_ref, f32[16,16,256]{2,1,0:T(8,128)} %all_to_all.37.back_ref, f32[64,1,128]{2,1,0:T(1,128)} %all_to_all.38.squares_ref), custom_call_target="tpu_custom_call" | custom-call | tf_op jit(solution)/shard_map/clip/pallas_call | solution.py:129
Async XLA Ops:
  0.6 18.2 %copy-start = (bf16[768,2048]{1,0:T(8,128)(2,1)S(1)}, bf16[768,2048]{1,0:T(8,128)(2,1)}, u32[]{:S(2)}) copy-start(bf16[768,2048]{1,0:T(8,128)(2,1)} %param.6) | copy-start | bytes 9437188
  0.6 23.8 %copy-start.2 = (s32[128]{0:T(128)S(1)}, s32[128]{0:T(128)}, u32[]{:S(2)}) copy-start(s32[128]{0:T(128)} %param.9) | copy-start | bytes 1540
  0.7 38.2 %copy-start.1 = (f32[2048]{0:T(1024)S(1)}, f32[2048]{0:T(1024)}, u32[]{:S(2)}) copy-start(f32[2048]{0:T(1024)} %param.7) | copy-start | bytes 24580
  20.2 20.1 %all-to-all-start.1 = ((bf16[16,8,2048]{2,1,0:T(8,128)(2,1)}), bf16[16,8,2048]{2,1,0:T(8,128)(2,1)}, u32[]{:S(2)}, u32[]{:S(2)}) async-start(bf16[16,8,2048]{2,1,0:T(8,128)(2,1)} %fusion), calls=%async_computation.1 | async-start | bytes 1048576 | tf_op jit(solution)/shard_map/all_to_all | solution.py:20
  24.6 27.6 %collective-permute-start.2 = (bf16[128,768]{1,0:T(8,128)(2,1)S(1)}, bf16[128,768]{1,0:T(8,128)(2,1)S(1)}, u32[]{:S(2)}, u32[]{:S(2)}) collective-permute-start(bf16[128,768]{1,0:T(8,128)(2,1)S(1)} %bitcast.20), channel_id=1, source_target_pairs={{0,192},{64,0},{128,64},{192,128},{1,193},{65,1},{129,65},{193,129... | collective-permute-start | bytes 589832 | tf_op jit(solution)/shard_map/ppermute | solution.py:161
  31.1 21.2 %collective-permute-start.1 = (bf16[128,768]{1,0:T(8,128)(2,1)S(1)}, bf16[128,768]{1,0:T(8,128)(2,1)}, u32[]{:S(2)}, u32[]{:S(2)}) collective-permute-start(bf16[128,768]{1,0:T(8,128)(2,1)S(1)} %bitcast.21), channel_id=1, source_target_pairs={{0,128},{64,192},{128,0},{192,64},{1,129},{65,193},{129,1},{193,65... | collective-permute-start | bytes 589832 | tf_op jit(solution)/shard_map/ppermute | solution.py:161
  34.6 17.6 %collective-permute-start = (bf16[128,768]{1,0:T(8,128)(2,1)S(1)}, bf16[128,768]{1,0:T(8,128)(2,1)}, u32[]{:S(2)}, u32[]{:S(2)}) collective-permute-start(bf16[128,768]{1,0:T(8,128)(2,1)S(1)} %bitcast.22), channel_id=1, source_target_pairs={{0,64},{64,128},{128,192},{192,0},{1,65},{65,129},{129,193},{193,1... | collective-permute-start | bytes 589832 | tf_op jit(solution)/shard_map/ppermute | solution.py:161
  42.2 17.2 %all-to-all-start.2 = ((bf16[8,8,256]{2,1,0:T(8,128)(2,1)}), bf16[8,8,256]{2,1,0:T(8,128)(2,1)}, u32[]{:S(2)}, u32[]{:S(2)}) async-start(bf16[8,8,256]{2,1,0:T(8,128)(2,1)} %norm_backward.1), calls=%async_computation.2 | async-start | bytes 65536 | tf_op jit(solution)/shard_map/all_to_all | solution.py:20
  61.0 22.9 %all-to-all-start.3 = ((bf16[16,8,8,256]{3,2,1,0:T(8,128)(2,1)}), bf16[16,8,8,256]{3,2,1,0:T(8,128)(2,1)}, u32[]{:S(2)}, u32[]{:S(2)}) async-start(bf16[16,8,8,256]{3,2,1,0:T(8,128)(2,1)} %broadcast_in_dim.2), calls=%async_computation.3 | async-start | bytes 1048576 | tf_op jit(solution)/shard_map/all_to_all | solution.py:20
  70.2 5.2 %collective-permute-start.3 = (bf16[4,128,768]{2,1,0:T(8,128)(2,1)}, bf16[4,128,768]{2,1,0:T(8,128)(2,1)}, u32[]{:S(2)}, u32[]{:S(2)}) collective-permute-start(bf16[4,128,768]{2,1,0:T(8,128)(2,1)} %pad_maximum_fusion.own_ref), channel_id=1, source_target_pairs={{0,16},{16,0},{1,17},{17,1},{2,18},{18,2},{3,19},{19,3},{4,20},{20... | collective-permute-start | bytes 2359304 | tf_op jit(solution)/shard_map/ppermute | solution.py:173
  87.5 6.6 %collective-permute-start.4 = (bf16[384,256]{1,0:T(8,128)(2,1)}, bf16[384,256]{1,0:T(8,128)(2,1)S(1)}, u32[]{:S(2)}, u32[]{:S(2)}) collective-permute-start(bf16[384,256]{1,0:T(8,128)(2,1)} %get-tuple-element.17), channel_id=1, source_target_pairs={{0,32},{32,0},{1,33},{33,1},{2,34},{34,2},{3,35},{35,3},{4,36},{36... | collective-permute-start | bytes 589832 | tf_op jit(solution)/shard_map/ppermute | solution.py:177

commit v6 on v3

--- a/solution.py
+++ b/solution.py
@@ -38,6 +38,7 @@
     return pl.pallas_call(
         norm_backward_kernel,
         out_shape=jax.ShapeDtypeStruct((slices, tok, width // slices), BF16),
+        compiler_params=pltpu.CompilerParams(vmem_limit_bytes=12 << 20),
         name="norm_backward",
     )(parts, scaled)
 
@@ -90,6 +91,7 @@
     return pl.pallas_call(
         functools.partial(gather_rows_kernel, own_rows),
         out_shape=jax.ShapeDtypeStruct((slices, padded, pieces.shape[2]), F32),
+        compiler_params=pltpu.CompilerParams(vmem_limit_bytes=12 << 20),
         name="gather_rows",
     )(pieces)
 
@@ -103,6 +105,7 @@
     return pl.pallas_call(
         functools.partial(squares_kernel, own_rows),
         out_shape=jax.ShapeDtypeStruct((size, 1, back.shape[2]), F32),
+        compiler_params=pltpu.CompilerParams(vmem_limit_bytes=12 << 20),
         name="spread_squares",
     )(back)
 
@@ -129,6 +132,7 @@
             pl.BlockSpec(memory_space=pltpu.VMEM),
             pl.BlockSpec(memory_space=pltpu.SMEM),
         ),
+        compiler_params=pltpu.CompilerParams(vmem_limit_bytes=12 << 20),
         name="clip",
     )(back, squares)
 
@@ -142,15 +146,17 @@
     own_rows = shard // (ZHI * slices)
 
     sent = lax.optimization_barrier(hidden.reshape(tok, groups, shard).transpose(1, 0, 2))
-    columns = exchange(sent, GROUP).reshape(groups * tok, shard)
+    offset = lax.axis_index(GROUP) * tok
+    own_cotangent = lax.dynamic_slice_in_dim(upstream, offset, tok, 0)
+    own_mask = lax.dynamic_slice_in_dim(loss_mask, offset, tok, 0)
+    scaled = norm_gain * (own_cotangent.astype(F32) * own_mask.astype(F32)[:, None])
+    columns = exchange(sent, GROUP)
+    columns, scaled = lax.optimization_barrier((columns, scaled))
+    columns = columns.reshape(groups * tok, shard)
     all_columns = lax.all_gather(columns, ALONG, axis=0, tiled=True)
 
     partial_value = jnp.dot(columns, projection_weight, preferred_element_type=F32).astype(BF16)
     parts = exchange(lax.optimization_barrier(partial_value.reshape(groups, tok, width)), GROUP)
-    offset = lax.axis_index(GROUP) * tok
-    own_cotangent = lax.dynamic_slice_in_dim(upstream, offset, tok, 0)
-    own_mask = lax.dynamic_slice_in_dim(loss_mask, offset, tok, 0)
-    scaled = norm_gain * (own_cotangent.astype(F32) * own_mask.astype(F32)[:, None])
 
     cut = exchange(norm_backward(parts, scaled, slices), ALONG)
     spread = lax.optimization_barrier(jnp.broadcast_to(cut[None], (groups, slices, tok, part)))

time: 169 us -> 160 us (0.947)
  starting transfers between devices: 4.29 us -> 10.7 us
  Pallas kernels: 11.1 us -> 5.42 us
  blocking collectives: 125 us -> 120 us
  waiting for transfers between devices: 9.61 us -> 5.91 us
    all_to_all x1, starting transfers between devices: 4.25 us -> 10.7 us  [exchange(): return lax.all_to_all(blocks, axes, split_axis=0, concat_axis=0, tiled=True)]
    all_to_all x6, blocking collectives: 125 us -> 120 us  [exchange(): return lax.all_to_all(blocks, axes, split_axis=0, concat_axis=0, tiled=True)]
    all_to_all x1, waiting for transfers between devices: 9.59 us -> 5.89 us  [exchange(): return lax.all_to_all(blocks, axes, split_axis=0, concat_axis=0, tiled=True)]
  transfers between devices with their start and end apart: 2 -> 2, of which waited for: 1 -> 1; matrix products, arithmetic and copies ran while one was open for 2% -> 2% of each run, Pallas kernels for 1% -> 0%
where the time goes in v6:
time: 160 us
  blocking collectives  120 us (75%)
  between operations  14.1 us (9%)
  starting transfers between devices  10.7 us (7%)
  waiting for transfers between devices  5.91 us (4%)
  Pallas kernels  5.42 us (3%)
    all_to_all x6, blocking collectives, exchange(): return lax.all_to_all(blocks, axes, split_axis=0, concat_axis=0, tiled=True)  120 us
    all_to_all x1, starting transfers between devices, exchange(): return lax.all_to_all(blocks, axes, split_axis=0, concat_axis=0, tiled=True)  10.7 us
    all_to_all x1, waiting for transfers between devices, exchange(): return lax.all_to_all(blocks, axes, split_axis=0, concat_axis=0, tiled=True)  5.89 us
    pallas_call x1, Pallas kernels, product(): pl.pallas_call(product_kernel, grid=(steps,), in_specs=[pl.BlockSpec((tok...  4.16 us
  transfers between devices with their start and end apart: 2, of which 1 were waited for; matrix products, arithmetic and copies ran while one was open for 2% of the time, Pallas kernels for 0%

profile of v6, /device:TPU:1, one launch (start us, length us, event | category | flops | bytes accessed | tf_op | source)
XLA Modules:
  0.0 159.8 jit_solution(9159160402857681215)
XLA Ops:
  7.2 0.0 copy-start
  7.2 10.7 %all-to-all-start = ((bf16[16,8,768]{2,1,0:T(8,128)(2,1)}), bf16[16,8,768]{2,1,0:T(8,128)(2,1)S(1)}, u32[]{:S(2)}, u32[]{:S(2)}) async-start(bf16[16,8,768]{2,1,0:T(8,128)(2,1)} %bitcast.14), calls=%async_computation | async-start | bytes 393216 | tf_op jit(solution)/shard_map/all_to_all | solution.py:19
  17.8 0.0 all-gather.2.cloned.1.call-start
  17.9 0.7 dynamic-slice_convert_fusion
  18.6 0.8 multiply_multiply_fusion.scaled_ref
  19.5 5.9 %all-to-all-done = bf16[16,8,768]{2,1,0:T(8,128)(2,1)S(1)} async-done(((bf16[16,8,768]{2,1,0:T(8,128)(2,1)}), bf16[16,8,768]{2,1,0:T(8,128)(2,1)S(1)}, u32[]{:S(2)}, u32[]{:S(2)}) %all-to-all-start) | async-done | bytes 196640 | tf_op jit(solution)/shard_map/all_to_all | solution.py:19
  25.4 0.0 copy-start.1
  25.4 0.7 copy-done.1
  26.0 0.0 all-gather.2.cloned.1.call-update
  26.0 0.0 copy-done
  26.1 1.5 fusion
  27.6 13.9 %all_to_all.35.parts_ref = bf16[16,8,2048]{2,1,0:T(8,128)(2,1)S(1)} all-to-all(bf16[16,8,2048]{2,1,0:T(8,128)(2,1)S(1)} %fusion), channel_id=1, replica_groups=mesh['zh'=4,'y'=8,'core'=2,'blk'=4,'tp'=4] {'blk','tp'}, dimensions={0} | all-to-all | bytes 1048576 | tf_op jit(solution)/shard_map/all_to_all | solution.py:19
  41.5 0.3 norm_backward.1
  41.8 22.5 %all_to_all.36 = bf16[16,8,128]{2,1,0:T(8,128)(2,1)S(1)} all-to-all(bf16[16,8,128]{2,1,0:T(8,128)(2,1)S(1)} %norm_backward.1), channel_id=1, replica_groups=mesh['zh'=4,'y'=8,'core'=2,'blk'=4,'tp'=4] {'y','core'}, dimensions={0} | all-to-all | bytes 65536 | tf_op jit(solution)/shard_map/all_to_all | solution.py:19
  64.2 0.1 broadcast_in_dim.2
  64.3 19.2 %all_to_all.37.grads_ref = bf16[16,16,8,128]{3,2,1,0:T(8,128)(2,1)} all-to-all(bf16[16,16,8,128]{3,2,1,0:T(8,128)(2,1)S(1)} %broadcast_in_dim.2), channel_id=1, replica_groups=mesh['zh'=4,'y'=8,'core'=2,'blk'=4,'tp'=4] {'blk','tp'}, dimensions={0} | all-to-all | bytes 1048576 | tf_op jit(solution)/shard_map/all_to_all | solution.py:19
  83.5 0.0 all-gather.2.cloned.1.call-done.columns_ref
  83.5 4.2 %product.1 = bf16[768,128]{1,0:T(8,128)(2,1)} custom-call(bf16[2048,768]{1,0:T(8,128)(2,1)} %all-gather.2.cloned.1.call-done.columns_ref, bf16[16,16,8,128]{3,2,1,0:T(8,128)(2,1)} %all_to_all.37.grads_ref), custom_call_target="tpu_custom_call" | custom-call | tf_op jit(solution)/shard_map/product/pallas_call | solution.py:65
  87.7 29.6 %all_to_all.38.pieces_ref = bf16[4,192,128]{2,1,0:T(8,128)(2,1)S(1)} all-to-all(bf16[4,192,128]{2,1,0:T(8,128)(2,1)} %bitcast.13), channel_id=1, replica_groups=mesh['zh'=4,'y'=8,'core'=2,'blk'=4,'tp'=4] {'zh'}, dimensions={0} | all-to-all | bytes 393216 | tf_op jit(solution)/shard_map/all_to_all | solution.py:19
  117.3 0.2 gather_rows.1
  117.5 15.6 %all_to_all.39.back_ref = f32[16,16,128]{2,1,0:T(8,128)S(1)} all-to-all(f32[16,16,128]{2,1,0:T(8,128)S(1)} %gather_rows.1), channel_id=1, replica_groups=mesh['zh'=4,'y'=8,'core'=2,'blk'=4,'tp'=4] {'y','core'}, dimensions={0} | all-to-all | bytes 262144 | tf_op jit(solution)/shard_map/all_to_all | solution.py:19
  133.1 19.1 %all_to_all.40.squares_ref = f32[64,1,128]{2,1,0:T(1,128)S(1)} all-to-all(f32[64,1,128]{2,1,0:T(1,128)S(1)} %spread_squares.1), channel_id=1, replica_groups=mesh['zh'=4,'y'=8,'core'=2,'blk'=4,'tp'=4] {'zh','blk','tp'}, dimensions={0} | all-to-all | bytes 65536 | tf_op jit(solution)/shard_map/all_to_all | solution.py:19
  152.2 0.8 clip.1
  (1 shorter events, 0.0 us)
Async XLA Ops:
  7.2 18.9 %copy-start = (bf16[768,2048]{1,0:T(8,128)(2,1)S(1)}, bf16[768,2048]{1,0:T(8,128)(2,1)}, u32[]{:S(2)}) copy-start(bf16[768,2048]{1,0:T(8,128)(2,1)} %param.6) | copy-start | bytes 9437188
  7.2 18.2 %all-to-all-start = ((bf16[16,8,768]{2,1,0:T(8,128)(2,1)}), bf16[16,8,768]{2,1,0:T(8,128)(2,1)S(1)}, u32[]{:S(2)}, u32[]{:S(2)}) async-start(bf16[16,8,768]{2,1,0:T(8,128)(2,1)} %bitcast.14), calls=%async_computation | async-start | bytes 393216 | tf_op jit(solution)/shard_map/all_to_all | solution.py:19
  17.8 65.7 %all-gather.2.cloned.1.call-start = ((), (), s32[]{:S(2)}) async-start(), calls=%async_computation.7 | async-start | bytes 3342336 | tf_op jit(solution)/shard_map/all_gather | solution.py:156
  25.4 0.7 copy-start.1
Sparse Core Ops, SparseCore 0:
  26.2 54.4 all-gather.1

commit v7 on v6

--- a/solution.py
+++ b/solution.py
@@ -12,11 +12,16 @@
 ALONG = ("y", "core")
 GROUP = ("blk", "tp")
 LANES = 128
+HELD = (-1, 0, 1, -4, -3, -2, 2, 3)
 BF16, F32 = jnp.bfloat16, jnp.float32
 
 
 def exchange(blocks, axes):
     return lax.all_to_all(blocks, axes, split_axis=0, concat_axis=0, tiled=True)
+
+
+def move(value, step):
+    return lax.ppermute(value, "y", [(i, (i + step) % YS) for i in range(YS)])
 
 
 def norm_backward_kernel(parts_ref, scaled_ref, out_ref):
@@ -43,37 +48,44 @@
     )(parts, scaled)
 
 
-def product_kernel(columns_ref, grads_ref, out_ref, total_ref):
-    step = pl.program_id(0)
-
-    @pl.when(step == 0)
+def product_kernel(own_ref, other_ref, grads_ref, out_ref, total_ref):
+    half = pl.program_id(0)
+    y, core = lax.axis_index("y"), lax.axis_index("core")
+    groups, _, _, tok, part = grads_ref.shape
+    count = own_ref.shape[0]
+    term = None
+    for columns_ref, place in ((own_ref, core), (other_ref, 1 - core)):
+        grads = []
+        for k in range(count):
+            source = lax.rem(y + jnp.where(half == 0, HELD[k], HELD[count + k]) + YS, YS)
+            grads.append(grads_ref[:, source, place].astype(F32).reshape(groups * tok, part).T)
+        grads = jnp.concatenate(grads, axis=1).astype(BF16)
+        columns = columns_ref[...].reshape(-1, columns_ref.shape[2])
+        dot = jnp.dot(grads, columns, preferred_element_type=F32)
+        term = dot if term is None else term + dot
+
+    @pl.when(half == 0)
     def _():
-        total_ref[...] = jnp.zeros_like(total_ref)
-
-    groups, chunk, tok, part = grads_ref.shape
-    grads = grads_ref[...].astype(F32).transpose(1, 0, 2, 3).reshape(chunk * groups * tok, part)
-    total_ref[...] += jnp.dot(grads.T.astype(BF16), columns_ref[...], preferred_element_type=F32)
-
-    @pl.when(step == pl.num_programs(0) - 1)
+        total_ref[...] = term
+
+    @pl.when(half == 1)
     def _():
-        out_ref[...] = total_ref[...].T.astype(BF16)
-
-
-def product(all_columns, arrived, steps):
-    groups, slices, tok, part = arrived.shape
-    tokens, shard = all_columns.shape
+        out_ref[...] = (total_ref[...] + term).T.astype(BF16)
+
+
+def product(own, other, arrived):
+    part = arrived.shape[-1]
+    _, tokens, shard = own.shape
+    held = pl.BlockSpec((YS // 2, tokens, shard), lambda i: (i, 0, 0))
     return pl.pallas_call(
         product_kernel,
-        grid=(steps,),
-        in_specs=[
-            pl.BlockSpec((tokens // steps, shard), lambda i: (i, 0)),
-            pl.BlockSpec((groups, slices // steps, tok, part), lambda i: (0, i, 0, 0)),
-        ],
+        grid=(2,),
+        in_specs=[held, held, pl.BlockSpec(arrived.shape, lambda i: (0, 0, 0, 0, 0))],
         out_specs=pl.BlockSpec((shard, part), lambda i: (0, 0)),
         out_shape=jax.ShapeDtypeStruct((shard, part), BF16),
         scratch_shapes=[pltpu.VMEM((part, shard), F32)],
         name="product",
-    )(all_columns, arrived)
+    )(own, other, arrived)
 
 
 def gather_rows_kernel(own_rows, pieces_ref, out_ref):
@@ -153,7 +165,10 @@
     columns = exchange(sent, GROUP)
     columns, scaled = lax.optimization_barrier((columns, scaled))
     columns = columns.reshape(groups * tok, shard)
-    all_columns = lax.all_gather(columns, ALONG, axis=0, tiled=True)
+    up, down = move(columns, 1), move(columns, -1)
+    three = jnp.stack([up, columns, down])
+    own = jnp.concatenate([three, move(three, 3), move(three[:2], -3)])
+    other = lax.ppermute(own, "core", [(0, 1), (1, 0)])
 
     partial_value = jnp.dot(columns, projection_weight, preferred_element_type=F32).astype(BF16)
     parts = exchange(lax.optimization_barrier(partial_value.reshape(groups, tok, width)), GROUP)
@@ -161,7 +176,7 @@
     cut = exchange(norm_backward(parts, scaled, slices), ALONG)
     spread = lax.optimization_barrier(jnp.broadcast_to(cut[None], (groups, slices, tok, part)))
     arrived = exchange(spread, GROUP)
-    block = product(all_columns, arrived, 4)
+    block = product(own, other, arrived.reshape(groups, YS, CORES, tok, part))
     by_zh = exchange(block.reshape(ZHI, shard // ZHI, part), "zh")
 
     back = exchange(gather_rows(by_zh, own_rows, slices, 16), ALONG)

time: 160 us -> 183 us (1.14)
  blocking collectives: 120 us -> 69.2 us
  starting transfers between devices: 10.7 us -> 54.1 us
  waiting for transfers between devices: 5.91 us -> 38.6 us
  between operations: 14.1 us -> 0.74 us
  local copies, waits for them, and re-layouts: 0.77 us -> 8.19 us
    all_to_all x6 -> x3, blocking collectives: 120 us -> 69.2 us  [exchange(): return lax.all_to_all(blocks, axes, split_axis=0, concat_axis=0, tiled=True)]
    all_to_all x1 -> x4, waiting for transfers between devices: 5.89 us -> 32.6 us  [exchange(): return lax.all_to_all(blocks, axes, split_axis=0, concat_axis=0, tiled=True)]
    all_to_all x1 -> x4, starting transfers between devices: 10.7 us -> 34 us  [exchange(): return lax.all_to_all(blocks, axes, split_axis=0, concat_axis=0, tiled=True)]
    ppermute x0 -> x5, starting transfers between devices: none -> 20 us  [the longest x4 17.6 us: move(): return lax.ppermute(value, 'y', [(i, (i + step) % YS) for i in range(YS)])]
    ppermute x0 -> x5, waiting for transfers between devices: none -> 5.95 us  [the longest x1 3.36 us: body(): other = lax.ppermute(own, 'core', [(0, 1), (1, 0)])]
    unnamed x4 -> x10, local copies, waits for them, and re-layouts: 0.68 us -> 4.73 us
  transfers between devices with their start and end apart: 2 -> 9, of which waited for: 1 -> 6; matrix products, arithmetic and copies ran while one was open for 2% -> 6% of each run, Pallas kernels for 0% -> 1%
where the time goes in v7:
time: 183 us; the launch traced here: 182 us
  blocking collectives  69.2 us (38%)
  starting transfers between devices  54.1 us (30%)
  waiting for transfers between devices  38.6 us (21%)
  local copies, waits for them, and re-layouts  8.19 us (4%)
  Pallas kernels  6.19 us (3%)
  other arithmetic  3.24 us (2%)
    all_to_all x3, blocking collectives, exchange(): return lax.all_to_all(blocks, axes, split_axis=0, concat_axis=0, tiled=True)  69.2 us
    all_to_all x4, starting transfers between devices, exchange(): return lax.all_to_all(blocks, axes, split_axis=0, concat_axis=0, tiled=True)  34 us
    all_to_all x4, waiting for transfers between devices, exchange(): return lax.all_to_all(blocks, axes, split_axis=0, concat_axis=0, tiled=True)  32.6 us
    ppermute x4, starting transfers between devices, move(): return lax.ppermute(value, 'y', [(i, (i + step) % YS) for i in range(YS)])  17.6 us
    unnamed x10, local copies, waits for them, and re-layouts  4.73 us
  transfers between devices with their start and end apart: 9, of which 6 were waited for; matrix products, arithmetic and copies ran while one was open for 6% of the time, Pallas kernels for 1%

profile of v7, /device:TPU:1, one launch (start us, length us, event | category | flops | bytes accessed | tf_op | source)
XLA Modules:
  0.0 181.6 jit_solution(7853520342312863794)
XLA Ops:
  0.6 0.0 copy-start
  0.6 10.7 %all-to-all-start = ((bf16[16,8,768]{2,1,0:T(8,128)(2,1)}), bf16[16,8,768]{2,1,0:T(8,128)(2,1)S(1)}, u32[]{:S(2)}, u32[]{:S(2)}) async-start(bf16[16,8,768]{2,1,0:T(8,128)(2,1)} %bitcast.27), calls=%async_computation | async-start | bytes 393216 | tf_op jit(solution)/shard_map/all_to_all | solution.py:20
  11.3 0.7 dynamic-slice_convert_fusion
  12.0 0.8 multiply_multiply_fusion.scaled_ref
  12.9 5.9 %all-to-all-done = bf16[16,8,768]{2,1,0:T(8,128)(2,1)S(1)} async-done(((bf16[16,8,768]{2,1,0:T(8,128)(2,1)}), bf16[16,8,768]{2,1,0:T(8,128)(2,1)S(1)}, u32[]{:S(2)}, u32[]{:S(2)}) %all-to-all-start) | async-done | bytes 196640 | tf_op jit(solution)/shard_map/all_to_all | solution.py:20
  18.8 0.0 copy-done
  18.8 1.4 fusion
  20.2 4.3 %all-to-all-start.1 = ((bf16[16,8,2048]{2,1,0:T(8,128)(2,1)}), bf16[16,8,2048]{2,1,0:T(8,128)(2,1)}, u32[]{:S(2)}, u32[]{:S(2)}) async-start(bf16[16,8,2048]{2,1,0:T(8,128)(2,1)} %fusion), calls=%async_computation.1 | async-start | bytes 1048576 | tf_op jit(solution)/shard_map/all_to_all | solution.py:20
  24.5 3.8 %collective-permute-start = (bf16[128,768]{1,0:T(8,128)(2,1)S(1)}, bf16[128,768]{1,0:T(8,128)(2,1)S(1)}, u32[]{:S(2)}, u32[]{:S(2)}) collective-permute-start(bf16[128,768]{1,0:T(8,128)(2,1)S(1)} %bitcast.19), channel_id=1, source_target_pairs={{0,32},{32,64},{64,96},{96,128},{128,160},{160,192},{192,224},{224... | collective-permute-start | bytes 589832 | tf_op jit(solution)/shard_map/ppermute | solution.py:24
  28.3 3.8 %collective-permute-start.1 = (bf16[128,768]{1,0:T(8,128)(2,1)S(1)}, bf16[128,768]{1,0:T(8,128)(2,1)S(1)}, u32[]{:S(2)}, u32[]{:S(2)}) collective-permute-start(bf16[128,768]{1,0:T(8,128)(2,1)S(1)} %bitcast.20), channel_id=1, source_target_pairs={{0,224},{32,0},{64,32},{96,64},{128,96},{160,128},{192,160},{224,1... | collective-permute-start | bytes 589832 | tf_op jit(solution)/shard_map/ppermute | solution.py:24
  32.1 1.1 collective-permute-done
  33.2 1.5 collective-permute-done.1
  34.7 0.0 copy-start.1
  34.7 0.7 copy-done.1
  35.4 0.9 pad_maximum_fusion
  36.3 8.0 %collective-permute-start.2 = (bf16[3,128,768]{2,1,0:T(8,128)(2,1)}, bf16[3,128,768]{2,1,0:T(8,128)(2,1)}, u32[]{:S(2)}, u32[]{:S(2)}) collective-permute-start(bf16[3,128,768]{2,1,0:T(8,128)(2,1)} %pad_maximum_fusion), channel_id=1, source_target_pairs={{0,96},{32,128},{64,160},{96,192},{128,224},{160,0},{192,32},{224,... | collective-permute-start | bytes 1769480 | tf_op jit(solution)/shard_map/ppermute | solution.py:24
  44.3 0.8 pad_maximum_fusion.1
  45.1 1.9 %collective-permute-start.3 = (bf16[2,128,768]{2,1,0:T(8,128)(2,1)}, bf16[2,128,768]{2,1,0:T(8,128)(2,1)}, u32[]{:S(2)}, u32[]{:S(2)}) collective-permute-start(bf16[2,128,768]{2,1,0:T(8,128)(2,1)} %pad_maximum_fusion.1), channel_id=1, source_target_pairs={{0,160},{32,192},{64,224},{96,0},{128,32},{160,64},{192,96},{224,1... | collective-permute-start | bytes 1179656 | tf_op jit(solution)/shard_map/ppermute | solution.py:24
  47.1 0.7 constant_dynamic-update-slice_fusion.4
  47.7 0.0 all-to-all-done.1.parts_ref
  47.8 1.9 %norm_backward.1 = bf16[16,8,128]{2,1,0:T(8,128)(2,1)} custom-call(bf16[16,8,2048]{2,1,0:T(8,128)(2,1)} %all-to-all-done.1.parts_ref, f32[8,2048]{1,0:T(8,128)S(1)} %multiply_multiply_fusion.scaled_ref), custom_call_target="tpu_custom_call" | custom-call | tf_op jit(solution)/shard_map/norm_backward/pallas_call | solution.py:43
  49.7 0.0 copy-start.2
  49.7 11.3 %all-to-all-start.2 = ((bf16[16,8,128]{2,1,0:T(8,128)(2,1)}), bf16[16,8,128]{2,1,0:T(8,128)(2,1)}, u32[]{:S(2)}, u32[]{:S(2)}) async-start(bf16[16,8,128]{2,1,0:T(8,128)(2,1)} %norm_backward.1), calls=%async_computation.2 | async-start | bytes 65536 | tf_op jit(solution)/shard_map/all_to_all | solution.py:20
  61.0 0.7 constant_dynamic-update-slice_fusion.3
  61.7 21.1 %all-to-all-done.2 = bf16[16,8,128]{2,1,0:T(8,128)(2,1)} async-done(((bf16[16,8,128]{2,1,0:T(8,128)(2,1)}), bf16[16,8,128]{2,1,0:T(8,128)(2,1)}, u32[]{:S(2)}, u32[]{:S(2)}) %all-to-all-start.2) | async-done | bytes 32800 | tf_op jit(solution)/shard_map/all_to_all | solution.py:20
  82.8 1.7 broadcast_in_dim.2
  84.5 7.8 %all-to-all-start.3 = ((bf16[16,16,8,128]{3,2,1,0:T(8,128)(2,1)}), bf16[16,16,8,128]{3,2,1,0:T(8,128)(2,1)}, u32[]{:S(2)}, u32[]{:S(2)}) async-start(bf16[16,16,8,128]{3,2,1,0:T(8,128)(2,1)} %broadcast_in_dim.2), calls=%async_computation.3 | async-start | bytes 1048576 | tf_op jit(solution)/shard_map/all_to_all | solution.py:20
  92.3 0.0 copy-done.2
  92.3 0.7 constant_dynamic-update-slice_fusion.2
  93.0 0.0 collective-permute-done.2
  93.0 1.9 %constant_dynamic-update-slice_fusion.1 = bf16[8,128,768]{2,1,0:T(8,128)(2,1)} fusion(bf16[8,128,768]{2,1,0:T(8,128)(2,1)} %constant_dynamic-update-slice_fusion.2, bf16[3,128,768]{2,1,0:T(8,128)(2,1)} %collective-permute-done.2), kind=kLoop, calls=%fused_computation.6 | loop fusion | bytes 1179648
  95.0 0.0 collective-permute-done.3
  95.0 1.8 constant_dynamic-update-slice_fusion.own_ref
  96.7 2.5 %collective-permute-start.4 = (bf16[8,128,768]{2,1,0:T(8,128)(2,1)}, bf16[8,128,768]{2,1,0:T(8,128)(2,1)}, u32[]{:S(2)}, u32[]{:S(2)}) collective-permute-start(bf16[8,128,768]{2,1,0:T(8,128)(2,1)} %constant_dynamic-update-slice_fusion.own_ref), channel_id=1, source_target_pairs={{0,16},{16,0},{1,17},{17,1},{2,18},{18,2},{3,19},{19,3},{4,20},{20... | collective-permute-start | bytes 4718600 | tf_op jit(solution)/shard_map/ppermute | solution.py:171
  99.2 3.4 %collective-permute-done.4.other_ref = bf16[8,128,768]{2,1,0:T(8,128)(2,1)} collective-permute-done((bf16[8,128,768]{2,1,0:T(8,128)(2,1)}, bf16[8,128,768]{2,1,0:T(8,128)(2,1)}, u32[]{:S(2)}, u32[]{:S(2)}) %collective-permute-start.4) | collective-permute-done | bytes 1572896 | tf_op jit(solution)/shard_map/ppermute | solution.py:171
  102.6 5.6 %all-to-all-done.3 = bf16[16,16,8,128]{3,2,1,0:T(8,128)(2,1)} async-done(((bf16[16,16,8,128]{3,2,1,0:T(8,128)(2,1)}), bf16[16,16,8,128]{3,2,1,0:T(8,128)(2,1)}, u32[]{:S(2)}, u32[]{:S(2)}) %all-to-all-start.3) | async-done | bytes 524320 | tf_op jit(solution)/shard_map/all_to_all | solution.py:20
  108.1 3.3 %product.1 = bf16[768,128]{1,0:T(8,128)(2,1)} custom-call(bf16[8,128,768]{2,1,0:T(8,128)(2,1)} %constant_dynamic-update-slice_fusion.own_ref, bf16[8,128,768]{2,1,0:T(8,128)(2,1)} %collective-permute-done.4.other_ref, bf16[16,8,2,8,128]{4,3,2,1,0:T(8,128)(2,1)} %bitcast.7.grads_ref), custom_call_target="tpu_custom_call" | custom-call | tf_op jit(solution)/shard_map/product/pallas_call | solution.py:80
  111.4 29.3 %all_to_all.35.pieces_ref = bf16[4,192,128]{2,1,0:T(8,128)(2,1)S(1)} all-to-all(bf16[4,192,128]{2,1,0:T(8,128)(2,1)} %bitcast.26), channel_id=1, replica_groups=mesh['zh'=4,'y'=8,'core'=2,'blk'=4,'tp'=4] {'zh'}, dimensions={0} | all-to-all | bytes 393216 | tf_op jit(solution)/shard_map/all_to_all | solution.py:20
  140.7 0.2 gather_rows.1
  140.9 20.8 %all_to_all.36.back_ref = f32[16,16,128]{2,1,0:T(8,128)S(1)} all-to-all(f32[16,16,128]{2,1,0:T(8,128)S(1)} %gather_rows.1), channel_id=1, replica_groups=mesh['zh'=4,'y'=8,'core'=2,'blk'=4,'tp'=4] {'y','core'}, dimensions={0} | all-to-all | bytes 262144 | tf_op jit(solution)/shard_map/all_to_all | solution.py:20
  161.7 19.1 %all_to_all.37.squares_ref = f32[64,1,128]{2,1,0:T(1,128)S(1)} all-to-all(f32[64,1,128]{2,1,0:T(1,128)S(1)} %spread_squares.1), channel_id=1, replica_groups=mesh['zh'=4,'y'=8,'core'=2,'blk'=4,'tp'=4] {'zh','blk','tp'}, dimensions={0} | all-to-all | bytes 65536 | tf_op jit(solution)/shard_map/all_to_all | solution.py:20
  180.8 0.8 clip.1
  (1 shorter events, 0.0 us)
Async XLA Ops:
  0.6 18.2 %copy-start = (bf16[768,2048]{1,0:T(8,128)(2,1)S(1)}, bf16[768,2048]{1,0:T(8,128)(2,1)}, u32[]{:S(2)}) copy-start(bf16[768,2048]{1,0:T(8,128)(2,1)} %param.6) | copy-start | bytes 9437188
  0.6 18.2 %all-to-all-start = ((bf16[16,8,768]{2,1,0:T(8,128)(2,1)}), bf16[16,8,768]{2,1,0:T(8,128)(2,1)S(1)}, u32[]{:S(2)}, u32[]{:S(2)}) async-start(bf16[16,8,768]{2,1,0:T(8,128)(2,1)} %bitcast.27), calls=%async_computation | async-start | bytes 393216 | tf_op jit(solution)/shard_map/all_to_all | solution.py:20
  20.2 27.5 %all-to-all-start.1 = ((bf16[16,8,2048]{2,1,0:T(8,128)(2,1)}), bf16[16,8,2048]{2,1,0:T(8,128)(2,1)}, u32[]{:S(2)}, u32[]{:S(2)}) async-start(bf16[16,8,2048]{2,1,0:T(8,128)(2,1)} %fusion), calls=%async_computation.1 | async-start | bytes 1048576 | tf_op jit(solution)/shard_map/all_to_all | solution.py:20
  24.5 8.7 %collective-permute-start = (bf16[128,768]{1,0:T(8,128)(2,1)S(1)}, bf16[128,768]{1,0:T(8,128)(2,1)S(1)}, u32[]{:S(2)}, u32[]{:S(2)}) collective-permute-start(bf16[128,768]{1,0:T(8,128)(2,1)S(1)} %bitcast.19), channel_id=1, source_target_pairs={{0,32},{32,64},{64,96},{96,128},{128,160},{160,192},{192,224},{224... | collective-permute-start | bytes 589832 | tf_op jit(solution)/shard_map/ppermute | solution.py:24
  28.3 6.4 %collective-permute-start.1 = (bf16[128,768]{1,0:T(8,128)(2,1)S(1)}, bf16[128,768]{1,0:T(8,128)(2,1)S(1)}, u32[]{:S(2)}, u32[]{:S(2)}) collective-permute-start(bf16[128,768]{1,0:T(8,128)(2,1)S(1)} %bitcast.20), channel_id=1, source_target_pairs={{0,224},{32,0},{64,32},{96,64},{128,96},{160,128},{192,160},{224,1... | collective-permute-start | bytes 589832 | tf_op jit(solution)/shard_map/ppermute | solution.py:24
  34.7 0.7 copy-start.1
  36.3 56.7 %collective-permute-start.2 = (bf16[3,128,768]{2,1,0:T(8,128)(2,1)}, bf16[3,128,768]{2,1,0:T(8,128)(2,1)}, u32[]{:S(2)}, u32[]{:S(2)}) collective-permute-start(bf16[3,128,768]{2,1,0:T(8,128)(2,1)} %pad_maximum_fusion), channel_id=1, source_target_pairs={{0,96},{32,128},{64,160},{96,192},{128,224},{160,0},{192,32},{224,... | collective-permute-start | bytes 1769480 | tf_op jit(solution)/shard_map/ppermute | solution.py:24
  45.1 49.8 %collective-permute-start.3 = (bf16[2,128,768]{2,1,0:T(8,128)(2,1)}, bf16[2,128,768]{2,1,0:T(8,128)(2,1)}, u32[]{:S(2)}, u32[]{:S(2)}) collective-permute-start(bf16[2,128,768]{2,1,0:T(8,128)(2,1)} %pad_maximum_fusion.1), channel_id=1, source_target_pairs={{0,160},{32,192},{64,224},{96,0},{128,32},{160,64},{192,96},{224,1... | collective-permute-start | bytes 1179656 | tf_op jit(solution)/shard_map/ppermute | solution.py:24
  49.7 42.7 %copy-start.2 = (bf16[128,768]{1,0:T(8,128)(2,1)S(1)}, bf16[128,768]{1,0:T(8,128)(2,1)}, u32[]{:S(2)}) copy-start(bf16[128,768]{1,0:T(8,128)(2,1)} %copy-done.1) | copy-start | bytes 589828
  49.7 33.1 %all-to-all-start.2 = ((bf16[16,8,128]{2,1,0:T(8,128)(2,1)}), bf16[16,8,128]{2,1,0:T(8,128)(2,1)}, u32[]{:S(2)}, u32[]{:S(2)}) async-start(bf16[16,8,128]{2,1,0:T(8,128)(2,1)} %norm_backward.1), calls=%async_computation.2 | async-start | bytes 65536 | tf_op jit(solution)/shard_map/all_to_all | solution.py:20
  84.5 23.7 %all-to-all-start.3 = ((bf16[16,16,8,128]{3,2,1,0:T(8,128)(2,1)}), bf16[16,16,8,128]{3,2,1,0:T(8,128)(2,1)}, u32[]{:S(2)}, u32[]{:S(2)}) async-start(bf16[16,16,8,128]{3,2,1,0:T(8,128)(2,1)} %broadcast_in_dim.2), calls=%async_computation.3 | async-start | bytes 1048576 | tf_op jit(solution)/shard_map/all_to_all | solution.py:20
  96.7 5.8 %collective-permute-start.4 = (bf16[8,128,768]{2,1,0:T(8,128)(2,1)}, bf16[8,128,768]{2,1,0:T(8,128)(2,1)}, u32[]{:S(2)}, u32[]{:S(2)}) collective-permute-start(bf16[8,128,768]{2,1,0:T(8,128)(2,1)} %constant_dynamic-update-slice_fusion.own_ref), channel_id=1, source_target_pairs={{0,16},{16,0},{1,17},{17,1},{2,18},{18,2},{3,19},{19,3},{4,20},{20... | collective-permute-start | bytes 4718600 | tf_op jit(solution)/shard_map/ppermute | solution.py:171

commit v8 on v6

--- a/solution.py
+++ b/solution.py
@@ -161,7 +161,7 @@
     cut = exchange(norm_backward(parts, scaled, slices), ALONG)
     spread = lax.optimization_barrier(jnp.broadcast_to(cut[None], (groups, slices, tok, part)))
     arrived = exchange(spread, GROUP)
-    block = product(all_columns, arrived, 4)
+    block = product(all_columns, arrived, 2)
     by_zh = exchange(block.reshape(ZHI, shard // ZHI, part), "zh")
 
     back = exchange(gather_rows(by_zh, own_rows, slices, 16), ALONG)

time: 160 us -> 159 us (level)
  no operation moved by 1% of the time
where the time goes in v8:
time: 159 us
  blocking collectives  120 us (75%)
  between operations  14.1 us (9%)
  starting transfers between devices  10.7 us (7%)
  waiting for transfers between devices  5.91 us (4%)
  Pallas kernels  4.46 us (3%)
    all_to_all x6, blocking collectives, exchange(): return lax.all_to_all(blocks, axes, split_axis=0, concat_axis=0, tiled=True)  120 us
    all_to_all x1, starting transfers between devices, exchange(): return lax.all_to_all(blocks, axes, split_axis=0, concat_axis=0, tiled=True)  10.7 us
    all_to_all x1, waiting for transfers between devices, exchange(): return lax.all_to_all(blocks, axes, split_axis=0, concat_axis=0, tiled=True)  5.89 us
    pallas_call x1, Pallas kernels, product(): pl.pallas_call(product_kernel, grid=(steps,), in_specs=[pl.BlockSpec((tok...  3.2 us
  transfers between devices with their start and end apart: 2, of which 1 were waited for; matrix products, arithmetic and copies ran while one was open for 2% of the time, Pallas kernels for 0%

profile of v8, /device:TPU:1, one launch (start us, length us, event | category | flops | bytes accessed | tf_op | source)
XLA Modules:
  0.0 158.9 jit_solution(4666296342662263678)
XLA Ops:
  7.2 0.0 copy-start
  7.2 10.7 %all-to-all-start = ((bf16[16,8,768]{2,1,0:T(8,128)(2,1)}), bf16[16,8,768]{2,1,0:T(8,128)(2,1)S(1)}, u32[]{:S(2)}, u32[]{:S(2)}) async-start(bf16[16,8,768]{2,1,0:T(8,128)(2,1)} %bitcast.14), calls=%async_computation | async-start | bytes 393216 | tf_op jit(solution)/shard_map/all_to_all | solution.py:19
  17.8 0.0 all-gather.2.cloned.1.call-start
  17.9 0.7 dynamic-slice_convert_fusion
  18.6 0.8 multiply_multiply_fusion.scaled_ref
  19.5 5.9 %all-to-all-done = bf16[16,8,768]{2,1,0:T(8,128)(2,1)S(1)} async-done(((bf16[16,8,768]{2,1,0:T(8,128)(2,1)}), bf16[16,8,768]{2,1,0:T(8,128)(2,1)S(1)}, u32[]{:S(2)}, u32[]{:S(2)}) %all-to-all-start) | async-done | bytes 196640 | tf_op jit(solution)/shard_map/all_to_all | solution.py:19
  25.4 0.0 copy-start.1
  25.4 0.7 copy-done.1
  26.0 0.0 all-gather.2.cloned.1.call-update
  26.0 0.0 copy-done
  26.1 1.5 fusion
  27.6 13.9 %all_to_all.35.parts_ref = bf16[16,8,2048]{2,1,0:T(8,128)(2,1)S(1)} all-to-all(bf16[16,8,2048]{2,1,0:T(8,128)(2,1)S(1)} %fusion), channel_id=1, replica_groups=mesh['zh'=4,'y'=8,'core'=2,'blk'=4,'tp'=4] {'blk','tp'}, dimensions={0} | all-to-all | bytes 1048576 | tf_op jit(solution)/shard_map/all_to_all | solution.py:19
  41.5 0.3 norm_backward.1
  41.8 22.5 %all_to_all.36 = bf16[16,8,128]{2,1,0:T(8,128)(2,1)S(1)} all-to-all(bf16[16,8,128]{2,1,0:T(8,128)(2,1)S(1)} %norm_backward.1), channel_id=1, replica_groups=mesh['zh'=4,'y'=8,'core'=2,'blk'=4,'tp'=4] {'y','core'}, dimensions={0} | all-to-all | bytes 65536 | tf_op jit(solution)/shard_map/all_to_all | solution.py:19
  64.2 0.1 broadcast_in_dim.2
  64.3 19.2 %all_to_all.37.grads_ref = bf16[16,16,8,128]{3,2,1,0:T(8,128)(2,1)} all-to-all(bf16[16,16,8,128]{3,2,1,0:T(8,128)(2,1)S(1)} %broadcast_in_dim.2), channel_id=1, replica_groups=mesh['zh'=4,'y'=8,'core'=2,'blk'=4,'tp'=4] {'blk','tp'}, dimensions={0} | all-to-all | bytes 1048576 | tf_op jit(solution)/shard_map/all_to_all | solution.py:19
  83.5 0.0 all-gather.2.cloned.1.call-done.columns_ref
  83.5 3.2 %product.1 = bf16[768,128]{1,0:T(8,128)(2,1)} custom-call(bf16[2048,768]{1,0:T(8,128)(2,1)} %all-gather.2.cloned.1.call-done.columns_ref, bf16[16,16,8,128]{3,2,1,0:T(8,128)(2,1)} %all_to_all.37.grads_ref), custom_call_target="tpu_custom_call" | custom-call | tf_op jit(solution)/shard_map/product/pallas_call | solution.py:65
  86.7 29.6 %all_to_all.38.pieces_ref = bf16[4,192,128]{2,1,0:T(8,128)(2,1)S(1)} all-to-all(bf16[4,192,128]{2,1,0:T(8,128)(2,1)} %bitcast.13), channel_id=1, replica_groups=mesh['zh'=4,'y'=8,'core'=2,'blk'=4,'tp'=4] {'zh'}, dimensions={0} | all-to-all | bytes 393216 | tf_op jit(solution)/shard_map/all_to_all | solution.py:19
  116.3 0.2 gather_rows.1
  116.5 15.6 %all_to_all.39.back_ref = f32[16,16,128]{2,1,0:T(8,128)S(1)} all-to-all(f32[16,16,128]{2,1,0:T(8,128)S(1)} %gather_rows.1), channel_id=1, replica_groups=mesh['zh'=4,'y'=8,'core'=2,'blk'=4,'tp'=4] {'y','core'}, dimensions={0} | all-to-all | bytes 262144 | tf_op jit(solution)/shard_map/all_to_all | solution.py:19
  132.1 19.1 %all_to_all.40.squares_ref = f32[64,1,128]{2,1,0:T(1,128)S(1)} all-to-all(f32[64,1,128]{2,1,0:T(1,128)S(1)} %spread_squares.1), channel_id=1, replica_groups=mesh['zh'=4,'y'=8,'core'=2,'blk'=4,'tp'=4] {'zh','blk','tp'}, dimensions={0} | all-to-all | bytes 65536 | tf_op jit(solution)/shard_map/all_to_all | solution.py:19
  151.2 0.8 clip.1
  (1 shorter events, 0.0 us)
Async XLA Ops:
  7.2 18.9 %copy-start = (bf16[768,2048]{1,0:T(8,128)(2,1)S(1)}, bf16[768,2048]{1,0:T(8,128)(2,1)}, u32[]{:S(2)}) copy-start(bf16[768,2048]{1,0:T(8,128)(2,1)} %param.6) | copy-start | bytes 9437188
  7.2 18.2 %all-to-all-start = ((bf16[16,8,768]{2,1,0:T(8,128)(2,1)}), bf16[16,8,768]{2,1,0:T(8,128)(2,1)S(1)}, u32[]{:S(2)}, u32[]{:S(2)}) async-start(bf16[16,8,768]{2,1,0:T(8,128)(2,1)} %bitcast.14), calls=%async_computation | async-start | bytes 393216 | tf_op jit(solution)/shard_map/all_to_all | solution.py:19
  17.8 65.7 %all-gather.2.cloned.1.call-start = ((), (), s32[]{:S(2)}) async-start(), calls=%async_computation.7 | async-start | bytes 3342336 | tf_op jit(solution)/shard_map/all_gather | solution.py:156
  25.4 0.7 copy-start.1
Sparse Core Ops, SparseCore 0:
  26.2 54.4 all-gather.1

commit v9 on v8

--- a/solution.py
+++ b/solution.py
@@ -7,10 +7,11 @@
 from jax.experimental.pallas import tpu as pltpu
 from jax.sharding import Mesh, PartitionSpec as P
 
-ZHI, YS, CORES = 4, 8, 2
+ZHI, YS, CORES, HALVES = 4, 8, 2, 2
 REP = ("zh", "y", "core")
 ALONG = ("y", "core")
-GROUP = ("blk", "tp")
+GROUP = ("blk", "ta", "tb")
+PAIR = [(0, 1), (1, 0)]
 LANES = 128
 BF16, F32 = jnp.bfloat16, jnp.float32
 
@@ -110,9 +111,21 @@
     )(back)
 
 
-def clip_kernel(limit_square, back_ref, squares_ref, out_ref, norm_ref):
-    squares = jnp.sum(squares_ref[...], axis=0)
-    norm = jnp.sqrt(squares)
+def add_squares_kernel(squares_ref, out_ref):
+    out_ref[...] = jnp.sum(squares_ref[...], axis=0)
+
+
+def add_squares(squares):
+    return pl.pallas_call(
+        add_squares_kernel,
+        out_shape=jax.ShapeDtypeStruct(squares.shape[1:], F32),
+        compiler_params=pltpu.CompilerParams(vmem_limit_bytes=12 << 20),
+        name="add_squares",
+    )(squares)
+
+
+def clip_kernel(limit_square, back_ref, squares_ref, other_ref, out_ref, norm_ref):
+    norm = jnp.sqrt(squares_ref[...] + other_ref[...])
     factor = jnp.minimum(1.0, jnp.sqrt(jnp.full_like(norm, limit_square)) / (norm + 1e-06))
     norm_ref[0, 0] = jnp.max(norm)
     slices, _, part = back_ref.shape
@@ -121,7 +134,7 @@
             out_ref[r, :, j * part : (j + 1) * part] = back_ref[j, r : r + 1, :] * factor
 
 
-def clip(back, squares, own_rows, width, limit_square):
+def clip(back, squares, other, own_rows, width, limit_square):
     return pl.pallas_call(
         functools.partial(clip_kernel, limit_square),
         out_shape=(
@@ -134,7 +147,7 @@
         ),
         compiler_params=pltpu.CompilerParams(vmem_limit_bytes=12 << 20),
         name="clip",
-    )(back, squares)
+    )(back, squares, other)
 
 
 def body(hidden, projection_weight, norm_gain, upstream, loss_mask):
@@ -153,9 +166,9 @@
     columns = exchange(sent, GROUP)
     columns, scaled = lax.optimization_barrier((columns, scaled))
     columns = columns.reshape(groups * tok, shard)
+    partial_value = jnp.dot(columns, projection_weight, preferred_element_type=F32).astype(BF16)
+    columns, partial_value = lax.optimization_barrier((columns, partial_value))
     all_columns = lax.all_gather(columns, ALONG, axis=0, tiled=True)
-
-    partial_value = jnp.dot(columns, projection_weight, preferred_element_type=F32).astype(BF16)
     parts = exchange(lax.optimization_barrier(partial_value.reshape(groups, tok, width)), GROUP)
 
     cut = exchange(norm_backward(parts, scaled, slices), ALONG)
@@ -165,13 +178,15 @@
     by_zh = exchange(block.reshape(ZHI, shard // ZHI, part), "zh")
 
     back = exchange(gather_rows(by_zh, own_rows, slices, 16), ALONG)
-    squares = exchange(spread_squares(back, own_rows, ZHI * groups), ("zh",) + GROUP)
-    rows, grad_norm = clip(back, squares, own_rows, width, float(joined * width))
+    squares = spread_squares(back, own_rows, ZHI * groups // HALVES)
+    squares = add_squares(exchange(squares, ("zh", "blk", "ta")))
+    other = lax.ppermute(squares, "tb", PAIR)
+    rows, grad_norm = clip(back, squares, other, own_rows, width, float(joined * width))
     return (rows.transpose(1, 0, 2), grad_norm.reshape(()))
 
 
 def solution(mesh):
-    sizes = (ZHI, YS, CORES, mesh.shape["blk"], mesh.shape["tp"])
+    sizes = (ZHI, YS, CORES, mesh.shape["blk"], mesh.shape["tp"] // HALVES, HALVES)
     fine = Mesh(mesh.devices.reshape(sizes), REP + GROUP)
     return jax.shard_map(
         body,

time: 159 us -> 162 us (1.019)
  waiting for transfers between devices: 5.91 us -> 8.26 us
  starting transfers between devices: 10.7 us -> 12.6 us
    ppermute x0 -> x1, waiting for transfers between devices: none -> 2.36 us  [body(): other = lax.ppermute(squares, 'tb', PAIR)]
    ppermute x0 -> x1, starting transfers between devices: none -> 1.91 us  [body(): other = lax.ppermute(squares, 'tb', PAIR)]
  transfers between devices with their start and end apart: 2 -> 3, of which waited for: 1 -> 2; matrix products, arithmetic and copies ran while one was open for 2% -> 1% of each run, Pallas kernels for 0% -> 0%
where the time goes in v9:
time: 162 us
  blocking collectives  119 us (73%)
  between operations  14.1 us (9%)
  starting transfers between devices  12.6 us (8%)
  waiting for transfers between devices  8.26 us (5%)
  Pallas kernels  4.42 us (3%)
    all_to_all x6, blocking collectives, exchange(): return lax.all_to_all(blocks, axes, split_axis=0, concat_axis=0, tiled=True)  119 us
    all_to_all x1, starting transfers between devices, exchange(): return lax.all_to_all(blocks, axes, split_axis=0, concat_axis=0, tiled=True)  10.7 us
    all_to_all x1, waiting for transfers between devices, exchange(): return lax.all_to_all(blocks, axes, split_axis=0, concat_axis=0, tiled=True)  5.89 us
  transfers between devices with their start and end apart: 3, of which 2 were waited for; matrix products, arithmetic and copies ran while one was open for 1% of the time, Pallas kernels for 0%

profile of v9, /device:TPU:1, one launch (start us, length us, event | category | flops | bytes accessed | tf_op | source)
XLA Modules:
  0.0 161.7 jit_solution(17600314517934647741)
XLA Ops:
  7.2 0.0 copy-start
  7.2 10.7 %all-to-all-start = ((bf16[16,8,768]{2,1,0:T(8,128)(2,1)}), bf16[16,8,768]{2,1,0:T(8,128)(2,1)S(1)}, u32[]{:S(2)}, u32[]{:S(2)}) async-start(bf16[16,8,768]{2,1,0:T(8,128)(2,1)} %bitcast.14), calls=%async_computation | async-start | bytes 393216 | tf_op jit(solution)/shard_map/all_to_all | solution.py:20
  17.8 0.0 all-gather.2.cloned.1.call-start
  17.9 0.7 dynamic-slice_convert_fusion
  18.6 0.8 multiply_multiply_fusion.scaled_ref
  19.5 5.9 %all-to-all-done = bf16[16,8,768]{2,1,0:T(8,128)(2,1)S(1)} async-done(((bf16[16,8,768]{2,1,0:T(8,128)(2,1)}), bf16[16,8,768]{2,1,0:T(8,128)(2,1)S(1)}, u32[]{:S(2)}, u32[]{:S(2)}) %all-to-all-start) | async-done | bytes 196640 | tf_op jit(solution)/shard_map/all_to_all | solution.py:20
  25.4 0.0 copy-done
  25.4 0.0 copy-start.1
  25.4 1.4 convolution_convert_fusion
  26.7 0.0 copy-done.1
  26.7 0.0 all-gather.2.cloned.1.call-update
  26.8 14.7 %all_to_all.35.parts_ref = bf16[16,8,2048]{2,1,0:T(8,128)(2,1)S(1)} all-to-all(bf16[16,8,2048]{2,1,0:T(8,128)(2,1)} %bitcast.11), channel_id=1, replica_groups=mesh['zh'=4,'y'=8,'core'=2,'blk'=4,'ta'=2,'tb'=2] {'blk','ta','tb'}, dimensions={0} | all-to-all | bytes 1048576 | tf_op jit(solution)/shard_map/all_to_all | solution.py:20
  41.5 0.3 norm_backward.1
  41.7 22.1 %all_to_all.36 = bf16[16,8,128]{2,1,0:T(8,128)(2,1)S(1)} all-to-all(bf16[16,8,128]{2,1,0:T(8,128)(2,1)S(1)} %norm_backward.1), channel_id=1, replica_groups=mesh['zh'=4,'y'=8,'core'=2,'blk'=4,'ta'=2,'tb'=2] {'y','core'}, dimensions={0} | all-to-all | bytes 65536 | tf_op jit(solution)/shard_map/all_to_all | solution.py:20
  63.8 0.1 broadcast_in_dim.2
  63.9 19.2 %all_to_all.37.grads_ref = bf16[16,16,8,128]{3,2,1,0:T(8,128)(2,1)} all-to-all(bf16[16,16,8,128]{3,2,1,0:T(8,128)(2,1)S(1)} %broadcast_in_dim.2), channel_id=1, replica_groups=mesh['zh'=4,'y'=8,'core'=2,'blk'=4,'ta'=2,'tb'=2] {'blk','ta','tb'}, dimensions={0} | all-to-all | bytes 1048576 | tf_op jit(solution)/shard_map/all_to_all | solution.py:20
  83.1 0.0 all-gather.2.cloned.1.call-done.columns_ref
  83.1 3.2 %product.1 = bf16[768,128]{1,0:T(8,128)(2,1)} custom-call(bf16[2048,768]{1,0:T(8,128)(2,1)} %all-gather.2.cloned.1.call-done.columns_ref, bf16[16,16,8,128]{3,2,1,0:T(8,128)(2,1)} %all_to_all.37.grads_ref), custom_call_target="tpu_custom_call" | custom-call | tf_op jit(solution)/shard_map/product/pallas_call | solution.py:66
  86.3 29.4 %all_to_all.38.pieces_ref = bf16[4,192,128]{2,1,0:T(8,128)(2,1)S(1)} all-to-all(bf16[4,192,128]{2,1,0:T(8,128)(2,1)} %bitcast.13), channel_id=1, replica_groups=mesh['zh'=4,'y'=8,'core'=2,'blk'=4,'ta'=2,'tb'=2] {'zh'}, dimensions={0} | all-to-all | bytes 393216 | tf_op jit(solution)/shard_map/all_to_all | solution.py:20
  115.8 0.2 gather_rows.1
  115.9 15.3 %all_to_all.39.back_ref = f32[16,16,128]{2,1,0:T(8,128)S(1)} all-to-all(f32[16,16,128]{2,1,0:T(8,128)S(1)} %gather_rows.1), channel_id=1, replica_groups=mesh['zh'=4,'y'=8,'core'=2,'blk'=4,'ta'=2,'tb'=2] {'y','core'}, dimensions={0} | all-to-all | bytes 262144 | tf_op jit(solution)/shard_map/all_to_all | solution.py:20
  131.3 18.5 %all_to_all.40.squares_ref = f32[32,1,128]{2,1,0:T(1,128)S(1)} all-to-all(f32[32,1,128]{2,1,0:T(1,128)S(1)} %spread_squares.1), channel_id=1, replica_groups=mesh['zh'=4,'y'=8,'core'=2,'blk'=4,'ta'=2,'tb'=2] {'zh','blk','ta'}, dimensions={0} | all-to-all | bytes 32768 | tf_op jit(solution)/shard_map/all_to_all | solution.py:20
  149.8 1.9 %collective-permute-start = (f32[1,128]{1,0:T(1,128)S(1)}, f32[1,128]{1,0:T(1,128)S(1)}, u32[]{:S(2)}, u32[]{:S(2)}) collective-permute-start(f32[1,128]{1,0:T(1,128)S(1)} %add_squares.1.squares_ref), channel_id=1, source_target_pairs={{0,1},{1,0},{2,3},{3,2},{4,5},{5,4},{6,7},{7,6},{8,9},{9,8},{10,11... | collective-permute-start | bytes 1544 | tf_op jit(solution)/shard_map/ppermute | solution.py:183
  151.8 2.4 %collective-permute-done.other_ref = f32[1,128]{1,0:T(1,128)S(1)} collective-permute-done((f32[1,128]{1,0:T(1,128)S(1)}, f32[1,128]{1,0:T(1,128)S(1)}, u32[]{:S(2)}, u32[]{:S(2)}) %collective-permute-start) | collective-permute-done | bytes 544 | tf_op jit(solution)/shard_map/ppermute | solution.py:183
  154.1 0.7 clip.1
  (2 shorter events, 0.1 us)
Async XLA Ops:
  7.2 18.2 %copy-start = (bf16[768,2048]{1,0:T(8,128)(2,1)S(1)}, bf16[768,2048]{1,0:T(8,128)(2,1)}, u32[]{:S(2)}) copy-start(bf16[768,2048]{1,0:T(8,128)(2,1)} %param.6) | copy-start | bytes 9437188
  7.2 18.2 %all-to-all-start = ((bf16[16,8,768]{2,1,0:T(8,128)(2,1)}), bf16[16,8,768]{2,1,0:T(8,128)(2,1)S(1)}, u32[]{:S(2)}, u32[]{:S(2)}) async-start(bf16[16,8,768]{2,1,0:T(8,128)(2,1)} %bitcast.14), calls=%async_computation | async-start | bytes 393216 | tf_op jit(solution)/shard_map/all_to_all | solution.py:20
  17.8 65.3 %all-gather.2.cloned.1.call-start = ((), (), s32[]{:S(2)}) async-start(), calls=%async_computation.7 | async-start | bytes 3342336 | tf_op jit(solution)/shard_map/all_gather | solution.py:171
  25.4 1.4 copy-start.1
  149.8 4.3 %collective-permute-start = (f32[1,128]{1,0:T(1,128)S(1)}, f32[1,128]{1,0:T(1,128)S(1)}, u32[]{:S(2)}, u32[]{:S(2)}) collective-permute-start(f32[1,128]{1,0:T(1,128)S(1)} %add_squares.1.squares_ref), channel_id=1, source_target_pairs={{0,1},{1,0},{2,3},{3,2},{4,5},{5,4},{6,7},{7,6},{8,9},{9,8},{10,11... | collective-permute-start | bytes 1544 | tf_op jit(solution)/shard_map/ppermute | solution.py:183
Sparse Core Ops, SparseCore 0:
  26.9 53.9 all-gather.1

commit v10 on v8

--- a/solution.py
+++ b/solution.py
@@ -72,6 +72,7 @@
         out_specs=pl.BlockSpec((shard, part), lambda i: (0, 0)),
         out_shape=jax.ShapeDtypeStruct((shard, part), BF16),
         scratch_shapes=[pltpu.VMEM((part, shard), F32)],
+        compiler_params=pltpu.CompilerParams(vmem_limit_bytes=53 << 20),
         name="product",
     )(all_columns, arrived)
 
@@ -153,9 +154,9 @@
     columns = exchange(sent, GROUP)
     columns, scaled = lax.optimization_barrier((columns, scaled))
     columns = columns.reshape(groups * tok, shard)
+    partial_value = jnp.dot(columns, projection_weight, preferred_element_type=F32).astype(BF16)
+    columns, partial_value = lax.optimization_barrier((columns, partial_value))
     all_columns = lax.all_gather(columns, ALONG, axis=0, tiled=True)
-
-    partial_value = jnp.dot(columns, projection_weight, preferred_element_type=F32).astype(BF16)
     parts = exchange(lax.optimization_barrier(partial_value.reshape(groups, tok, width)), GROUP)
 
     cut = exchange(norm_backward(parts, scaled, slices), ALONG)

time: 159 us -> 159 us (level)
  transfers between devices with their start and end apart: 2 -> 2, of which waited for: 1 -> 1; matrix products, arithmetic and copies ran while one was open for 2% -> 1% of each run, Pallas kernels for 0% -> 0%
where the time goes in v10:
time: 159 us; the launch traced here: 158 us
  blocking collectives  119 us (75%)
  between operations  14.1 us (9%)
  starting transfers between devices  10.7 us (7%)
  waiting for transfers between devices  5.91 us (4%)
  Pallas kernels  3.71 us (2%)
    all_to_all x6, blocking collectives, exchange(): return lax.all_to_all(blocks, axes, split_axis=0, concat_axis=0, tiled=True)  119 us
    all_to_all x1, starting transfers between devices, exchange(): return lax.all_to_all(blocks, axes, split_axis=0, concat_axis=0, tiled=True)  10.7 us
    all_to_all x1, waiting for transfers between devices, exchange(): return lax.all_to_all(blocks, axes, split_axis=0, concat_axis=0, tiled=True)  5.89 us
  transfers between devices with their start and end apart: 2, of which 1 were waited for; matrix products, arithmetic and copies ran while one was open for 1% of the time, Pallas kernels for 0%

profile of v10, /device:TPU:1, one launch (start us, length us, event | category | flops | bytes accessed | tf_op | source)
XLA Modules:
  0.0 158.0 jit_solution(16761123630062728332)
XLA Ops:
  7.2 0.0 copy-start
  7.2 10.7 %all-to-all-start = ((bf16[16,8,768]{2,1,0:T(8,128)(2,1)}), bf16[16,8,768]{2,1,0:T(8,128)(2,1)S(1)}, u32[]{:S(2)}, u32[]{:S(2)}) async-start(bf16[16,8,768]{2,1,0:T(8,128)(2,1)} %bitcast.14), calls=%async_computation | async-start | bytes 393216 | tf_op jit(solution)/shard_map/all_to_all | solution.py:19
  17.8 0.0 all-gather.2.cloned.1.call-start
  17.9 0.7 dynamic-slice_convert_fusion
  18.6 0.8 multiply_multiply_fusion.scaled_ref
  19.5 5.9 %all-to-all-done = bf16[16,8,768]{2,1,0:T(8,128)(2,1)S(1)} async-done(((bf16[16,8,768]{2,1,0:T(8,128)(2,1)}), bf16[16,8,768]{2,1,0:T(8,128)(2,1)S(1)}, u32[]{:S(2)}, u32[]{:S(2)}) %all-to-all-start) | async-done | bytes 196640 | tf_op jit(solution)/shard_map/all_to_all | solution.py:19
  25.4 0.0 copy-done
  25.4 0.0 copy-start.2
  25.4 1.4 convolution_convert_fusion
  26.7 0.0 copy-done.2
  26.7 0.0 all-gather.2.cloned.1.call-update
  26.8 14.7 %all_to_all.35.parts_ref = bf16[16,8,2048]{2,1,0:T(8,128)(2,1)S(1)} all-to-all(bf16[16,8,2048]{2,1,0:T(8,128)(2,1)} %bitcast.12), channel_id=1, replica_groups=mesh['zh'=4,'y'=8,'core'=2,'blk'=4,'tp'=4] {'blk','tp'}, dimensions={0} | all-to-all | bytes 1048576 | tf_op jit(solution)/shard_map/all_to_all | solution.py:19
  41.5 0.3 norm_backward.1
  41.7 22.1 %all_to_all.36 = bf16[16,8,128]{2,1,0:T(8,128)(2,1)S(1)} all-to-all(bf16[16,8,128]{2,1,0:T(8,128)(2,1)S(1)} %norm_backward.1), channel_id=1, replica_groups=mesh['zh'=4,'y'=8,'core'=2,'blk'=4,'tp'=4] {'y','core'}, dimensions={0} | all-to-all | bytes 65536 | tf_op jit(solution)/shard_map/all_to_all | solution.py:19
  63.8 0.1 broadcast_in_dim.2
  63.9 19.2 %all_to_all.37.grads_ref = bf16[16,16,8,128]{3,2,1,0:T(8,128)(2,1)} all-to-all(bf16[16,16,8,128]{3,2,1,0:T(8,128)(2,1)S(1)} %broadcast_in_dim.2), channel_id=1, replica_groups=mesh['zh'=4,'y'=8,'core'=2,'blk'=4,'tp'=4] {'blk','tp'}, dimensions={0} | all-to-all | bytes 1048576 | tf_op jit(solution)/shard_map/all_to_all | solution.py:19
  83.1 0.0 all-gather.2.cloned.1.call-done.columns_ref
  83.1 0.0 copy-start.1
  83.1 1.0 copy-done.1
  84.2 2.5 %product.1 = bf16[768,128]{1,0:T(8,128)(2,1)S(1)} custom-call(bf16[2048,768]{1,0:T(8,128)(2,1)} %all-gather.2.cloned.1.call-done.columns_ref, bf16[16,16,8,128]{3,2,1,0:T(8,128)(2,1)S(1)} %copy-done.1), custom_call_target="tpu_custom_call" | custom-call | tf_op jit(solution)/shard_map/product/pallas_call | solution.py:65
  86.6 29.3 %all_to_all.38.pieces_ref = bf16[4,192,128]{2,1,0:T(8,128)(2,1)S(1)} all-to-all(bf16[4,192,128]{2,1,0:T(8,128)(2,1)S(1)} %bitcast.11), channel_id=1, replica_groups=mesh['zh'=4,'y'=8,'core'=2,'blk'=4,'tp'=4] {'zh'}, dimensions={0} | all-to-all | bytes 393216 | tf_op jit(solution)/shard_map/all_to_all | solution.py:19
  115.9 0.2 gather_rows.1
  116.1 15.3 %all_to_all.39.back_ref = f32[16,16,128]{2,1,0:T(8,128)S(1)} all-to-all(f32[16,16,128]{2,1,0:T(8,128)S(1)} %gather_rows.1), channel_id=1, replica_groups=mesh['zh'=4,'y'=8,'core'=2,'blk'=4,'tp'=4] {'y','core'}, dimensions={0} | all-to-all | bytes 262144 | tf_op jit(solution)/shard_map/all_to_all | solution.py:19
  131.4 18.9 %all_to_all.40.squares_ref = f32[64,1,128]{2,1,0:T(1,128)S(1)} all-to-all(f32[64,1,128]{2,1,0:T(1,128)S(1)} %spread_squares.1), channel_id=1, replica_groups=mesh['zh'=4,'y'=8,'core'=2,'blk'=4,'tp'=4] {'zh','blk','tp'}, dimensions={0} | all-to-all | bytes 65536 | tf_op jit(solution)/shard_map/all_to_all | solution.py:19
  150.3 0.8 clip.1
  (1 shorter events, 0.0 us)
Async XLA Ops:
  7.2 18.2 %copy-start = (bf16[768,2048]{1,0:T(8,128)(2,1)S(1)}, bf16[768,2048]{1,0:T(8,128)(2,1)}, u32[]{:S(2)}) copy-start(bf16[768,2048]{1,0:T(8,128)(2,1)} %param.6) | copy-start | bytes 9437188
  7.2 18.2 %all-to-all-start = ((bf16[16,8,768]{2,1,0:T(8,128)(2,1)}), bf16[16,8,768]{2,1,0:T(8,128)(2,1)S(1)}, u32[]{:S(2)}, u32[]{:S(2)}) async-start(bf16[16,8,768]{2,1,0:T(8,128)(2,1)} %bitcast.14), calls=%async_computation | async-start | bytes 393216 | tf_op jit(solution)/shard_map/all_to_all | solution.py:19
  17.8 65.3 %all-gather.2.cloned.1.call-start = ((), (), s32[]{:S(2)}) async-start(), calls=%async_computation.7 | async-start | bytes 3342336 | tf_op jit(solution)/shard_map/all_gather | solution.py:159
  25.4 1.4 copy-start.2
  83.1 1.0 copy-start.1
Sparse Core Ops, SparseCore 0:
  26.9 53.9 all-gather.1

commit v11 on v10

--- a/solution.py
+++ b/solution.py
@@ -72,7 +72,7 @@
         out_specs=pl.BlockSpec((shard, part), lambda i: (0, 0)),
         out_shape=jax.ShapeDtypeStruct((shard, part), BF16),
         scratch_shapes=[pltpu.VMEM((part, shard), F32)],
-        compiler_params=pltpu.CompilerParams(vmem_limit_bytes=53 << 20),
+        compiler_params=pltpu.CompilerParams(vmem_limit_bytes=55040 << 10),
         name="product",
     )(all_columns, arrived)
 

time: 159 us -> 158 us (level)
  no operation moved by 1% of the time
where the time goes in v11:
time: 158 us; the launch traced here: 157 us
  blocking collectives  119 us (75%)
  between operations  14.1 us (9%)
  starting transfers between devices  10.7 us (7%)
  waiting for transfers between devices  5.91 us (4%)
  Pallas kernels  3.8 us (2%)
    all_to_all x6, blocking collectives, exchange(): return lax.all_to_all(blocks, axes, split_axis=0, concat_axis=0, tiled=True)  119 us
    all_to_all x1, starting transfers between devices, exchange(): return lax.all_to_all(blocks, axes, split_axis=0, concat_axis=0, tiled=True)  10.7 us
    all_to_all x1, waiting for transfers between devices, exchange(): return lax.all_to_all(blocks, axes, split_axis=0, concat_axis=0, tiled=True)  5.89 us
  transfers between devices with their start and end apart: 2, of which 1 were waited for; matrix products, arithmetic and copies ran while one was open for 1% of the time, Pallas kernels for 0%

profile of v11, /device:TPU:1, one launch (start us, length us, event | category | flops | bytes accessed | tf_op | source)
XLA Modules:
  0.0 157.0 jit_solution(2368111981146883951)
XLA Ops:
  7.2 0.0 copy-start
  7.2 10.7 %all-to-all-start = ((bf16[16,8,768]{2,1,0:T(8,128)(2,1)}), bf16[16,8,768]{2,1,0:T(8,128)(2,1)S(1)}, u32[]{:S(2)}, u32[]{:S(2)}) async-start(bf16[16,8,768]{2,1,0:T(8,128)(2,1)} %bitcast.14), calls=%async_computation | async-start | bytes 393216 | tf_op jit(solution)/shard_map/all_to_all | solution.py:19
  17.8 0.0 all-gather.2.cloned.1.call-start
  17.9 0.7 dynamic-slice_convert_fusion
  18.6 0.8 multiply_multiply_fusion.scaled_ref
  19.5 5.9 %all-to-all-done = bf16[16,8,768]{2,1,0:T(8,128)(2,1)S(1)} async-done(((bf16[16,8,768]{2,1,0:T(8,128)(2,1)}), bf16[16,8,768]{2,1,0:T(8,128)(2,1)S(1)}, u32[]{:S(2)}, u32[]{:S(2)}) %all-to-all-start) | async-done | bytes 196640 | tf_op jit(solution)/shard_map/all_to_all | solution.py:19
  25.4 0.0 copy-done
  25.4 0.0 copy-start.1
  25.4 1.4 convolution_convert_fusion
  26.7 0.0 copy-done.1
  26.7 0.0 all-gather.2.cloned.1.call-update
  26.8 14.7 %all_to_all.35.parts_ref = bf16[16,8,2048]{2,1,0:T(8,128)(2,1)S(1)} all-to-all(bf16[16,8,2048]{2,1,0:T(8,128)(2,1)} %bitcast.12), channel_id=1, replica_groups=mesh['zh'=4,'y'=8,'core'=2,'blk'=4,'tp'=4] {'blk','tp'}, dimensions={0} | all-to-all | bytes 1048576 | tf_op jit(solution)/shard_map/all_to_all | solution.py:19
  41.4 0.3 norm_backward.1
  41.7 22.1 %all_to_all.36 = bf16[16,8,128]{2,1,0:T(8,128)(2,1)S(1)} all-to-all(bf16[16,8,128]{2,1,0:T(8,128)(2,1)S(1)} %norm_backward.1), channel_id=1, replica_groups=mesh['zh'=4,'y'=8,'core'=2,'blk'=4,'tp'=4] {'y','core'}, dimensions={0} | all-to-all | bytes 65536 | tf_op jit(solution)/shard_map/all_to_all | solution.py:19
  63.8 0.1 broadcast_in_dim.2
  63.9 19.2 %all_to_all.37.grads_ref = bf16[16,16,8,128]{3,2,1,0:T(8,128)(2,1)} all-to-all(bf16[16,16,8,128]{3,2,1,0:T(8,128)(2,1)S(1)} %broadcast_in_dim.2), channel_id=1, replica_groups=mesh['zh'=4,'y'=8,'core'=2,'blk'=4,'tp'=4] {'blk','tp'}, dimensions={0} | all-to-all | bytes 1048576 | tf_op jit(solution)/shard_map/all_to_all | solution.py:19
  83.1 0.0 all-gather.2.cloned.1.call-done.columns_ref
  83.1 2.5 %product.1 = bf16[768,128]{1,0:T(8,128)(2,1)S(1)} custom-call(bf16[2048,768]{1,0:T(8,128)(2,1)} %all-gather.2.cloned.1.call-done.columns_ref, bf16[16,16,8,128]{3,2,1,0:T(8,128)(2,1)} %all_to_all.37.grads_ref), custom_call_target="tpu_custom_call" | custom-call | tf_op jit(solution)/shard_map/product/pallas_call | solution.py:65
  85.6 29.3 %all_to_all.38.pieces_ref = bf16[4,192,128]{2,1,0:T(8,128)(2,1)S(1)} all-to-all(bf16[4,192,128]{2,1,0:T(8,128)(2,1)S(1)} %bitcast.11), channel_id=1, replica_groups=mesh['zh'=4,'y'=8,'core'=2,'blk'=4,'tp'=4] {'zh'}, dimensions={0} | all-to-all | bytes 393216 | tf_op jit(solution)/shard_map/all_to_all | solution.py:19
  114.9 0.2 gather_rows.1
  115.1 15.3 %all_to_all.39.back_ref = f32[16,16,128]{2,1,0:T(8,128)S(1)} all-to-all(f32[16,16,128]{2,1,0:T(8,128)S(1)} %gather_rows.1), channel_id=1, replica_groups=mesh['zh'=4,'y'=8,'core'=2,'blk'=4,'tp'=4] {'y','core'}, dimensions={0} | all-to-all | bytes 262144 | tf_op jit(solution)/shard_map/all_to_all | solution.py:19
  130.5 18.9 %all_to_all.40.squares_ref = f32[64,1,128]{2,1,0:T(1,128)S(1)} all-to-all(f32[64,1,128]{2,1,0:T(1,128)S(1)} %spread_squares.1), channel_id=1, replica_groups=mesh['zh'=4,'y'=8,'core'=2,'blk'=4,'tp'=4] {'zh','blk','tp'}, dimensions={0} | all-to-all | bytes 65536 | tf_op jit(solution)/shard_map/all_to_all | solution.py:19
  149.4 0.8 clip.1
  (1 shorter events, 0.0 us)
Async XLA Ops:
  7.2 18.2 %copy-start = (bf16[768,2048]{1,0:T(8,128)(2,1)S(1)}, bf16[768,2048]{1,0:T(8,128)(2,1)}, u32[]{:S(2)}) copy-start(bf16[768,2048]{1,0:T(8,128)(2,1)} %param.6) | copy-start | bytes 9437188
  7.2 18.2 %all-to-all-start = ((bf16[16,8,768]{2,1,0:T(8,128)(2,1)}), bf16[16,8,768]{2,1,0:T(8,128)(2,1)S(1)}, u32[]{:S(2)}, u32[]{:S(2)}) async-start(bf16[16,8,768]{2,1,0:T(8,128)(2,1)} %bitcast.14), calls=%async_computation | async-start | bytes 393216 | tf_op jit(solution)/shard_map/all_to_all | solution.py:19
  17.8 65.3 %all-gather.2.cloned.1.call-start = ((), (), s32[]{:S(2)}) async-start(), calls=%async_computation.7 | async-start | bytes 3342336 | tf_op jit(solution)/shard_map/all_gather | solution.py:159
  25.4 1.4 copy-start.1
Sparse Core Ops, SparseCore 0:
  26.9 53.9 all-gather.1

commit v12 on v11

--- a/solution.py
+++ b/solution.py
@@ -30,14 +30,15 @@
     along = jnp.mean(scaled * normed, axis=1, keepdims=True)
     token_grad = (inverse_rms * (scaled - normed * along)).astype(BF16)
     for j in range(out_ref.shape[0]):
-        out_ref[j] = token_grad[:, j * LANES : (j + 1) * LANES]
+        for k in range(out_ref.shape[1]):
+            out_ref[j, k] = token_grad[:, j * LANES : (j + 1) * LANES]
 
 
-def norm_backward(parts, scaled, slices):
+def norm_backward(parts, scaled, slices, copies):
     _, tok, width = parts.shape
     return pl.pallas_call(
         norm_backward_kernel,
-        out_shape=jax.ShapeDtypeStruct((slices, tok, width // slices), BF16),
+        out_shape=jax.ShapeDtypeStruct((slices, copies, tok, width // slices), BF16),
         compiler_params=pltpu.CompilerParams(vmem_limit_bytes=12 << 20),
         name="norm_backward",
     )(parts, scaled)
@@ -50,8 +51,9 @@
     def _():
         total_ref[...] = jnp.zeros_like(total_ref)
 
-    groups, chunk, tok, part = grads_ref.shape
-    grads = grads_ref[...].astype(F32).transpose(1, 0, 2, 3).reshape(chunk * groups * tok, part)
+    blks, chunk, tps, tok, part = grads_ref.shape
+    grads = grads_ref[...].astype(F32).transpose(1, 0, 2, 3, 4)
+    grads = grads.reshape(chunk * blks * tps * tok, part)
     total_ref[...] += jnp.dot(grads.T.astype(BF16), columns_ref[...], preferred_element_type=F32)
 
     @pl.when(step == pl.num_programs(0) - 1)
@@ -60,14 +62,14 @@
 
 
 def product(all_columns, arrived, steps):
-    groups, slices, tok, part = arrived.shape
+    blks, slices, tps, tok, part = arrived.shape
     tokens, shard = all_columns.shape
     return pl.pallas_call(
         product_kernel,
         grid=(steps,),
         in_specs=[
             pl.BlockSpec((tokens // steps, shard), lambda i: (i, 0)),
-            pl.BlockSpec((groups, slices // steps, tok, part), lambda i: (0, i, 0, 0)),
+            pl.BlockSpec((blks, slices // steps, tps, tok, part), lambda i: (0, i, 0, 0, 0)),
         ],
         out_specs=pl.BlockSpec((shard, part), lambda i: (0, 0)),
         out_shape=jax.ShapeDtypeStruct((shard, part), BF16),
@@ -159,9 +161,11 @@
     all_columns = lax.all_gather(columns, ALONG, axis=0, tiled=True)
     parts = exchange(lax.optimization_barrier(partial_value.reshape(groups, tok, width)), GROUP)
 
-    cut = exchange(norm_backward(parts, scaled, slices), ALONG)
-    spread = lax.optimization_barrier(jnp.broadcast_to(cut[None], (groups, slices, tok, part)))
-    arrived = exchange(spread, GROUP)
+    blks, tps = lax.axis_size("blk"), lax.axis_size("tp")
+    cut = norm_backward(parts, scaled, slices, tps).reshape(slices * tps, tok, part)
+    cut = exchange(cut, ALONG + ("tp",))
+    spread = lax.optimization_barrier(jnp.broadcast_to(cut[None], (blks, slices * tps, tok, part)))
+    arrived = exchange(spread, "blk").reshape(blks, slices, tps, tok, part)
     block = product(all_columns, arrived, 2)
     by_zh = exchange(block.reshape(ZHI, shard // ZHI, part), "zh")
 

time: 158 us -> 158 us (level)
  waiting for transfers between devices: 5.91 us -> 10.5 us
  blocking collectives: 119 us -> 116 us
    all_gather x1, waiting for transfers between devices: 0.01 us -> 4.6 us  [body(): all_columns = lax.all_gather(columns, ALONG, axis=0, tiled=True)]
    all_to_all x6, blocking collectives: 119 us -> 116 us  [exchange(): return lax.all_to_all(blocks, axes, split_axis=0, concat_axis=0, tiled=True)]
  transfers between devices with their start and end apart: 2 -> 2, of which waited for: 1 -> 2; matrix products, arithmetic and copies ran while one was open for 1% -> 1% of each run, Pallas kernels for 0% -> 0%
where the time goes in v12:
time: 158 us
  blocking collectives  116 us (73%)
  between operations  14.1 us (9%)
  starting transfers between devices  10.7 us (7%)
  waiting for transfers between devices  10.5 us (7%)
  Pallas kernels  3.81 us (2%)
    all_to_all x6, blocking collectives, exchange(): return lax.all_to_all(blocks, axes, split_axis=0, concat_axis=0, tiled=True)  116 us
    all_to_all x1, starting transfers between devices, exchange(): return lax.all_to_all(blocks, axes, split_axis=0, concat_axis=0, tiled=True)  10.7 us
    all_to_all x1, waiting for transfers between devices, exchange(): return lax.all_to_all(blocks, axes, split_axis=0, concat_axis=0, tiled=True)  5.89 us
    all_gather x1, waiting for transfers between devices, body(): all_columns = lax.all_gather(columns, ALONG, axis=0, tiled=True)  4.6 us
  transfers between devices with their start and end apart: 2, of which 2 were waited for; matrix products, arithmetic and copies ran while one was open for 1% of the time, Pallas kernels for 0%

profile of v12, /device:TPU:1, one launch (start us, length us, event | category | flops | bytes accessed | tf_op | source)
XLA Modules:
  0.0 157.8 jit_solution(7680529235377661472)
XLA Ops:
  7.2 0.0 copy-start
  7.2 10.7 %all-to-all-start = ((bf16[16,8,768]{2,1,0:T(8,128)(2,1)}), bf16[16,8,768]{2,1,0:T(8,128)(2,1)S(1)}, u32[]{:S(2)}, u32[]{:S(2)}) async-start(bf16[16,8,768]{2,1,0:T(8,128)(2,1)} %bitcast.18), calls=%async_computation | async-start | bytes 393216 | tf_op jit(solution)/shard_map/all_to_all | solution.py:19
  17.8 0.0 all-gather.2.cloned.1.call-start
  17.9 0.7 dynamic-slice_convert_fusion
  18.6 0.8 multiply_multiply_fusion.scaled_ref
  19.5 5.9 %all-to-all-done = bf16[16,8,768]{2,1,0:T(8,128)(2,1)S(1)} async-done(((bf16[16,8,768]{2,1,0:T(8,128)(2,1)}), bf16[16,8,768]{2,1,0:T(8,128)(2,1)S(1)}, u32[]{:S(2)}, u32[]{:S(2)}) %all-to-all-start) | async-done | bytes 196640 | tf_op jit(solution)/shard_map/all_to_all | solution.py:19
  25.4 0.0 copy-done
  25.4 0.0 copy-start.1
  25.4 1.4 convolution_convert_fusion
  26.7 0.0 copy-done.1
  26.7 0.0 all-gather.2.cloned.1.call-update
  26.8 14.7 %all_to_all.35.parts_ref = bf16[16,8,2048]{2,1,0:T(8,128)(2,1)S(1)} all-to-all(bf16[16,8,2048]{2,1,0:T(8,128)(2,1)} %bitcast.15), channel_id=1, replica_groups=mesh['zh'=4,'y'=8,'core'=2,'blk'=4,'tp'=4] {'blk','tp'}, dimensions={0} | all-to-all | bytes 1048576 | tf_op jit(solution)/shard_map/all_to_all | solution.py:19
  41.4 0.3 norm_backward.1
  41.7 25.1 %all_to_all.36 = bf16[64,8,128]{2,1,0:T(8,128)(2,1)S(1)} all-to-all(bf16[64,8,128]{2,1,0:T(8,128)(2,1)S(1)} %bitcast.14), channel_id=1, replica_groups=mesh['zh'=4,'y'=8,'core'=2,'blk'=4,'tp'=4] {'y','core','tp'}, dimensions={0} | all-to-all | bytes 262144 | tf_op jit(solution)/shard_map/all_to_all | solution.py:19
  66.8 0.1 broadcast_in_dim.2
  66.9 10.9 %all_to_all.37 = bf16[4,64,8,128]{3,2,1,0:T(8,128)(2,1)} all-to-all(bf16[4,64,8,128]{3,2,1,0:T(8,128)(2,1)S(1)} %broadcast_in_dim.2), channel_id=1, replica_groups=mesh['zh'=4,'y'=8,'core'=2,'blk'=4,'tp'=4] {'blk'}, dimensions={0} | all-to-all | bytes 1048576 | tf_op jit(solution)/shard_map/all_to_all | solution.py:19
  77.8 4.6 %all-gather.2.cloned.1.call-done.columns_ref = bf16[2048,768]{1,0:T(8,128)(2,1)} async-done(((bf16[128,768]{1,0:T(8,128)(2,1)}), bf16[2048,768]{1,0:T(8,128)(2,1)}) %all-gather.2.cloned.1.call-update) | async-done | bytes 3145744 | tf_op jit(solution)/shard_map/all_gather | solution.py:161
  82.4 2.5 %product.1 = bf16[768,128]{1,0:T(8,128)(2,1)S(1)} custom-call(bf16[2048,768]{1,0:T(8,128)(2,1)} %all-gather.2.cloned.1.call-done.columns_ref, bf16[4,16,4,8,128]{4,3,2,1,0:T(8,128)(2,1)} %bitcast.16), custom_call_target="tpu_custom_call" | custom-call | tf_op jit(solution)/shard_map/product/pallas_call | solution.py:67
  85.0 26.0 %all_to_all.38.pieces_ref = bf16[4,192,128]{2,1,0:T(8,128)(2,1)S(1)} all-to-all(bf16[4,192,128]{2,1,0:T(8,128)(2,1)S(1)} %bitcast.13), channel_id=1, replica_groups=mesh['zh'=4,'y'=8,'core'=2,'blk'=4,'tp'=4] {'zh'}, dimensions={0} | all-to-all | bytes 393216 | tf_op jit(solution)/shard_map/all_to_all | solution.py:19
  111.0 0.2 gather_rows.1
  111.1 18.6 %all_to_all.39.back_ref = f32[16,16,128]{2,1,0:T(8,128)S(1)} all-to-all(f32[16,16,128]{2,1,0:T(8,128)S(1)} %gather_rows.1), channel_id=1, replica_groups=mesh['zh'=4,'y'=8,'core'=2,'blk'=4,'tp'=4] {'y','core'}, dimensions={0} | all-to-all | bytes 262144 | tf_op jit(solution)/shard_map/all_to_all | solution.py:19
  129.8 20.4 %all_to_all.40.squares_ref = f32[64,1,128]{2,1,0:T(1,128)S(1)} all-to-all(f32[64,1,128]{2,1,0:T(1,128)S(1)} %spread_squares.1), channel_id=1, replica_groups=mesh['zh'=4,'y'=8,'core'=2,'blk'=4,'tp'=4] {'zh','blk','tp'}, dimensions={0} | all-to-all | bytes 65536 | tf_op jit(solution)/shard_map/all_to_all | solution.py:19
  150.2 0.8 clip.1
  (1 shorter events, 0.0 us)
Async XLA Ops:
  7.2 18.2 %copy-start = (bf16[768,2048]{1,0:T(8,128)(2,1)S(1)}, bf16[768,2048]{1,0:T(8,128)(2,1)}, u32[]{:S(2)}) copy-start(bf16[768,2048]{1,0:T(8,128)(2,1)} %param.6) | copy-start | bytes 9437188
  7.2 18.2 %all-to-all-start = ((bf16[16,8,768]{2,1,0:T(8,128)(2,1)}), bf16[16,8,768]{2,1,0:T(8,128)(2,1)S(1)}, u32[]{:S(2)}, u32[]{:S(2)}) async-start(bf16[16,8,768]{2,1,0:T(8,128)(2,1)} %bitcast.18), calls=%async_computation | async-start | bytes 393216 | tf_op jit(solution)/shard_map/all_to_all | solution.py:19
  17.8 64.6 %all-gather.2.cloned.1.call-start = ((), (), s32[]{:S(2)}) async-start(), calls=%async_computation.7 | async-start | bytes 3342336 | tf_op jit(solution)/shard_map/all_gather | solution.py:161
  25.4 1.4 copy-start.1
Sparse Core Ops, SparseCore 0:
  26.9 55.5 all-gather.1

commit v13 on v12

--- a/solution.py
+++ b/solution.py
@@ -11,7 +11,6 @@
 REP = ("zh", "y", "core")
 ALONG = ("y", "core")
 GROUP = ("blk", "tp")
-LANES = 128
 BF16, F32 = jnp.bfloat16, jnp.float32
 
 
@@ -29,9 +28,10 @@
     normed = projected * inverse_rms
     along = jnp.mean(scaled * normed, axis=1, keepdims=True)
     token_grad = (inverse_rms * (scaled - normed * along)).astype(BF16)
+    cols = out_ref.shape[3]
     for j in range(out_ref.shape[0]):
         for k in range(out_ref.shape[1]):
-            out_ref[j, k] = token_grad[:, j * LANES : (j + 1) * LANES]
+            out_ref[j, k] = token_grad[:, j * cols : (j + 1) * cols]
 
 
 def norm_backward(parts, scaled, slices, copies):
@@ -44,37 +44,45 @@
     )(parts, scaled)
 
 
-def product_kernel(columns_ref, grads_ref, out_ref, total_ref):
+def product_kernel(columns_ref, grads_ref, keep_ref, give_ref, total_ref):
     step = pl.program_id(0)
+    blks, chunk, tps, tok, cols = grads_ref.shape
+    part = keep_ref.shape[1]
+    grads = grads_ref[...].astype(F32).transpose(1, 0, 2, 3, 4)
+    grads = grads.reshape(chunk * blks * tps * tok, cols).T.astype(BF16)
+    term = jnp.dot(grads, columns_ref[...], preferred_element_type=F32)
 
     @pl.when(step == 0)
     def _():
-        total_ref[...] = jnp.zeros_like(total_ref)
-
-    blks, chunk, tps, tok, part = grads_ref.shape
-    grads = grads_ref[...].astype(F32).transpose(1, 0, 2, 3, 4)
-    grads = grads.reshape(chunk * blks * tps * tok, part)
-    total_ref[...] += jnp.dot(grads.T.astype(BF16), columns_ref[...], preferred_element_type=F32)
+        total_ref[...] = term
+
+    @pl.when(step != 0)
+    def _():
+        total_ref[...] += term
 
     @pl.when(step == pl.num_programs(0) - 1)
     def _():
-        out_ref[...] = total_ref[...].T.astype(BF16)
+        core = lax.axis_index("core")
+        keep_ref[...] = total_ref[pl.ds(pl.multiple_of(core * part, part), part)].T
+        given = total_ref[pl.ds(pl.multiple_of((1 - core) * part, part), part)]
+        give_ref[...] = given.T.astype(BF16)
 
 
 def product(all_columns, arrived, steps):
-    blks, slices, tps, tok, part = arrived.shape
+    blks, ys, tps, tok, cols = arrived.shape
     tokens, shard = all_columns.shape
+    half = (shard, cols // CORES)
     return pl.pallas_call(
         product_kernel,
         grid=(steps,),
         in_specs=[
             pl.BlockSpec((tokens // steps, shard), lambda i: (i, 0)),
-            pl.BlockSpec((blks, slices // steps, tps, tok, part), lambda i: (0, i, 0, 0, 0)),
+            pl.BlockSpec((blks, ys // steps, tps, tok, cols), lambda i: (0, i, 0, 0, 0)),
         ],
-        out_specs=pl.BlockSpec((shard, part), lambda i: (0, 0)),
-        out_shape=jax.ShapeDtypeStruct((shard, part), BF16),
-        scratch_shapes=[pltpu.VMEM((part, shard), F32)],
-        compiler_params=pltpu.CompilerParams(vmem_limit_bytes=55040 << 10),
+        out_specs=[pl.BlockSpec(half, lambda i: (0, 0))] * 2,
+        out_shape=[jax.ShapeDtypeStruct(half, F32), jax.ShapeDtypeStruct(half, BF16)],
+        scratch_shapes=[pltpu.VMEM((cols, shard), F32)],
+        compiler_params=pltpu.CompilerParams(vmem_limit_bytes=54528 << 10),
         name="product",
     )(all_columns, arrived)
 
@@ -158,15 +166,16 @@
     columns = columns.reshape(groups * tok, shard)
     partial_value = jnp.dot(columns, projection_weight, preferred_element_type=F32).astype(BF16)
     columns, partial_value = lax.optimization_barrier((columns, partial_value))
-    all_columns = lax.all_gather(columns, ALONG, axis=0, tiled=True)
+    all_columns = lax.all_gather(columns, "y", axis=0, tiled=True)
     parts = exchange(lax.optimization_barrier(partial_value.reshape(groups, tok, width)), GROUP)
 
-    blks, tps = lax.axis_size("blk"), lax.axis_size("tp")
-    cut = norm_backward(parts, scaled, slices, tps).reshape(slices * tps, tok, part)
-    cut = exchange(cut, ALONG + ("tp",))
-    spread = lax.optimization_barrier(jnp.broadcast_to(cut[None], (blks, slices * tps, tok, part)))
-    arrived = exchange(spread, "blk").reshape(blks, slices, tps, tok, part)
-    block = product(all_columns, arrived, 2)
+    blks, tps, cols = lax.axis_size("blk"), lax.axis_size("tp"), CORES * part
+    cut = norm_backward(parts, scaled, YS, tps).reshape(YS * tps, tok, cols)
+    cut = exchange(cut, ("y", "tp"))
+    spread = lax.optimization_barrier(jnp.broadcast_to(cut[None], (blks, YS * tps, tok, cols)))
+    arrived = exchange(spread, "blk").reshape(blks, YS, tps, tok, cols)
+    keep, give = product(all_columns, arrived, 2)
+    block = (keep + lax.ppermute(give, "core", [(0, 1), (1, 0)]).astype(F32)).astype(BF16)
     by_zh = exchange(block.reshape(ZHI, shard // ZHI, part), "zh")
 
     back = exchange(gather_rows(by_zh, own_rows, slices, 16), ALONG)

time: 158 us -> 170 us (1.076)
  blocking collectives: 116 us -> 86.6 us
  waiting for transfers between devices: 10.5 us -> 34.2 us
  starting transfers between devices: 10.7 us -> 25.4 us
    all_to_all x6 -> x4, blocking collectives: 116 us -> 86.6 us  [exchange(): return lax.all_to_all(blocks, axes, split_axis=0, concat_axis=0, tiled=True)]
    all_gather x1, waiting for transfers between devices: 4.6 us -> 16.1 us  [body(): all_columns = lax.all_gather(columns, 'y', axis=0, tiled=True)]
    all_to_all x1 -> x3, waiting for transfers between devices: 5.89 us -> 16.4 us  [exchange(): return lax.all_to_all(blocks, axes, split_axis=0, concat_axis=0, tiled=True)]
    all_to_all x1 -> x3, starting transfers between devices: 10.7 us -> 19 us  [exchange(): return lax.all_to_all(blocks, axes, split_axis=0, concat_axis=0, tiled=True)]
    ppermute x0 -> x1, starting transfers between devices: none -> 6.37 us  [body(): lax.ppermute(give, 'core', [(0, 1), (1, 0)]).astype(F32)]
  transfers between devices with their start and end apart: 2 -> 5, of which waited for: 2 -> 4; matrix products, arithmetic and copies ran while one was open for 1% -> 1% of each run, Pallas kernels for 0% -> 1%
where the time goes in v13:
time: 170 us; the launch traced here: 169 us
  blocking collectives  86.6 us (51%)
  waiting for transfers between devices  34.2 us (20%)
  starting transfers between devices  25.4 us (15%)
  between operations  14.1 us (8%)
  Pallas kernels  4.72 us (3%)
    all_to_all x4, blocking collectives, exchange(): return lax.all_to_all(blocks, axes, split_axis=0, concat_axis=0, tiled=True)  86.6 us
    all_to_all x3, starting transfers between devices, exchange(): return lax.all_to_all(blocks, axes, split_axis=0, concat_axis=0, tiled=True)  19 us
    all_to_all x3, waiting for transfers between devices, exchange(): return lax.all_to_all(blocks, axes, split_axis=0, concat_axis=0, tiled=True)  16.4 us
    all_gather x1, waiting for transfers between devices, body(): all_columns = lax.all_gather(columns, 'y', axis=0, tiled=True)  16.1 us
    ppermute x1, starting transfers between devices, body(): lax.ppermute(give, 'core', [(0, 1), (1, 0)]).astype(F32)  6.37 us
  transfers between devices with their start and end apart: 5, of which 4 were waited for; matrix products, arithmetic and copies ran while one was open for 1% of the time, Pallas kernels for 1%

profile of v13, /device:TPU:1, one launch (start us, length us, event | category | flops | bytes accessed | tf_op | source)
XLA Modules:
  0.0 168.9 jit_solution(10223690731444871500)
XLA Ops:
  7.2 0.0 copy-start
  7.2 10.7 %all-to-all-start = ((bf16[16,8,768]{2,1,0:T(8,128)(2,1)}), bf16[16,8,768]{2,1,0:T(8,128)(2,1)S(1)}, u32[]{:S(2)}, u32[]{:S(2)}) async-start(bf16[16,8,768]{2,1,0:T(8,128)(2,1)} %bitcast.17), calls=%async_computation | async-start | bytes 393216 | tf_op jit(solution)/shard_map/all_to_all | solution.py:18
  17.8 0.7 dynamic-slice_convert_fusion
  18.6 0.8 multiply_multiply_fusion.scaled_ref
  19.4 5.9 %all-to-all-done = bf16[16,8,768]{2,1,0:T(8,128)(2,1)S(1)} async-done(((bf16[16,8,768]{2,1,0:T(8,128)(2,1)}), bf16[16,8,768]{2,1,0:T(8,128)(2,1)S(1)}, u32[]{:S(2)}, u32[]{:S(2)}) %all-to-all-start) | async-done | bytes 196640 | tf_op jit(solution)/shard_map/all_to_all | solution.py:18
  25.4 0.0 copy-done
  25.4 0.0 copy-start.1
  25.4 1.4 convolution_convert_fusion
  26.7 4.2 %all-to-all-start.1 = ((bf16[16,8,2048]{2,1,0:T(8,128)(2,1)}), bf16[16,8,2048]{2,1,0:T(8,128)(2,1)}, u32[]{:S(2)}, u32[]{:S(2)}) async-start(bf16[16,8,2048]{2,1,0:T(8,128)(2,1)} %bitcast.14), calls=%async_computation.1 | async-start | bytes 1048576 | tf_op jit(solution)/shard_map/all_to_all | solution.py:18
  31.0 0.0 all-gather.2.cloned.1.call-start
  31.0 0.0 copy-done.1
  31.1 0.7 all-gather.2.cloned.1.call-update
  31.7 10.4 %all-to-all-done.1.parts_ref = bf16[16,8,2048]{2,1,0:T(8,128)(2,1)} async-done(((bf16[16,8,2048]{2,1,0:T(8,128)(2,1)}), bf16[16,8,2048]{2,1,0:T(8,128)(2,1)}, u32[]{:S(2)}, u32[]{:S(2)}) %all-to-all-start.1) | async-done | bytes 524320 | tf_op jit(solution)/shard_map/all_to_all | solution.py:18
  42.1 1.3 norm_backward.1
  43.5 21.8 %all_to_all.35 = bf16[32,8,256]{2,1,0:T(8,128)(2,1)S(1)} all-to-all(bf16[32,8,256]{2,1,0:T(8,128)(2,1)S(1)} %bitcast.13), channel_id=1, replica_groups=mesh['zh'=4,'y'=8,'core'=2,'blk'=4,'tp'=4] {'y','tp'}, dimensions={0} | all-to-all | bytes 262144 | tf_op jit(solution)/shard_map/all_to_all | solution.py:18
  65.2 0.8 broadcast_in_dim.2
  66.1 4.1 %all-to-all-start.3 = ((bf16[4,32,8,256]{3,2,1,0:T(8,128)(2,1)}), bf16[4,32,8,256]{3,2,1,0:T(8,128)(2,1)}, u32[]{:S(2)}, u32[]{:S(2)}) async-start(bf16[4,32,8,256]{3,2,1,0:T(8,128)(2,1)} %broadcast_in_dim.2), calls=%async_computation.3 | async-start | bytes 1048576 | tf_op jit(solution)/shard_map/all_to_all | solution.py:18
  70.2 16.1 %all-gather.2.cloned.1.call-done.columns_ref = bf16[1024,768]{1,0:T(8,128)(2,1)} async-done(((bf16[128,768]{1,0:T(8,128)(2,1)}), bf16[1024,768]{1,0:T(8,128)(2,1)}) %all-gather.2.cloned.1.call-update) | async-done | bytes 1572880 | tf_op jit(solution)/shard_map/all_gather | solution.py:169
  86.3 0.0 all-to-all-done.3
  86.3 2.4 %product.1 = (f32[768,128]{1,0:T(8,128)S(1)}, bf16[768,128]{1,0:T(8,128)(2,1)S(1)}) custom-call(bf16[1024,768]{1,0:T(8,128)(2,1)} %all-gather.2.cloned.1.call-done.columns_ref, bf16[4,8,4,8,256]{4,3,2,1,0:T(8,128)(2,1)} %bitcast.5.grads_ref), custom_call_target="tpu_custom_call" | custom-call | tf_op jit(solution)/shard_map/product/pallas_call | solution.py:75
  88.7 6.4 %collective-permute-start = (bf16[768,128]{1,0:T(8,128)(2,1)S(1)}, bf16[768,128]{1,0:T(8,128)(2,1)S(1)}, u32[]{:S(2)}, u32[]{:S(2)}) collective-permute-start(bf16[768,128]{1,0:T(8,128)(2,1)S(1)} %get-tuple-element.15), channel_id=1, source_target_pairs={{0,16},{16,0},{1,17},{17,1},{2,18},{18,2},{3,19},{19,3},{4,20},{20... | collective-permute-start | bytes 589832 | tf_op jit(solution)/shard_map/ppermute | solution.py:178
  95.1 1.0 collective-permute-done
  96.1 0.1 add_convert_fusion
  96.2 26.8 %all_to_all.36.pieces_ref = bf16[4,192,128]{2,1,0:T(8,128)(2,1)S(1)} all-to-all(bf16[4,192,128]{2,1,0:T(8,128)(2,1)S(1)} %bitcast.16), channel_id=1, replica_groups=mesh['zh'=4,'y'=8,'core'=2,'blk'=4,'tp'=4] {'zh'}, dimensions={0} | all-to-all | bytes 393216 | tf_op jit(solution)/shard_map/all_to_all | solution.py:18
  123.0 0.2 gather_rows.1
  123.2 17.5 %all_to_all.37.back_ref = f32[16,16,128]{2,1,0:T(8,128)S(1)} all-to-all(f32[16,16,128]{2,1,0:T(8,128)S(1)} %gather_rows.1), channel_id=1, replica_groups=mesh['zh'=4,'y'=8,'core'=2,'blk'=4,'tp'=4] {'y','core'}, dimensions={0} | all-to-all | bytes 262144 | tf_op jit(solution)/shard_map/all_to_all | solution.py:18
  140.7 20.5 %all_to_all.38.squares_ref = f32[64,1,128]{2,1,0:T(1,128)S(1)} all-to-all(f32[64,1,128]{2,1,0:T(1,128)S(1)} %spread_squares.1), channel_id=1, replica_groups=mesh['zh'=4,'y'=8,'core'=2,'blk'=4,'tp'=4] {'zh','blk','tp'}, dimensions={0} | all-to-all | bytes 65536 | tf_op jit(solution)/shard_map/all_to_all | solution.py:18
  161.2 0.8 clip.1
  (1 shorter events, 0.0 us)
Async XLA Ops:
  7.2 18.2 %copy-start = (bf16[768,2048]{1,0:T(8,128)(2,1)S(1)}, bf16[768,2048]{1,0:T(8,128)(2,1)}, u32[]{:S(2)}) copy-start(bf16[768,2048]{1,0:T(8,128)(2,1)} %param.6) | copy-start | bytes 9437188
  7.2 18.2 %all-to-all-start = ((bf16[16,8,768]{2,1,0:T(8,128)(2,1)}), bf16[16,8,768]{2,1,0:T(8,128)(2,1)S(1)}, u32[]{:S(2)}, u32[]{:S(2)}) async-start(bf16[16,8,768]{2,1,0:T(8,128)(2,1)} %bitcast.17), calls=%async_computation | async-start | bytes 393216 | tf_op jit(solution)/shard_map/all_to_all | solution.py:18
  25.4 5.7 %copy-start.1 = (bf16[16,8,768]{2,1,0:T(8,128)(2,1)}, bf16[16,8,768]{2,1,0:T(8,128)(2,1)S(1)}, u32[]{:S(2)}) copy-start(bf16[16,8,768]{2,1,0:T(8,128)(2,1)S(1)} %all-to-all-done) | copy-start | bytes 589828
  26.7 15.4 %all-to-all-start.1 = ((bf16[16,8,2048]{2,1,0:T(8,128)(2,1)}), bf16[16,8,2048]{2,1,0:T(8,128)(2,1)}, u32[]{:S(2)}, u32[]{:S(2)}) async-start(bf16[16,8,2048]{2,1,0:T(8,128)(2,1)} %bitcast.14), calls=%async_computation.1 | async-start | bytes 1048576 | tf_op jit(solution)/shard_map/all_to_all | solution.py:18
  31.0 55.3 %all-gather.2.cloned.1.call-start = ((), (), s32[]{:S(2)}) async-start(), calls=%async_computation.7 | async-start | bytes 1769472 | tf_op jit(solution)/shard_map/all_gather | solution.py:169
  66.1 20.2 %all-to-all-start.3 = ((bf16[4,32,8,256]{3,2,1,0:T(8,128)(2,1)}), bf16[4,32,8,256]{3,2,1,0:T(8,128)(2,1)}, u32[]{:S(2)}, u32[]{:S(2)}) async-start(bf16[4,32,8,256]{3,2,1,0:T(8,128)(2,1)} %broadcast_in_dim.2), calls=%async_computation.3 | async-start | bytes 1048576 | tf_op jit(solution)/shard_map/all_to_all | solution.py:18
  88.7 7.4 %collective-permute-start = (bf16[768,128]{1,0:T(8,128)(2,1)S(1)}, bf16[768,128]{1,0:T(8,128)(2,1)S(1)}, u32[]{:S(2)}, u32[]{:S(2)}) collective-permute-start(bf16[768,128]{1,0:T(8,128)(2,1)S(1)} %get-tuple-element.15), channel_id=1, source_target_pairs={{0,16},{16,0},{1,17},{17,1},{2,18},{18,2},{3,19},{19,3},{4,20},{20... | collective-permute-start | bytes 589832 | tf_op jit(solution)/shard_map/ppermute | solution.py:178
Sparse Core Ops, SparseCore 0:
  34.5 51.7 all-gather.1

commit v14 on v12

--- a/solution.py
+++ b/solution.py
@@ -156,9 +156,8 @@
     columns = exchange(sent, GROUP)
     columns, scaled = lax.optimization_barrier((columns, scaled))
     columns = columns.reshape(groups * tok, shard)
+    all_columns = lax.all_gather(columns, ALONG, axis=0, tiled=True)
     partial_value = jnp.dot(columns, projection_weight, preferred_element_type=F32).astype(BF16)
-    columns, partial_value = lax.optimization_barrier((columns, partial_value))
-    all_columns = lax.all_gather(columns, ALONG, axis=0, tiled=True)
     parts = exchange(lax.optimization_barrier(partial_value.reshape(groups, tok, width)), GROUP)
 
     blks, tps = lax.axis_size("blk"), lax.axis_size("tp")

time: 158 us -> 158 us (level)
  transfers between devices with their start and end apart: 2 -> 2, of which waited for: 2 -> 2; matrix products, arithmetic and copies ran while one was open for 1% -> 2% of each run, Pallas kernels for 0% -> 0%
where the time goes in v14:
time: 158 us; the launch traced here: 157 us
  blocking collectives  116 us (73%)
  between operations  14.1 us (9%)
  starting transfers between devices  10.7 us (7%)
  waiting for transfers between devices  9.09 us (6%)
  Pallas kernels  3.81 us (2%)
    all_to_all x6, blocking collectives, exchange(): return lax.all_to_all(blocks, axes, split_axis=0, concat_axis=0, tiled=True)  116 us
    all_to_all x1, starting transfers between devices, exchange(): return lax.all_to_all(blocks, axes, split_axis=0, concat_axis=0, tiled=True)  10.7 us
    all_to_all x1, waiting for transfers between devices, exchange(): return lax.all_to_all(blocks, axes, split_axis=0, concat_axis=0, tiled=True)  5.89 us
    all_gather x1, waiting for transfers between devices, body(): all_columns = lax.all_gather(columns, ALONG, axis=0, tiled=True)  3.19 us
  transfers between devices with their start and end apart: 2, of which 2 were waited for; matrix products, arithmetic and copies ran while one was open for 2% of the time, Pallas kernels for 0%

profile of v14, /device:TPU:1, one launch (start us, length us, event | category | flops | bytes accessed | tf_op | source)
XLA Modules:
  0.0 157.5 jit_solution(11324866136653529126)
XLA Ops:
  7.2 0.0 copy-start
  7.2 10.7 %all-to-all-start = ((bf16[16,8,768]{2,1,0:T(8,128)(2,1)}), bf16[16,8,768]{2,1,0:T(8,128)(2,1)S(1)}, u32[]{:S(2)}, u32[]{:S(2)}) async-start(bf16[16,8,768]{2,1,0:T(8,128)(2,1)} %bitcast.18), calls=%async_computation | async-start | bytes 393216 | tf_op jit(solution)/shard_map/all_to_all | solution.py:19
  17.8 0.0 all-gather.2.cloned.1.call-start
  17.9 0.7 dynamic-slice_convert_fusion
  18.6 0.8 multiply_multiply_fusion.scaled_ref
  19.5 5.9 %all-to-all-done = bf16[16,8,768]{2,1,0:T(8,128)(2,1)S(1)} async-done(((bf16[16,8,768]{2,1,0:T(8,128)(2,1)}), bf16[16,8,768]{2,1,0:T(8,128)(2,1)S(1)}, u32[]{:S(2)}, u32[]{:S(2)}) %all-to-all-start) | async-done | bytes 196640 | tf_op jit(solution)/shard_map/all_to_all | solution.py:19
  25.4 0.0 copy-start.1
  25.4 0.7 copy-done.1
  26.0 0.0 all-gather.2.cloned.1.call-update
  26.0 0.0 copy-done
  26.1 1.5 fusion
  27.6 13.9 %all_to_all.35.parts_ref = bf16[16,8,2048]{2,1,0:T(8,128)(2,1)S(1)} all-to-all(bf16[16,8,2048]{2,1,0:T(8,128)(2,1)S(1)} %fusion), channel_id=1, replica_groups=mesh['zh'=4,'y'=8,'core'=2,'blk'=4,'tp'=4] {'blk','tp'}, dimensions={0} | all-to-all | bytes 1048576 | tf_op jit(solution)/shard_map/all_to_all | solution.py:19
  41.5 0.3 norm_backward.1
  41.8 25.7 %all_to_all.36 = bf16[64,8,128]{2,1,0:T(8,128)(2,1)S(1)} all-to-all(bf16[64,8,128]{2,1,0:T(8,128)(2,1)S(1)} %bitcast.15), channel_id=1, replica_groups=mesh['zh'=4,'y'=8,'core'=2,'blk'=4,'tp'=4] {'y','core','tp'}, dimensions={0} | all-to-all | bytes 262144 | tf_op jit(solution)/shard_map/all_to_all | solution.py:19
  67.5 0.1 broadcast_in_dim.2
  67.5 10.9 %all_to_all.37 = bf16[4,64,8,128]{3,2,1,0:T(8,128)(2,1)} all-to-all(bf16[4,64,8,128]{3,2,1,0:T(8,128)(2,1)S(1)} %broadcast_in_dim.2), channel_id=1, replica_groups=mesh['zh'=4,'y'=8,'core'=2,'blk'=4,'tp'=4] {'blk'}, dimensions={0} | all-to-all | bytes 1048576 | tf_op jit(solution)/shard_map/all_to_all | solution.py:19
  78.4 3.2 %all-gather.2.cloned.1.call-done.columns_ref = bf16[2048,768]{1,0:T(8,128)(2,1)} async-done(((bf16[128,768]{1,0:T(8,128)(2,1)}), bf16[2048,768]{1,0:T(8,128)(2,1)}) %all-gather.2.cloned.1.call-update) | async-done | bytes 3145744 | tf_op jit(solution)/shard_map/all_gather | solution.py:159
  81.6 2.5 %product.1 = bf16[768,128]{1,0:T(8,128)(2,1)S(1)} custom-call(bf16[2048,768]{1,0:T(8,128)(2,1)} %all-gather.2.cloned.1.call-done.columns_ref, bf16[4,16,4,8,128]{4,3,2,1,0:T(8,128)(2,1)} %bitcast.16), custom_call_target="tpu_custom_call" | custom-call | tf_op jit(solution)/shard_map/product/pallas_call | solution.py:67
  84.2 27.3 %all_to_all.38.pieces_ref = bf16[4,192,128]{2,1,0:T(8,128)(2,1)S(1)} all-to-all(bf16[4,192,128]{2,1,0:T(8,128)(2,1)S(1)} %bitcast.14), channel_id=1, replica_groups=mesh['zh'=4,'y'=8,'core'=2,'blk'=4,'tp'=4] {'zh'}, dimensions={0} | all-to-all | bytes 393216 | tf_op jit(solution)/shard_map/all_to_all | solution.py:19
  111.4 0.2 gather_rows.1
  111.6 16.6 %all_to_all.39.back_ref = f32[16,16,128]{2,1,0:T(8,128)S(1)} all-to-all(f32[16,16,128]{2,1,0:T(8,128)S(1)} %gather_rows.1), channel_id=1, replica_groups=mesh['zh'=4,'y'=8,'core'=2,'blk'=4,'tp'=4] {'y','core'}, dimensions={0} | all-to-all | bytes 262144 | tf_op jit(solution)/shard_map/all_to_all | solution.py:19
  128.2 21.6 %all_to_all.40.squares_ref = f32[64,1,128]{2,1,0:T(1,128)S(1)} all-to-all(f32[64,1,128]{2,1,0:T(1,128)S(1)} %spread_squares.1), channel_id=1, replica_groups=mesh['zh'=4,'y'=8,'core'=2,'blk'=4,'tp'=4] {'zh','blk','tp'}, dimensions={0} | all-to-all | bytes 65536 | tf_op jit(solution)/shard_map/all_to_all | solution.py:19
  149.8 0.8 clip.1
  (1 shorter events, 0.0 us)
Async XLA Ops:
  7.2 18.9 %copy-start = (bf16[768,2048]{1,0:T(8,128)(2,1)S(1)}, bf16[768,2048]{1,0:T(8,128)(2,1)}, u32[]{:S(2)}) copy-start(bf16[768,2048]{1,0:T(8,128)(2,1)} %param.6) | copy-start | bytes 9437188
  7.2 18.2 %all-to-all-start = ((bf16[16,8,768]{2,1,0:T(8,128)(2,1)}), bf16[16,8,768]{2,1,0:T(8,128)(2,1)S(1)}, u32[]{:S(2)}, u32[]{:S(2)}) async-start(bf16[16,8,768]{2,1,0:T(8,128)(2,1)} %bitcast.18), calls=%async_computation | async-start | bytes 393216 | tf_op jit(solution)/shard_map/all_to_all | solution.py:19
  17.8 63.8 %all-gather.2.cloned.1.call-start = ((), (), s32[]{:S(2)}) async-start(), calls=%async_computation.7 | async-start | bytes 3342336 | tf_op jit(solution)/shard_map/all_gather | solution.py:159
  25.4 0.7 copy-start.1
Sparse Core Ops, SparseCore 0:
  26.2 55.4 all-gather.1
